TPU v7x, 512 devices: a whole 4x8x8 slice. The times are simulated.
512 devices in a mesh: dp: 16 (over y_hi, x, core), tm: 8 (over z), height: 4 (over y_lo).
Axes of the slice: x: 4, y: 8 (y_hi: 2, y_lo: 4; y = y_hi * 4 + y_lo), z: 8, core: 2. Of those that a mesh axis runs over, the one named last changes fastest.
Arguments:
- probe_vectors: bfloat16 [16, 48, 32, 3, 1536], P('dp', 'tm', 'height'), may hold values from -24 to 24
- lookup_vectors: bfloat16 [16, 48, 32, 3, 1536], P('dp', 'tm', 'height'), may hold values from -24 to 24
- payload_vectors: bfloat16 [16, 48, 32, 3, 1536], P('dp', 'tm', 'height'), may hold values from -4.5 to 4.5
- result_derivative: bfloat16 [16, 48, 32, 3, 1536], P('dp', 'tm', 'height'), may hold values from -48 to 48
- patch_occupancy: int32 [16, 8, 4], P('dp'), may hold values from 63 to 144, as said below
- patch_neighborhood_offset: int32 [16, 8, 4, 2], P('dp'), may hold values from -1 to 1
- sharpness: float32 [12], replicated, may hold values from 0.7 to 1.4
Outputs:
- probe_derivative: bfloat16 [16, 48, 32, 3, 1536], P('dp', 'tm', 'height')
- lookup_derivative: bfloat16 [16, 48, 32, 3, 1536], P('dp', 'tm', 'height')
- payload_derivative: bfloat16 [16, 48, 32, 3, 1536], P('dp', 'tm', 'height')
- sharpness_derivative: float32 [12], replicated
Inputs may be any that keep to these rules, and one draw needn't show every extreme that they name: `patch_occupancy`: valid slots are the first ones of a tile in slot order; every tile off the last time tile and the last height tile is full.
All inputs are finite; a program needn't handle non-finite values.
Results may differ from a plain program's by a relative error of at most 0.022.
Values may be sent and summed in bfloat16 or wider, within the bound.
No kernel may reach another device: no remote copies, remote signals or barrier semaphores. Data moves between devices by JAX's collectives and lax.ppermute only.
A program may use at most 128 MiB of HBM per device.

v0:
```python
import functools
import math

import jax
import jax.numpy as jnp
import numpy as np
from jax import lax
from jax.experimental import pallas as pl
from jax.experimental.pallas import tpu as pltpu
from jax.sharding import PartitionSpec as P

ALL_AXES = ("dp", "tm", "height")
HIDDEN = -1e30


def shifted(block, axis, step):
    count = lax.axis_size(axis)
    pairs = [(i, i + step) for i in range(count) if 0 <= i + step < count]
    return lax.ppermute(block, axis, pairs)


def gathered_everywhere(row):
    count = math.prod(lax.axis_size(axis) for axis in ALL_AXES)
    sent = jnp.broadcast_to(row[None], (count,) + row.shape)
    return lax.all_to_all(sent, ALL_AXES, 0, 0)


def sum_body(rows_ref, own_ref, below_ref, above_ref, row_ref, own_sum_ref, *side_refs):
    row_ref[...] = jnp.sum(rows_ref[...], axis=0)
    length = own_sum_ref.shape[0]
    for n in range(3):
        rows = slice(n * length, (n + 1) * length)
        summed = (
            own_ref[rows].astype(jnp.float32)
            + below_ref[rows].astype(jnp.float32)
            + above_ref[rows].astype(jnp.float32)
        )
        if n == 0:
            own_sum_ref[...] = summed
        else:
            side_refs[n - 1][...] = summed.astype(jnp.bfloat16)


def summed_parts(rows, own, below, above):
    tile = (own.shape[0] // 3, own.shape[1])
    vmem = pl.BlockSpec(memory_space=pltpu.VMEM)
    return pl.pallas_call(
        sum_body,
        in_specs=[vmem] * 4,
        out_specs=[vmem] * 4,
        out_shape=[
            jax.ShapeDtypeStruct(rows.shape[1:], jnp.float32),
            jax.ShapeDtypeStruct(tile, jnp.float32),
            jax.ShapeDtypeStruct(tile, jnp.bfloat16),
            jax.ShapeDtypeStruct(tile, jnp.bfloat16),
        ],
        compiler_params=pltpu.CompilerParams(vmem_limit_bytes=16 * 1024 * 1024),
    )(rows, own, below, above)


LINE = (0, -1, 1)
KEY_TILES = [(a, b) for b in LINE for a in LINE]
VALUE_SPOTS = [(LINE.index(a), LINE.index(b)) for a, b in KEY_TILES]


def raw_scores(query, grad, keys, values, logits_ref, grad_weight_ref):
    across = (((1,), (1,)), ((), ()))
    logits_ref[...] = lax.dot_general(query, keys, across, preferred_element_type=jnp.float32)
    grad_weight_ref[...] = lax.dot_general(
        grad, values, across, preferred_element_type=jnp.float32
    )


def score_gradients(multiplier, bias_ref, valid_ref, logits_ref, grad_weight_ref, low_ref, scaled_ref):
    rows_at_once = 16
    for first in range(0, logits_ref.shape[0], rows_at_once):
        rows = slice(first, first + rows_at_once)
        logits = logits_ref[rows] * multiplier + bias_ref[...]
        raised = jnp.exp2(logits - jnp.max(logits, axis=1, keepdims=True))
        total = jnp.sum(raised, axis=1, keepdims=True)
        weights = raised * (valid_ref[rows] / total)
        low = weights.astype(jnp.bfloat16)
        low_ref[rows] = low
        grad_weight = grad_weight_ref[rows]
        row_delta = jnp.sum(low.astype(jnp.float32) * grad_weight, axis=1, keepdims=True)
        scaled_ref[rows] = (weights * (grad_weight - row_delta)).astype(jnp.bfloat16)


def attention_body(
    opening,
    tile_len,
    together,
    kept,
    sharpness_ref,
    counts_ref,
    shifts_ref,
    slot_row_ref,
    slot_col_ref,
    query_ref,
    grad_ref,
    *refs,
):
    key_refs, value_refs = refs[:3], refs[3:6]
    refs = refs[6 + kept :]
    query_grad_ref, sharpness_grad_ref = refs[0], refs[1]
    key_part_refs, value_part_refs = refs[2:5], refs[5:8]
    bias_ref, valid_ref = refs[8], refs[9]
    work = [refs[10 + 4 * j : 14 + 4 * j] for j in range(together)]
    head_dim = query_ref.shape[1] // together
    time_tile = lax.axis_index("tm")
    high_tile = lax.axis_index("height")
    high_count, time_count = counts_ref.shape[0], counts_ref.shape[1]
    time_shift = shifts_ref[2 * high_tile, time_tile]
    high_shift = shifts_ref[2 * high_tile + 1, time_tile]

    @pl.when(pl.program_id(0) == 0)
    def _():
        limits = []
        for dt, dh in KEY_TILES:
            t, h = time_tile + dt, high_tile + dh
            inside = (t >= 0) & (t < time_count) & (h >= 0) & (h < high_count)
            inside &= (jnp.abs(dt - time_shift) <= 1) & (jnp.abs(dh - high_shift) <= 1)
            count = counts_ref[jnp.clip(h, 0, high_count - 1), jnp.clip(t, 0, time_count - 1)]
            limits.append(jnp.where(inside, count, 0))
        place = lax.broadcasted_iota(jnp.int32, slot_row_ref.shape, 1)
        limit_row = jnp.full(slot_row_ref.shape, limits[0], jnp.int32)
        for n in range(1, len(limits)):
            limit_row = jnp.where(place >= n * tile_len, limits[n], limit_row)
        bias_ref[...] = jnp.where(slot_row_ref[...] < limit_row, 0.0, HIDDEN)
        own_count = counts_ref[high_tile, time_tile]
        valid_ref[...] = jnp.where(slot_col_ref[...] < own_count, 1.0, 0.0)

    def tile(ref, n):
        return ref[n * tile_len : (n + 1) * tile_len]

    def operands(j):
        columns = slice(j * head_dim, (j + 1) * head_dim)
        keys = jnp.concatenate([ref[:, columns] for ref in key_refs], axis=0)
        values = jnp.concatenate(
            [tile(value_refs[b], n)[:, columns] for b, n in VALUE_SPOTS], axis=0
        )
        return query_ref[:, columns], grad_ref[:, columns], keys, values

    def gradients(j):
        columns = slice(j * head_dim, (j + 1) * head_dim)
        query, grad, keys, values = operands(j)
        sharp = sharpness_ref[opening + pl.program_id(0) * together + j]
        factor = sharp * (1.0 / math.sqrt(head_dim))
        logits_ref, grad_weight_ref, low_ref, scaled_ref = work[j]
        score_gradients(factor * math.log2(math.e), bias_ref, valid_ref, *work[j])
        low, scaled = low_ref[...], scaled_ref[...]
        down = (((0,), (0,)), ((), ()))
        query_grad = jnp.dot(scaled, keys, preferred_element_type=jnp.float32) * factor
        query_grad_ref[:, columns] = query_grad.astype(jnp.bfloat16)
        sharpness_grad_ref[j] = jnp.sum(
            query_grad * query.astype(jnp.float32), axis=0, keepdims=True
        ) * (1.0 / sharp)
        part_key = lax.dot_general(scaled, query, down, preferred_element_type=jnp.float32)
        part_key = (part_key * factor).astype(jnp.bfloat16)
        part_value = lax.dot_general(low, grad, down, preferred_element_type=jnp.float32)
        part_value = part_value.astype(jnp.bfloat16)
        for n, ref in enumerate(key_part_refs):
            ref[:, columns] = part_key[3 * n * tile_len : 3 * (n + 1) * tile_len]
        for place, (b, n) in enumerate(VALUE_SPOTS):
            value_part_refs[b][n * tile_len : (n + 1) * tile_len, columns] = tile(
                part_value, place
            )

    raw_scores(*operands(0), *work[0][:2])
    for j in range(together):
        if j + 1 < together:
            raw_scores(*operands(j + 1), *work[j + 1][:2])
        gradients(j)


def attention(chunk, branches, tile_len, head_dim, small, query, grad, keys, values, so_far):
    opening, heads = chunk
    together = 2
    first = opening // together
    smem = pl.BlockSpec(memory_space=pltpu.SMEM)
    whole = lambda array: pl.BlockSpec(array.shape, lambda h: (0, 0))
    side = pl.BlockSpec((tile_len, together * head_dim), lambda h: (0, first + h))
    near = pl.BlockSpec((3 * tile_len, together * head_dim), lambda h: (0, h))
    out_near = pl.BlockSpec((3 * tile_len, together * head_dim), lambda h: (0, first + h))
    part = jax.ShapeDtypeStruct((3 * tile_len, branches * head_dim), jnp.bfloat16)
    pairs = heads * tile_len * 9 * tile_len
    score = (tile_len, 9 * tile_len)
    return pl.pallas_call(
        functools.partial(attention_body, opening, tile_len, together, len(so_far)),
        grid=(heads // together,),
        in_specs=[smem] * 3
        + [whole(small[3]), whole(small[4]), side, side]
        + [near] * 6
        + [pl.BlockSpec(memory_space=pl.ANY)] * len(so_far),
        out_specs=[side, pl.BlockSpec((together, 1, head_dim), lambda h: (first + h, 0, 0))]
        + [out_near] * 6,
        out_shape=[
            jax.ShapeDtypeStruct((tile_len, branches * head_dim), jnp.bfloat16),
            jax.ShapeDtypeStruct((branches, 1, head_dim), jnp.float32),
        ]
        + [part] * 6,
        input_output_aliases={13 + n: n for n in range(len(so_far))},
        scratch_shapes=[
            pltpu.VMEM((1, 9 * tile_len), jnp.float32),
            pltpu.VMEM((tile_len, 1), jnp.float32),
        ]
        + [
            pltpu.VMEM(score, jnp.float32),
            pltpu.VMEM(score, jnp.float32),
            pltpu.VMEM(score, jnp.bfloat16),
            pltpu.VMEM(score, jnp.bfloat16),
        ]
        * together,
        compiler_params=pltpu.CompilerParams(vmem_limit_bytes=16 * 1024 * 1024),
        cost_estimate=pl.CostEstimate(
            flops=10 * pairs * head_dim,
            bytes_accessed=12 * 3 * tile_len * heads * head_dim * 2,
            transcendentals=pairs,
        ),
    )(*small, query, grad, *keys, *values, *so_far)


def pack_body(chunks, *refs):
    inputs, outputs = refs[:3], refs[3:]
    tile_len = inputs[0].shape[0]
    head_dim = inputs[0].shape[1] // sum(heads for _, heads in chunks)
    for (opening, heads), out_ref in zip(chunks, outputs):
        columns = slice(opening * head_dim, (opening + heads) * head_dim)
        for n in range(3):
            out_ref[n * tile_len : (n + 1) * tile_len] = inputs[n][:, columns]


def packed(chunks, line):
    tile_len, width = line[0].shape
    per_head = width // sum(heads for _, heads in chunks)
    vmem = pl.BlockSpec(memory_space=pltpu.VMEM)
    return pl.pallas_call(
        functools.partial(pack_body, chunks),
        in_specs=[vmem] * 3,
        out_specs=[vmem] * len(chunks),
        out_shape=[
            jax.ShapeDtypeStruct((3 * tile_len, heads * per_head), jnp.bfloat16)
            for _, heads in chunks
        ],
        compiler_params=pltpu.CompilerParams(vmem_limit_bytes=8 * 1024 * 1024),
    )(*line)


def on_device(
    probe_vectors,
    lookup_vectors,
    payload_vectors,
    result_derivative,
    patch_occupancy,
    patch_neighborhood_offset,
    sharpness,
):
    _, frames, rows, cols, width = probe_vectors.shape
    tile_len = frames * rows * cols
    branches = sharpness.shape[0]
    head_dim = width // branches

    def as_tokens(field):
        return jnp.transpose(field[0], (0, 2, 1, 3)).reshape(tile_len, width)

    def as_field(tokens):
        return jnp.transpose(tokens.reshape(frames, cols, rows, width), (0, 2, 1, 3))[None]

    spot = np.arange(tile_len)
    slot = (spot // (cols * rows) * rows + spot % rows) * cols + spot // rows % cols
    slot_row = jnp.asarray(np.tile(slot, 9)[None, :], jnp.int32)
    slot_col = jnp.asarray(slot[:, None], jnp.int32)
    counts = patch_occupancy[0].T
    shifts = jnp.transpose(patch_neighborhood_offset[0], (1, 2, 0)).reshape(-1, counts.shape[1])
    small = (sharpness, counts, shifts, slot_row, slot_col)

    query, key, value, grad = (
        as_tokens(f) for f in (probe_vectors, lookup_vectors, payload_vectors, result_derivative)
    )
    chunks = ((0, 6), (6, 6))
    key_blocks = packed(chunks, (key, shifted(key, "tm", 1), shifted(key, "tm", -1)))
    value_blocks = packed(
        chunks, (value, shifted(value, "height", 1), shifted(value, "height", -1))
    )
    near = [
        (
            (keys, shifted(keys, "height", 1), shifted(keys, "height", -1)),
            (values, shifted(values, "tm", 1), shifted(values, "tm", -1)),
        )
        for keys, values in zip(key_blocks, value_blocks)
    ]
    results = ()
    for chunk, (keys, values) in zip(chunks, near):
        results = attention(
            chunk, branches, tile_len, head_dim, small, query, grad, keys, values, results
        )
    query_grad, sharpness_grad = results[0], results[1]

    def met(parts, second):
        own, below, above = parts
        return own, shifted(below, second, -1), shifted(above, second, 1)

    def completed(own, below, above, first):
        return (
            own
            + shifted(below, first, -1).astype(jnp.float32)
            + shifted(above, first, 1).astype(jnp.float32)
        ).astype(jnp.bfloat16)

    key_parts = met(results[2:5], "height")
    value_parts = met(results[5:8], "tm")
    row = jnp.sum(sharpness_grad, axis=(1, 2))
    all_rows = gathered_everywhere(jnp.pad(row, (0, -branches % 128))[None])
    summed = sum(part.astype(jnp.float32) for part in key_parts)
    key_grad = completed(
        summed[:tile_len],
        summed[tile_len : 2 * tile_len].astype(jnp.bfloat16),
        summed[2 * tile_len :].astype(jnp.bfloat16),
        "tm",
    )
    row, *summed = summed_parts(all_rows, *value_parts)
    value_grad = completed(*summed, "height")
    return as_field(query_grad), as_field(key_grad), as_field(value_grad), row[0, :branches]


def solution(mesh):
    field = P("dp", "tm", "height", None, None)
    return jax.shard_map(
        on_device,
        mesh=mesh,
        in_specs=(field,) * 4 + (P("dp", None, None), P("dp", None, None, None), P()),
        out_specs=(field,) * 3 + (P(),),
        check_vma=False,
    )
```

profile of v0, /device:TPU:124, one launch (start us, length us, event | category | flops | bytes accessed | tf_op | source)
XLA Modules:
  0.0 155.0 jit_solution(8016092891747212055)
XLA Ops:
  0.6 3.3 %collective-permute-start.5 = (bf16[144,1536]{1,0:T(8,128)(2,1)}, bf16[144,1536]{1,0:T(8,128)(2,1)S(1)}, u32[]{:S(2)}, u32[]{:S(2)}) collective-permute-start(bf16[144,1536]{1,0:T(8,128)(2,1)} %bitcast.46), channel_id=1, source_target_pairs={{1,0},{2,1},{3,2},{5,4},{6,5},{7,6},{9,8},{10,9},{11,10},{13,12},{... | collective-permute-start | bytes 1327112 | tf_op jit(solution)/shard_map/ppermute | solution.py:19
  3.9 1.3 collective-permute-start.4
  5.2 0.0 copy-start.9
  5.2 1.9 %collective-permute-start.1 = (bf16[144,1536]{1,0:T(8,128)(2,1)}, bf16[144,1536]{1,0:T(8,128)(2,1)S(1)}, u32[]{:S(2)}, u32[]{:S(2)}) collective-permute-start(bf16[144,1536]{1,0:T(8,128)(2,1)} %bitcast.49), channel_id=1, source_target_pairs={{4,0},{8,4},{12,8},{16,12},{20,16},{24,20},{28,24},{5,1},{9,5},{13... | collective-permute-start | bytes 1327112 | tf_op jit(solution)/shard_map/ppermute | solution.py:19
  7.2 4.3 %collective-permute-start = (bf16[144,1536]{1,0:T(8,128)(2,1)}, bf16[144,1536]{1,0:T(8,128)(2,1)S(1)}, u32[]{:S(2)}, u32[]{:S(2)}) collective-permute-start(bf16[144,1536]{1,0:T(8,128)(2,1)} %bitcast.50), channel_id=1, source_target_pairs={{0,4},{4,8},{8,12},{12,16},{16,20},{20,24},{24,28},{1,5},{5,9},{9,... | collective-permute-start | bytes 1327112 | tf_op jit(solution)/shard_map/ppermute | solution.py:19
  11.4 2.2 %collective-permute-done.5.refs_2_ = bf16[144,1536]{1,0:T(8,128)(2,1)S(1)} collective-permute-done((bf16[144,1536]{1,0:T(8,128)(2,1)}, bf16[144,1536]{1,0:T(8,128)(2,1)S(1)}, u32[]{:S(2)}, u32[]{:S(2)}) %collective-permute-start.5) | collective-permute-done | bytes 442400 | tf_op jit(solution)/shard_map/ppermute | solution.py:19
  13.6 4.0 %collective-permute-done.4.refs_1_ = bf16[144,1536]{1,0:T(8,128)(2,1)S(1)} collective-permute-done((bf16[144,1536]{1,0:T(8,128)(2,1)}, bf16[144,1536]{1,0:T(8,128)(2,1)S(1)}, u32[]{:S(2)}, u32[]{:S(2)}) %collective-permute-start.4) | collective-permute-done | bytes 442400 | tf_op jit(solution)/shard_map/ppermute | solution.py:19
  17.7 1.0 copy-done.2
  18.7 0.0 copy-start.6
  18.7 0.0 copy-start.7
  18.7 0.0 copy-start.8
  18.7 0.1 shard_map.121
  18.8 2.1 %collective-permute-start.11 = (bf16[432,768]{1,0:T(8,128)(2,1)S(1)}, bf16[432,768]{1,0:T(8,128)(2,1)S(1)}, u32[]{:S(2)}, u32[]{:S(2)}) collective-permute-start(bf16[432,768]{1,0:T(8,128)(2,1)S(1)} %get-tuple-element.31.refs_3_), channel_id=1, source_target_pairs={{4,0},{8,4},{12,8},{16,12},{20,16},{24,20},{28,24},{5,1},{9,5},{13... | collective-permute-start | bytes 1990664 | tf_op jit(solution)/shard_map/ppermute | solution.py:19
  20.9 4.3 %collective-permute-start.10 = (bf16[432,768]{1,0:T(8,128)(2,1)S(1)}, bf16[432,768]{1,0:T(8,128)(2,1)S(1)}, u32[]{:S(2)}, u32[]{:S(2)}) collective-permute-start(bf16[432,768]{1,0:T(8,128)(2,1)S(1)} %get-tuple-element.31.refs_3_), channel_id=1, source_target_pairs={{0,4},{4,8},{8,12},{12,16},{16,20},{20,24},{24,28},{1,5},{5,9},{9,... | collective-permute-start | bytes 1990664 | tf_op jit(solution)/shard_map/ppermute | solution.py:19
  25.2 0.0 collective-permute-done.1.refs_2_
  25.2 0.0 collective-permute-done.refs_1_
  25.2 0.0 copy-done.3
  25.2 0.1 shard_map.120
  25.3 3.3 %collective-permute-start.9 = (bf16[432,768]{1,0:T(8,128)(2,1)S(1)}, bf16[432,768]{1,0:T(8,128)(2,1)S(1)}, u32[]{:S(2)}, u32[]{:S(2)}) collective-permute-start(bf16[432,768]{1,0:T(8,128)(2,1)S(1)} %get-tuple-element.30.refs_0_), channel_id=1, source_target_pairs={{1,0},{2,1},{3,2},{5,4},{6,5},{7,6},{9,8},{10,9},{11,10},{13,12},{... | collective-permute-start | bytes 1990664 | tf_op jit(solution)/shard_map/ppermute | solution.py:19
  28.6 1.3 collective-permute-start.8
  29.9 1.9 %collective-permute-start.7 = (bf16[432,768]{1,0:T(8,128)(2,1)S(1)}, bf16[432,768]{1,0:T(8,128)(2,1)S(1)}, u32[]{:S(2)}, u32[]{:S(2)}) collective-permute-start(bf16[432,768]{1,0:T(8,128)(2,1)S(1)} %get-tuple-element.29.refs_3_), channel_id=1, source_target_pairs={{4,0},{8,4},{12,8},{16,12},{20,16},{24,20},{28,24},{5,1},{9,5},{13... | collective-permute-start | bytes 1990664 | tf_op jit(solution)/shard_map/ppermute | solution.py:19
  31.8 7.2 %collective-permute-done.11.refs_5_ = bf16[432,768]{1,0:T(8,128)(2,1)S(1)} collective-permute-done((bf16[432,768]{1,0:T(8,128)(2,1)S(1)}, bf16[432,768]{1,0:T(8,128)(2,1)S(1)}, u32[]{:S(2)}, u32[]{:S(2)}) %collective-permute-start.11) | collective-permute-done | bytes 663584 | tf_op jit(solution)/shard_map/ppermute | solution.py:19
  39.0 4.3 %collective-permute-start.6 = (bf16[432,768]{1,0:T(8,128)(2,1)S(1)}, bf16[432,768]{1,0:T(8,128)(2,1)S(1)}, u32[]{:S(2)}, u32[]{:S(2)}) collective-permute-start(bf16[432,768]{1,0:T(8,128)(2,1)S(1)} %get-tuple-element.29.refs_3_), channel_id=1, source_target_pairs={{0,4},{4,8},{8,12},{12,16},{16,20},{20,24},{24,28},{1,5},{5,9},{9,... | collective-permute-start | bytes 1990664 | tf_op jit(solution)/shard_map/ppermute | solution.py:19
  43.3 0.0 collective-permute-done.10.refs_4_
  43.3 2.7 %collective-permute-start.3 = (bf16[432,768]{1,0:T(8,128)(2,1)S(1)}, bf16[432,768]{1,0:T(8,128)(2,1)S(1)}, u32[]{:S(2)}, u32[]{:S(2)}) collective-permute-start(bf16[432,768]{1,0:T(8,128)(2,1)S(1)} %get-tuple-element.28.refs_0_), channel_id=1, source_target_pairs={{1,0},{2,1},{3,2},{5,4},{6,5},{7,6},{9,8},{10,9},{11,10},{13,12},{... | collective-permute-start | bytes 1990664 | tf_op jit(solution)/shard_map/ppermute | solution.py:19
  46.0 0.0 collective-permute-done.9.refs_2_
  46.0 1.3 collective-permute-start.2
  47.4 0.0 copy-done.10
  47.4 0.0 collective-permute-done.8.refs_1_
  47.4 0.0 copy-done.9
  47.5 9.3 %shard_map.122 = (bf16[144,1536]{1,0:T(8,128)(2,1)}, f32[12,1,128]{2,1,0:T(1,128)S(1)}, bf16[432,1536]{1,0:T(8,128)(2,1)S(1)}, bf16[432,1536]{1,0:T(8,128)(2,1)}...) custom-call(f32[12]{0:T(128)S(1)} %copy-done.9, ...), custom_call_target="tpu_custom_call" | custom-call | flops 1433272320 | bytes 7962624 | tf_op jit(solution)/shard_map/pallas_call | solution.py:188
  56.7 0.0 collective-permute-done.7.refs_5_
  56.7 0.0 collective-permute-done.6.refs_4_
  56.7 0.0 collective-permute-done.3.refs_2_
  56.8 3.9 %collective-permute-done.2.refs_1_ = bf16[432,768]{1,0:T(8,128)(2,1)S(1)} collective-permute-done((bf16[432,768]{1,0:T(8,128)(2,1)S(1)}, bf16[432,768]{1,0:T(8,128)(2,1)S(1)}, u32[]{:S(2)}, u32[]{:S(2)}) %collective-permute-start.2) | collective-permute-done | bytes 663584 | tf_op jit(solution)/shard_map/ppermute | solution.py:19
  60.7 9.3 %shard_map.123 = (bf16[144,1536]{1,0:T(8,128)(2,1)}, f32[12,1,128]{2,1,0:T(1,128)S(1)}, bf16[432,1536]{1,0:T(8,128)(2,1)S(1)}, bf16[432,1536]{1,0:T(8,128)(2,1)}...) custom-call(f32[12]{0:T(128)S(1)} %copy-done.9, ...), custom_call_target="tpu_custom_call", output_to_operand_aliasing={{0}: (13, {}), {1}: (14, {}), {2}: (15, {}), {3}: (16, {}),... | custom-call | flops 1433272320 | bytes 7962624 | tf_op jit(solution)/shard_map/pallas_call | solution.py:188
  69.9 1.1 copy-done
  71.0 1.1 copy-done.1
  72.1 4.3 %collective-permute-start.12 = (bf16[432,1536]{1,0:T(8,128)(2,1)}, bf16[432,1536]{1,0:T(8,128)(2,1)}, u32[]{:S(2)}, u32[]{:S(2)}) collective-permute-start(bf16[432,1536]{1,0:T(8,128)(2,1)} %get-tuple-element.42), channel_id=1, source_target_pairs={{1,0},{2,1},{3,2},{5,4},{6,5},{7,6},{9,8},{10,9},{11,10},{13,12},{... | collective-permute-start | bytes 3981320 | tf_op jit(solution)/shard_map/ppermute | solution.py:19
  76.4 1.3 collective-permute-start.13
  77.7 0.2 reduce_sum.9
  77.8 0.8 broadcast_in_dim.16
  78.7 18.4 %all-to-all-start = ((f32[512,1,128]{2,1,0:T(1,128)}), f32[512,1,128]{2,1,0:T(1,128)S(1)}, u32[]{:S(2)}, u32[]{:S(2)}) async-start(f32[512,1,128]{2,1,0:T(1,128)} %broadcast_in_dim.16), calls=%async_computation | async-start | bytes 524288 | tf_op jit(solution)/shard_map/all_to_all | solution.py:25
  97.1 1.9 %collective-permute-start.16 = (bf16[432,1536]{1,0:T(8,128)(2,1)}, bf16[432,1536]{1,0:T(8,128)(2,1)}, u32[]{:S(2)}, u32[]{:S(2)}) collective-permute-start(bf16[432,1536]{1,0:T(8,128)(2,1)} %copy-done), channel_id=1, source_target_pairs={{4,0},{8,4},{12,8},{16,12},{20,16},{24,20},{28,24},{5,1},{9,5},{13... | collective-permute-start | bytes 3981320 | tf_op jit(solution)/shard_map/ppermute | solution.py:19
  99.0 3.9 %collective-permute-start.17 = (bf16[432,1536]{1,0:T(8,128)(2,1)}, bf16[432,1536]{1,0:T(8,128)(2,1)}, u32[]{:S(2)}, u32[]{:S(2)}) collective-permute-start(bf16[432,1536]{1,0:T(8,128)(2,1)} %copy-done.1), channel_id=1, source_target_pairs={{0,4},{4,8},{8,12},{12,16},{16,20},{20,24},{24,28},{1,5},{5,9},{9,... | collective-permute-start | bytes 3981320 | tf_op jit(solution)/shard_map/ppermute | solution.py:19
  102.9 0.4 collective-permute-done.12
  103.3 5.0 %collective-permute-done.13 = bf16[432,1536]{1,0:T(8,128)(2,1)} collective-permute-done((bf16[432,1536]{1,0:T(8,128)(2,1)}, bf16[432,1536]{1,0:T(8,128)(2,1)}, u32[]{:S(2)}, u32[]{:S(2)}) %collective-permute-start.13) | collective-permute-done | bytes 1327136 | tf_op jit(solution)/shard_map/ppermute | solution.py:19
  108.3 3.7 %fusion.2 = (bf16[432,1536]{1,0:T(8,128)(2,1)S(1)}, f32[432,1536]{1,0:T(8,128)}) fusion(bf16[432,1536]{1,0:T(8,128)(2,1)} %collective-permute-done.13, bf16[432,1536]{1,0:T(8,128)(2,1)} %collective-permute-done.12, bf16[432,1536]{1,0:T(8,128)(2,1)S(1)} %get-tuple-element.41), kind=kLoop, calls=%fused_computation.7 | loop fusion | flops 3981312 | bytes 7962624 | tf_op jit(solution)/shard_map/convert.1
  112.0 0.1 fusion.3
  112.1 1.9 %collective-permute-start.14 = (bf16[144,1536]{1,0:T(8,128)(2,1)S(1)}, bf16[144,1536]{1,0:T(8,128)(2,1)S(1)}, u32[]{:S(2)}, u32[]{:S(2)}) collective-permute-start(bf16[144,1536]{1,0:T(8,128)(2,1)S(1)} %get-tuple-element.54), channel_id=1, source_target_pairs={{4,0},{8,4},{12,8},{16,12},{20,16},{24,20},{28,24},{5,1},{9,5},{13... | collective-permute-start | bytes 1327112 | tf_op jit(solution)/shard_map/ppermute | solution.py:19
  114.0 4.9 %collective-permute-start.15 = (bf16[144,1536]{1,0:T(8,128)(2,1)S(1)}, bf16[144,1536]{1,0:T(8,128)(2,1)}, u32[]{:S(2)}, u32[]{:S(2)}) collective-permute-start(bf16[144,1536]{1,0:T(8,128)(2,1)S(1)} %get-tuple-element.55), channel_id=1, source_target_pairs={{0,4},{4,8},{8,12},{12,16},{16,20},{20,24},{24,28},{1,5},{5,9},{9,... | collective-permute-start | bytes 1327112 | tf_op jit(solution)/shard_map/ppermute | solution.py:19
  119.0 0.0 all-to-all-done.rows_ref
  119.0 15.3 %collective-permute-done.16.below_ref = bf16[432,1536]{1,0:T(8,128)(2,1)} collective-permute-done((bf16[432,1536]{1,0:T(8,128)(2,1)}, bf16[432,1536]{1,0:T(8,128)(2,1)}, u32[]{:S(2)}, u32[]{:S(2)}) %collective-permute-start.16) | collective-permute-done | bytes 1327136 | tf_op jit(solution)/shard_map/ppermute | solution.py:19
  134.3 1.0 collective-permute-done.17.above_ref
  135.2 2.7 %shard_map.124 = (f32[1,128]{1,0:T(1,128)S(1)}, f32[144,1536]{1,0:T(8,128)S(1)}, bf16[144,1536]{1,0:T(8,128)(2,1)S(1)}, bf16[144,1536]{1,0:T(8,128)(2,1)S(1)}) custom-call(f32[512,1,128]{2,1,0:T(1,128)S(1)} %all-to-all-done.rows_ref, bf16[432,1536]{1,0:T(8,128)(2,1)S(1)} %get-tuple-element.45.own_ref, bf16[432,1536]{1,0:T(8,128)(2,1)} %collective-permute-done.16.below_ref, ...), custom_call_target="tpu_custom_call" | custom-call | tf_op jit(solution)/shard_map/pallas_call | solution.py:47
  137.9 3.0 %collective-permute-start.18 = (bf16[144,1536]{1,0:T(8,128)(2,1)S(1)}, bf16[144,1536]{1,0:T(8,128)(2,1)S(1)}, u32[]{:S(2)}, u32[]{:S(2)}) collective-permute-start(bf16[144,1536]{1,0:T(8,128)(2,1)S(1)} %get-tuple-element.49), channel_id=1, source_target_pairs={{1,0},{2,1},{3,2},{5,4},{6,5},{7,6},{9,8},{10,9},{11,10},{13,12},{... | collective-permute-start | bytes 1327112 | tf_op jit(solution)/shard_map/ppermute | solution.py:19
  141.0 1.3 collective-permute-start.19
  142.3 0.5 slice_bitcast_fusion
  142.8 0.6 collective-permute-done.14
  143.3 0.9 collective-permute-done.15
  144.3 2.2 %fusion.1 = bf16[144,1536]{1,0:T(8,128)(2,1)} fusion(f32[432,1536]{1,0:T(8,128)} %get-tuple-element.53, bf16[144,1536]{1,0:T(8,128)(2,1)} %collective-permute-done.15, bf16[144,1536]{1,0:T(8,128)(2,1)S(1)} %collective-permute-done.14), kind=kLoop, calls=%fused_computation.3 | loop fusion | flops 1105920 | bytes 2211840 | tf_op jit(solution)/shard_map/convert_element_type | solution.py:308
  146.4 3.5 %collective-permute-done.18 = bf16[144,1536]{1,0:T(8,128)(2,1)S(1)} collective-permute-done((bf16[144,1536]{1,0:T(8,128)(2,1)S(1)}, bf16[144,1536]{1,0:T(8,128)(2,1)S(1)}, u32[]{:S(2)}, u32[]{:S(2)}) %collective-permute-start.18) | collective-permute-done | bytes 442400 | tf_op jit(solution)/shard_map/ppermute | solution.py:19
  150.0 4.1 %collective-permute-done.19 = bf16[144,1536]{1,0:T(8,128)(2,1)S(1)} collective-permute-done((bf16[144,1536]{1,0:T(8,128)(2,1)S(1)}, bf16[144,1536]{1,0:T(8,128)(2,1)S(1)}, u32[]{:S(2)}, u32[]{:S(2)}) %collective-permute-start.19) | collective-permute-done | bytes 442400 | tf_op jit(solution)/shard_map/ppermute | solution.py:19
  154.1 0.9 add_convert_fusion
  (15 shorter events, 0.0 us)
Async XLA Ops:
  0.6 13.0 %collective-permute-start.5 = (bf16[144,1536]{1,0:T(8,128)(2,1)}, bf16[144,1536]{1,0:T(8,128)(2,1)S(1)}, u32[]{:S(2)}, u32[]{:S(2)}) collective-permute-start(bf16[144,1536]{1,0:T(8,128)(2,1)} %bitcast.46), channel_id=1, source_target_pairs={{1,0},{2,1},{3,2},{5,4},{6,5},{7,6},{9,8},{10,9},{11,10},{13,12},{... | collective-permute-start | bytes 1327112 | tf_op jit(solution)/shard_map/ppermute | solution.py:19
  3.9 13.7 %collective-permute-start.4 = (bf16[144,1536]{1,0:T(8,128)(2,1)}, bf16[144,1536]{1,0:T(8,128)(2,1)S(1)}, u32[]{:S(2)}, u32[]{:S(2)}) collective-permute-start(bf16[144,1536]{1,0:T(8,128)(2,1)} %bitcast.47), channel_id=1, source_target_pairs={{0,1},{1,2},{2,3},{4,5},{5,6},{6,7},{8,9},{9,10},{10,11},{12,13},{... | collective-permute-start | bytes 1327112 | tf_op jit(solution)/shard_map/ppermute | solution.py:19
  5.2 42.2 %copy-start.9 = (f32[12]{0:T(128)S(1)}, f32[12]{0:T(128)}, u32[]{:S(2)}) copy-start(f32[12]{0:T(128)} %sharpness_ref.3) | copy-start | bytes 148
  5.2 19.9 %collective-permute-start.1 = (bf16[144,1536]{1,0:T(8,128)(2,1)}, bf16[144,1536]{1,0:T(8,128)(2,1)S(1)}, u32[]{:S(2)}, u32[]{:S(2)}) collective-permute-start(bf16[144,1536]{1,0:T(8,128)(2,1)} %bitcast.49), channel_id=1, source_target_pairs={{4,0},{8,4},{12,8},{16,12},{20,16},{24,20},{28,24},{5,1},{9,5},{13... | collective-permute-start | bytes 1327112 | tf_op jit(solution)/shard_map/ppermute | solution.py:19
  7.2 18.0 %collective-permute-start = (bf16[144,1536]{1,0:T(8,128)(2,1)}, bf16[144,1536]{1,0:T(8,128)(2,1)S(1)}, u32[]{:S(2)}, u32[]{:S(2)}) collective-permute-start(bf16[144,1536]{1,0:T(8,128)(2,1)} %bitcast.50), channel_id=1, source_target_pairs={{0,4},{4,8},{8,12},{12,16},{16,20},{20,24},{24,28},{1,5},{5,9},{9,... | collective-permute-start | bytes 1327112 | tf_op jit(solution)/shard_map/ppermute | solution.py:19
  17.7 1.0 copy-start.2
  18.7 6.5 %copy-start.3 = (bf16[1,6,8,3,1536]{4,2,3,1,0:T(8,128)(2,1)S(1)}, bf16[1,6,8,3,1536]{4,2,3,1,0:T(8,128)(2,1)}, u32[]{:S(2)}) copy-start(bf16[1,6,8,3,1536]{4,2,3,1,0:T(8,128)(2,1)} %param.10) | copy-start | bytes 1327108
  18.7 28.7 %copy-start.10 = (s32[1,8,4,2]{1,3,2,0:T(2,128)S(1)}, s32[1,8,4,2]{1,3,2,0:T(2,128)}, u32[]{:S(2)}) copy-start(s32[1,8,4,2]{1,3,2,0:T(2,128)} %param.14) | copy-start | bytes 772
  18.7 28.7 %copy-start.4 = (bf16[1,6,8,3,1536]{4,2,3,1,0:T(8,128)(2,1)S(1)}, bf16[1,6,8,3,1536]{4,2,3,1,0:T(8,128)(2,1)}, u32[]{:S(2)}) copy-start(bf16[1,6,8,3,1536]{4,2,3,1,0:T(8,128)(2,1)} %param.9) | copy-start | bytes 1327108
  18.7 28.7 %copy-start.5 = (bf16[1,6,8,3,1536]{4,2,3,1,0:T(8,128)(2,1)S(1)}, bf16[1,6,8,3,1536]{4,2,3,1,0:T(8,128)(2,1)}, u32[]{:S(2)}) copy-start(bf16[1,6,8,3,1536]{4,2,3,1,0:T(8,128)(2,1)} %param.12) | copy-start | bytes 1327108
  18.7 28.7 %copy-start.6 = (s32[144,1]{1,0:T(8,128)S(1)}, s32[144,1]{1,0:T(8,128)}, u32[]{:S(2)}) copy-start(s32[144,1]{1,0:T(8,128)} %constant.9.clone.slot_col_ref) | copy-start | bytes 1732
  18.7 28.7 %copy-start.7 = (s32[1,1296]{1,0:T(1,128)S(1)}, s32[1,1296]{1,0:T(1,128)}, u32[]{:S(2)}) copy-start(s32[1,1296]{1,0:T(1,128)} %constant.8.clone.slot_row_ref) | copy-start | bytes 15556
  18.7 28.7 %copy-start.8 = (s32[1,8,4]{1,2,0:T(4,128)S(1)}, s32[1,8,4]{1,2,0:T(4,128)}, u32[]{:S(2)}) copy-start(s32[1,8,4]{1,2,0:T(4,128)} %param.13) | copy-start | bytes 388
  18.8 20.2 %collective-permute-start.11 = (bf16[432,768]{1,0:T(8,128)(2,1)S(1)}, bf16[432,768]{1,0:T(8,128)(2,1)S(1)}, u32[]{:S(2)}, u32[]{:S(2)}) collective-permute-start(bf16[432,768]{1,0:T(8,128)(2,1)S(1)} %get-tuple-element.31.refs_3_), channel_id=1, source_target_pairs={{4,0},{8,4},{12,8},{16,12},{20,16},{24,20},{28,24},{5,1},{9,5},{13... | collective-permute-start | bytes 1990664 | tf_op jit(solution)/shard_map/ppermute | solution.py:19
  20.9 22.4 %collective-permute-start.10 = (bf16[432,768]{1,0:T(8,128)(2,1)S(1)}, bf16[432,768]{1,0:T(8,128)(2,1)S(1)}, u32[]{:S(2)}, u32[]{:S(2)}) collective-permute-start(bf16[432,768]{1,0:T(8,128)(2,1)S(1)} %get-tuple-element.31.refs_3_), channel_id=1, source_target_pairs={{0,4},{4,8},{8,12},{12,16},{16,20},{20,24},{24,28},{1,5},{5,9},{9,... | collective-permute-start | bytes 1990664 | tf_op jit(solution)/shard_map/ppermute | solution.py:19
  25.3 20.8 %collective-permute-start.9 = (bf16[432,768]{1,0:T(8,128)(2,1)S(1)}, bf16[432,768]{1,0:T(8,128)(2,1)S(1)}, u32[]{:S(2)}, u32[]{:S(2)}) collective-permute-start(bf16[432,768]{1,0:T(8,128)(2,1)S(1)} %get-tuple-element.30.refs_0_), channel_id=1, source_target_pairs={{1,0},{2,1},{3,2},{5,4},{6,5},{7,6},{9,8},{10,9},{11,10},{13,12},{... | collective-permute-start | bytes 1990664 | tf_op jit(solution)/shard_map/ppermute | solution.py:19
  28.6 18.8 %collective-permute-start.8 = (bf16[432,768]{1,0:T(8,128)(2,1)S(1)}, bf16[432,768]{1,0:T(8,128)(2,1)S(1)}, u32[]{:S(2)}, u32[]{:S(2)}) collective-permute-start(bf16[432,768]{1,0:T(8,128)(2,1)S(1)} %get-tuple-element.30.refs_0_), channel_id=1, source_target_pairs={{0,1},{1,2},{2,3},{4,5},{5,6},{6,7},{8,9},{9,10},{10,11},{12,13},{... | collective-permute-start | bytes 1990664 | tf_op jit(solution)/shard_map/ppermute | solution.py:19
  29.9 26.9 %collective-permute-start.7 = (bf16[432,768]{1,0:T(8,128)(2,1)S(1)}, bf16[432,768]{1,0:T(8,128)(2,1)S(1)}, u32[]{:S(2)}, u32[]{:S(2)}) collective-permute-start(bf16[432,768]{1,0:T(8,128)(2,1)S(1)} %get-tuple-element.29.refs_3_), channel_id=1, source_target_pairs={{4,0},{8,4},{12,8},{16,12},{20,16},{24,20},{28,24},{5,1},{9,5},{13... | collective-permute-start | bytes 1990664 | tf_op jit(solution)/shard_map/ppermute | solution.py:19
  39.0 17.7 %collective-permute-start.6 = (bf16[432,768]{1,0:T(8,128)(2,1)S(1)}, bf16[432,768]{1,0:T(8,128)(2,1)S(1)}, u32[]{:S(2)}, u32[]{:S(2)}) collective-permute-start(bf16[432,768]{1,0:T(8,128)(2,1)S(1)} %get-tuple-element.29.refs_3_), channel_id=1, source_target_pairs={{0,4},{4,8},{8,12},{12,16},{16,20},{20,24},{24,28},{1,5},{5,9},{9,... | collective-permute-start | bytes 1990664 | tf_op jit(solution)/shard_map/ppermute | solution.py:19
  43.3 13.4 %collective-permute-start.3 = (bf16[432,768]{1,0:T(8,128)(2,1)S(1)}, bf16[432,768]{1,0:T(8,128)(2,1)S(1)}, u32[]{:S(2)}, u32[]{:S(2)}) collective-permute-start(bf16[432,768]{1,0:T(8,128)(2,1)S(1)} %get-tuple-element.28.refs_0_), channel_id=1, source_target_pairs={{1,0},{2,1},{3,2},{5,4},{6,5},{7,6},{9,8},{10,9},{11,10},{13,12},{... | collective-permute-start | bytes 1990664 | tf_op jit(solution)/shard_map/ppermute | solution.py:19
  46.0 14.6 %collective-permute-start.2 = (bf16[432,768]{1,0:T(8,128)(2,1)S(1)}, bf16[432,768]{1,0:T(8,128)(2,1)S(1)}, u32[]{:S(2)}, u32[]{:S(2)}) collective-permute-start(bf16[432,768]{1,0:T(8,128)(2,1)S(1)} %get-tuple-element.28.refs_0_), channel_id=1, source_target_pairs={{0,1},{1,2},{2,3},{4,5},{5,6},{6,7},{8,9},{9,10},{10,11},{12,13},{... | collective-permute-start | bytes 1990664 | tf_op jit(solution)/shard_map/ppermute | solution.py:19
  69.9 1.1 copy-start
  71.0 1.1 copy-start.1
  72.1 31.2 %collective-permute-start.12 = (bf16[432,1536]{1,0:T(8,128)(2,1)}, bf16[432,1536]{1,0:T(8,128)(2,1)}, u32[]{:S(2)}, u32[]{:S(2)}) collective-permute-start(bf16[432,1536]{1,0:T(8,128)(2,1)} %get-tuple-element.42), channel_id=1, source_target_pairs={{1,0},{2,1},{3,2},{5,4},{6,5},{7,6},{9,8},{10,9},{11,10},{13,12},{... | collective-permute-start | bytes 3981320 | tf_op jit(solution)/shard_map/ppermute | solution.py:19
  76.4 31.9 %collective-permute-start.13 = (bf16[432,1536]{1,0:T(8,128)(2,1)}, bf16[432,1536]{1,0:T(8,128)(2,1)}, u32[]{:S(2)}, u32[]{:S(2)}) collective-permute-start(bf16[432,1536]{1,0:T(8,128)(2,1)} %get-tuple-element.43), channel_id=1, source_target_pairs={{0,1},{1,2},{2,3},{4,5},{5,6},{6,7},{8,9},{9,10},{10,11},{12,13},{... | collective-permute-start | bytes 3981320 | tf_op jit(solution)/shard_map/ppermute | solution.py:19
  78.7 40.3 %all-to-all-start = ((f32[512,1,128]{2,1,0:T(1,128)}), f32[512,1,128]{2,1,0:T(1,128)S(1)}, u32[]{:S(2)}, u32[]{:S(2)}) async-start(f32[512,1,128]{2,1,0:T(1,128)} %broadcast_in_dim.16), calls=%async_computation | async-start | bytes 524288 | tf_op jit(solution)/shard_map/all_to_all | solution.py:25
  97.1 37.2 %collective-permute-start.16 = (bf16[432,1536]{1,0:T(8,128)(2,1)}, bf16[432,1536]{1,0:T(8,128)(2,1)}, u32[]{:S(2)}, u32[]{:S(2)}) collective-permute-start(bf16[432,1536]{1,0:T(8,128)(2,1)} %copy-done), channel_id=1, source_target_pairs={{4,0},{8,4},{12,8},{16,12},{20,16},{24,20},{28,24},{5,1},{9,5},{13... | collective-permute-start | bytes 3981320 | tf_op jit(solution)/shard_map/ppermute | solution.py:19
  99.0 36.2 %collective-permute-start.17 = (bf16[432,1536]{1,0:T(8,128)(2,1)}, bf16[432,1536]{1,0:T(8,128)(2,1)}, u32[]{:S(2)}, u32[]{:S(2)}) collective-permute-start(bf16[432,1536]{1,0:T(8,128)(2,1)} %copy-done.1), channel_id=1, source_target_pairs={{0,4},{4,8},{8,12},{12,16},{16,20},{20,24},{24,28},{1,5},{5,9},{9,... | collective-permute-start | bytes 3981320 | tf_op jit(solution)/shard_map/ppermute | solution.py:19
  112.1 31.3 %collective-permute-start.14 = (bf16[144,1536]{1,0:T(8,128)(2,1)S(1)}, bf16[144,1536]{1,0:T(8,128)(2,1)S(1)}, u32[]{:S(2)}, u32[]{:S(2)}) collective-permute-start(bf16[144,1536]{1,0:T(8,128)(2,1)S(1)} %get-tuple-element.54), channel_id=1, source_target_pairs={{4,0},{8,4},{12,8},{16,12},{20,16},{24,20},{28,24},{5,1},{9,5},{13... | collective-permute-start | bytes 1327112 | tf_op jit(solution)/shard_map/ppermute | solution.py:19
  114.0 30.2 %collective-permute-start.15 = (bf16[144,1536]{1,0:T(8,128)(2,1)S(1)}, bf16[144,1536]{1,0:T(8,128)(2,1)}, u32[]{:S(2)}, u32[]{:S(2)}) collective-permute-start(bf16[144,1536]{1,0:T(8,128)(2,1)S(1)} %get-tuple-element.55), channel_id=1, source_target_pairs={{0,4},{4,8},{8,12},{12,16},{16,20},{20,24},{24,28},{1,5},{5,9},{9,... | collective-permute-start | bytes 1327112 | tf_op jit(solution)/shard_map/ppermute | solution.py:19
  137.9 12.1 %collective-permute-start.18 = (bf16[144,1536]{1,0:T(8,128)(2,1)S(1)}, bf16[144,1536]{1,0:T(8,128)(2,1)S(1)}, u32[]{:S(2)}, u32[]{:S(2)}) collective-permute-start(bf16[144,1536]{1,0:T(8,128)(2,1)S(1)} %get-tuple-element.49), channel_id=1, source_target_pairs={{1,0},{2,1},{3,2},{5,4},{6,5},{7,6},{9,8},{10,9},{11,10},{13,12},{... | collective-permute-start | bytes 1327112 | tf_op jit(solution)/shard_map/ppermute | solution.py:19
  141.0 13.2 %collective-permute-start.19 = (bf16[144,1536]{1,0:T(8,128)(2,1)S(1)}, bf16[144,1536]{1,0:T(8,128)(2,1)S(1)}, u32[]{:S(2)}, u32[]{:S(2)}) collective-permute-start(bf16[144,1536]{1,0:T(8,128)(2,1)S(1)} %get-tuple-element.50), channel_id=1, source_target_pairs={{0,1},{1,2},{2,3},{4,5},{5,6},{6,7},{8,9},{9,10},{10,11},{12,13},{... | collective-permute-start | bytes 1327112 | tf_op jit(solution)/shard_map/ppermute | solution.py:19
where the time goes:
time: 156 us; the launch traced here: 155 us
  starting transfers between devices  72.8 us (47%)
  waiting for transfers between devices  48.2 us (31%)
  Pallas kernels  21.4 us (14%)
  other arithmetic  6.99 us (4%)
  local copies, waits for them, and re-layouts  4.66 us (3%)
    ppermute x20, starting transfers between devices, shifted(): return lax.ppermute(block, axis, pairs)  54.5 us
    ppermute x20, waiting for transfers between devices, shifted(): return lax.ppermute(block, axis, pairs)  48.2 us
    pallas_call x2, Pallas kernels, attention(): pl.pallas_call(functools.partial(attention_body, opening, tile_len, toget...  18.6 us
    all_to_all x1, starting transfers between devices, gathered_everywhere(): return lax.all_to_all(sent, ALL_AXES, 0, 0)  18.4 us
    another operation x1, other arithmetic  3.73 us
    unnamed x23, local copies, waits for them, and re-layouts  3.23 us
  transfers between devices with their start and end apart: 21, of which 12 were waited for; matrix products, arithmetic and copies ran while one was open for 5% of the time, Pallas kernels for 8%

commit v1 on v0

--- a/solution.py
+++ b/solution.py
@@ -9,24 +9,27 @@
 from jax.experimental.pallas import tpu as pltpu
 from jax.sharding import PartitionSpec as P
 
-ALL_AXES = ("dp", "tm", "height")
 HIDDEN = -1e30
 
 
-def shifted(block, axis, step):
+def exchanged(block, axis, turn):
     count = lax.axis_size(axis)
-    pairs = [(i, i + step) for i in range(count) if 0 <= i + step < count]
-    return lax.ppermute(block, axis, pairs)
-
-
-def gathered_everywhere(row):
-    count = math.prod(lax.axis_size(axis) for axis in ALL_AXES)
+    partner = [(i + turn) // 2 * 4 + 1 - 2 * turn - i for i in range(count)]
+    return lax.ppermute(block, axis, [(i, j) for i, j in enumerate(partner) if 0 <= j < count])
+
+
+def gathered(row, axes):
+    count = math.prod(lax.axis_size(axis) for axis in axes)
     sent = jnp.broadcast_to(row[None], (count,) + row.shape)
-    return lax.all_to_all(sent, ALL_AXES, 0, 0)
-
-
-def sum_body(rows_ref, own_ref, below_ref, above_ref, row_ref, own_sum_ref, *side_refs):
-    row_ref[...] = jnp.sum(rows_ref[...], axis=0)
+    return lax.all_to_all(sent, axes, 0, 0)
+
+
+def sum_body(with_rows, *refs):
+    if with_rows:
+        rows_ref, row_ref = refs[0], refs[4]
+        row_ref[...] = jnp.sum(rows_ref[...], axis=0)
+        refs = refs[1:4] + refs[5:]
+    own_ref, below_ref, above_ref, own_sum_ref, *side_refs = refs
     length = own_sum_ref.shape[0]
     for n in range(3):
         rows = slice(n * length, (n + 1) * length)
@@ -41,26 +44,59 @@
             side_refs[n - 1][...] = summed.astype(jnp.bfloat16)
 
 
-def summed_parts(rows, own, below, above):
-    tile = (own.shape[0] // 3, own.shape[1])
+def summed_parts(parts, rows=None):
+    tile = (parts[0].shape[0] // 3, parts[0].shape[1])
     vmem = pl.BlockSpec(memory_space=pltpu.VMEM)
+    given = (() if rows is None else (rows,)) + tuple(parts)
+    out_shape = [
+        jax.ShapeDtypeStruct(tile, jnp.float32),
+        jax.ShapeDtypeStruct(tile, jnp.bfloat16),
+        jax.ShapeDtypeStruct(tile, jnp.bfloat16),
+    ]
+    if rows is not None:
+        out_shape = [jax.ShapeDtypeStruct(rows.shape[1:], jnp.float32)] + out_shape
     return pl.pallas_call(
-        sum_body,
-        in_specs=[vmem] * 4,
-        out_specs=[vmem] * 4,
-        out_shape=[
-            jax.ShapeDtypeStruct(rows.shape[1:], jnp.float32),
-            jax.ShapeDtypeStruct(tile, jnp.float32),
-            jax.ShapeDtypeStruct(tile, jnp.bfloat16),
-            jax.ShapeDtypeStruct(tile, jnp.bfloat16),
-        ],
+        functools.partial(sum_body, rows is not None),
+        in_specs=[vmem] * len(given),
+        out_specs=[vmem] * len(out_shape),
+        out_shape=out_shape,
         compiler_params=pltpu.CompilerParams(vmem_limit_bytes=16 * 1024 * 1024),
-    )(rows, own, below, above)
-
-
-LINE = (0, -1, 1)
-KEY_TILES = [(a, b) for b in LINE for a in LINE]
-VALUE_SPOTS = [(LINE.index(a), LINE.index(b)) for a, b in KEY_TILES]
+    )(*given)
+
+
+def final_body(with_rows, *refs):
+    if with_rows:
+        rows_ref, row_ref = refs[0], refs[4]
+        row_ref[...] = jnp.sum(rows_ref[...], axis=0)
+        refs = refs[1:4] + refs[5:]
+    own_ref, below_ref, above_ref, out_ref = refs
+    out_ref[...] = (
+        own_ref[...] + below_ref[...].astype(jnp.float32) + above_ref[...].astype(jnp.float32)
+    ).astype(out_ref.dtype)
+
+
+def final_sum(parts, rows=None):
+    vmem = pl.BlockSpec(memory_space=pltpu.VMEM)
+    given = (() if rows is None else (rows,)) + tuple(parts)
+    out_shape = [jax.ShapeDtypeStruct(parts[0].shape, jnp.bfloat16)]
+    if rows is not None:
+        out_shape = [jax.ShapeDtypeStruct(rows.shape[1:], jnp.float32)] + out_shape
+    return pl.pallas_call(
+        functools.partial(final_body, rows is not None),
+        in_specs=[vmem] * len(given),
+        out_specs=[vmem] * len(out_shape),
+        out_shape=out_shape,
+        compiler_params=pltpu.CompilerParams(vmem_limit_bytes=8 * 1024 * 1024),
+    )(*given)
+
+
+KEY_SPOTS = [(a, b) for a in range(3) for b in range(3)]
+VALUE_SPOTS = [(b, a) for a, b in KEY_SPOTS]
+
+
+def line(place):
+    first = 1 - 2 * (place % 2)
+    return place, place + first, place - first
 
 
 def raw_scores(query, grad, keys, values, logits_ref, grad_weight_ref):
@@ -116,10 +152,12 @@
     @pl.when(pl.program_id(0) == 0)
     def _():
         limits = []
-        for dt, dh in KEY_TILES:
-            t, h = time_tile + dt, high_tile + dh
+        times, highs = line(time_tile), line(high_tile)
+        for a, b in KEY_SPOTS:
+            t, h = times[b], highs[a]
             inside = (t >= 0) & (t < time_count) & (h >= 0) & (h < high_count)
-            inside &= (jnp.abs(dt - time_shift) <= 1) & (jnp.abs(dh - high_shift) <= 1)
+            inside &= jnp.abs(t - time_tile - time_shift) <= 1
+            inside &= jnp.abs(h - high_tile - high_shift) <= 1
             count = counts_ref[jnp.clip(h, 0, high_count - 1), jnp.clip(t, 0, time_count - 1)]
             limits.append(jnp.where(inside, count, 0))
         place = lax.broadcasted_iota(jnp.int32, slot_row_ref.shape, 1)
@@ -135,9 +173,12 @@
 
     def operands(j):
         columns = slice(j * head_dim, (j + 1) * head_dim)
-        keys = jnp.concatenate([ref[:, columns] for ref in key_refs], axis=0)
+        place = (pl.program_id(0) * together + j) * head_dim
+        near = pl.ds(pl.multiple_of(place, head_dim), head_dim)
+        keys = jnp.concatenate([ref[:, near] for ref in key_refs], axis=0)
         values = jnp.concatenate(
-            [tile(value_refs[b], n)[:, columns] for b, n in VALUE_SPOTS], axis=0
+            [value_refs[b][n * tile_len : (n + 1) * tile_len, near] for b, n in VALUE_SPOTS],
+            axis=0,
         )
         return query_ref[:, columns], grad_ref[:, columns], keys, values
 
@@ -180,7 +221,6 @@
     smem = pl.BlockSpec(memory_space=pltpu.SMEM)
     whole = lambda array: pl.BlockSpec(array.shape, lambda h: (0, 0))
     side = pl.BlockSpec((tile_len, together * head_dim), lambda h: (0, first + h))
-    near = pl.BlockSpec((3 * tile_len, together * head_dim), lambda h: (0, h))
     out_near = pl.BlockSpec((3 * tile_len, together * head_dim), lambda h: (0, first + h))
     part = jax.ShapeDtypeStruct((3 * tile_len, branches * head_dim), jnp.bfloat16)
     pairs = heads * tile_len * 9 * tile_len
@@ -190,7 +230,7 @@
         grid=(heads // together,),
         in_specs=[smem] * 3
         + [whole(small[3]), whole(small[4]), side, side]
-        + [near] * 6
+        + [pl.BlockSpec(memory_space=pltpu.VMEM)] * 6
         + [pl.BlockSpec(memory_space=pl.ANY)] * len(so_far),
         out_specs=[side, pl.BlockSpec((together, 1, head_dim), lambda h: (first + h, 0, 0))]
         + [out_near] * 6,
@@ -211,7 +251,7 @@
             pltpu.VMEM(score, jnp.bfloat16),
         ]
         * together,
-        compiler_params=pltpu.CompilerParams(vmem_limit_bytes=16 * 1024 * 1024),
+        compiler_params=pltpu.CompilerParams(vmem_limit_bytes=24 * 1024 * 1024),
         cost_estimate=pl.CostEstimate(
             flops=10 * pairs * head_dim,
             bytes_accessed=12 * 3 * tile_len * heads * head_dim * 2,
@@ -255,8 +295,8 @@
     patch_neighborhood_offset,
     sharpness,
 ):
-    _, frames, rows, cols, width = probe_vectors.shape
-    tile_len = frames * rows * cols
+    _, frames, high, cols, width = probe_vectors.shape
+    tile_len = frames * high * cols
     branches = sharpness.shape[0]
     head_dim = width // branches
 
@@ -264,10 +304,10 @@
         return jnp.transpose(field[0], (0, 2, 1, 3)).reshape(tile_len, width)
 
     def as_field(tokens):
-        return jnp.transpose(tokens.reshape(frames, cols, rows, width), (0, 2, 1, 3))[None]
+        return jnp.transpose(tokens.reshape(frames, cols, high, width), (0, 2, 1, 3))[None]
 
     spot = np.arange(tile_len)
-    slot = (spot // (cols * rows) * rows + spot % rows) * cols + spot // rows % cols
+    slot = (spot // (cols * high) * high + spot % high) * cols + spot // high % cols
     slot_row = jnp.asarray(np.tile(slot, 9)[None, :], jnp.int32)
     slot_col = jnp.asarray(slot[:, None], jnp.int32)
     counts = patch_occupancy[0].T
@@ -278,14 +318,14 @@
         as_tokens(f) for f in (probe_vectors, lookup_vectors, payload_vectors, result_derivative)
     )
     chunks = ((0, 6), (6, 6))
-    key_blocks = packed(chunks, (key, shifted(key, "tm", 1), shifted(key, "tm", -1)))
+    key_blocks = packed(chunks, (key, exchanged(key, "tm", 0), exchanged(key, "tm", 1)))
     value_blocks = packed(
-        chunks, (value, shifted(value, "height", 1), shifted(value, "height", -1))
+        chunks, (value, exchanged(value, "height", 0), exchanged(value, "height", 1))
     )
     near = [
         (
-            (keys, shifted(keys, "height", 1), shifted(keys, "height", -1)),
-            (values, shifted(values, "tm", 1), shifted(values, "tm", -1)),
+            (keys, exchanged(keys, "height", 0), exchanged(keys, "height", 1)),
+            (values, exchanged(values, "tm", 0), exchanged(values, "tm", 1)),
         )
         for keys, values in zip(key_blocks, value_blocks)
     ]
@@ -296,31 +336,18 @@
         )
     query_grad, sharpness_grad = results[0], results[1]
 
-    def met(parts, second):
-        own, below, above = parts
-        return own, shifted(below, second, -1), shifted(above, second, 1)
-
-    def completed(own, below, above, first):
-        return (
-            own
-            + shifted(below, first, -1).astype(jnp.float32)
-            + shifted(above, first, 1).astype(jnp.float32)
-        ).astype(jnp.bfloat16)
+    def met(parts, axis):
+        return parts[0], exchanged(parts[1], axis, 0), exchanged(parts[2], axis, 1)
 
     key_parts = met(results[2:5], "height")
     value_parts = met(results[5:8], "tm")
-    row = jnp.sum(sharpness_grad, axis=(1, 2))
-    all_rows = gathered_everywhere(jnp.pad(row, (0, -branches % 128))[None])
-    summed = sum(part.astype(jnp.float32) for part in key_parts)
-    key_grad = completed(
-        summed[:tile_len],
-        summed[tile_len : 2 * tile_len].astype(jnp.bfloat16),
-        summed[2 * tile_len :].astype(jnp.bfloat16),
-        "tm",
-    )
-    row, *summed = summed_parts(all_rows, *value_parts)
-    value_grad = completed(*summed, "height")
-    return as_field(query_grad), as_field(key_grad), as_field(value_grad), row[0, :branches]
+    row = jnp.sum(sharpness_grad, axis=(1, 2))[None]
+    row, *summed = summed_parts(key_parts, gathered(row, ("dp",)))
+    (key_grad,) = final_sum(met(summed, "tm"))
+    row, *summed = summed_parts(value_parts, row[None])
+    rows = gathered(row, ("tm", "height"))
+    row, value_grad = final_sum(met(summed, "height"), rows)
+    return as_field(query_grad), as_field(key_grad), as_field(value_grad), row[0]
 
 
 def solution(mesh):

time: 156 us -> 145 us (0.929)
  the two profiles are of different devices: /device:TPU:124 before, /device:TPU:2 now
where the time goes in v1:
time: 145 us; the launch traced here: 144 us
  starting transfers between devices  75.2 us (52%)
  Pallas kernels  27.1 us (19%)
  blocking collectives  26.5 us (18%)
  waiting for transfers between devices  12.2 us (8%)
  local copies, waits for them, and re-layouts  1.67 us (1%)
    ppermute x20, starting transfers between devices, exchanged(): lax.ppermute(block, axis, [(i, j) for i, j in enumerate(partner) if 0 <=...  61.1 us
    all_to_all x1, blocking collectives, gathered(): return lax.all_to_all(sent, axes, 0, 0)  26.5 us
    pallas_call x2, Pallas kernels, attention(): pl.pallas_call(functools.partial(attention_body, opening, tile_len, toget...  18.3 us
    all_to_all x1, starting transfers between devices, gathered(): return lax.all_to_all(sent, axes, 0, 0)  14.1 us
    all_to_all x1, waiting for transfers between devices, gathered(): return lax.all_to_all(sent, axes, 0, 0)  8.06 us
    pallas_call x2, Pallas kernels, summed_parts(): pl.pallas_call(functools.partial(sum_body, rows is not None), in_specs=[v...  5.62 us
    ppermute x20, waiting for transfers between devices, exchanged(): lax.ppermute(block, axis, [(i, j) for i, j in enumerate(partner) if 0 <=...  4.18 us
    pallas_call x2, Pallas kernels, final_sum(): pl.pallas_call(functools.partial(final_body, rows is not None), in_specs=...  2.95 us
  transfers between devices with their start and end apart: 21, of which 3 were waited for; matrix products, arithmetic and copies ran while one was open for 1% of the time, Pallas kernels for 12%

profile of v1, /device:TPU:2, one launch (start us, length us, event | category | flops | bytes accessed | tf_op | source)
XLA Modules:
  0.0 143.8 jit_solution(6165029858247088543)
XLA Ops:
  0.6 0.7 collective-permute-start.5
  1.3 6.3 %collective-permute-start.4 = (bf16[144,1536]{1,0:T(8,128)(2,1)}, bf16[144,1536]{1,0:T(8,128)(2,1)S(1)}, u32[]{:S(2)}, u32[]{:S(2)}) collective-permute-start(bf16[144,1536]{1,0:T(8,128)(2,1)} %bitcast.48), channel_id=1, source_target_pairs={{0,1},{1,0},{2,3},{3,2},{4,5},{5,4},{6,7},{7,6},{8,9},{9,8},{10,11... | collective-permute-start | bytes 1327112 | tf_op jit(solution)/shard_map/ppermute | solution.py:18
  7.6 0.0 copy-start.7
  7.6 0.7 collective-permute-start.1
  8.3 7.9 %collective-permute-start = (bf16[144,1536]{1,0:T(8,128)(2,1)}, bf16[144,1536]{1,0:T(8,128)(2,1)S(1)}, u32[]{:S(2)}, u32[]{:S(2)}) collective-permute-start(bf16[144,1536]{1,0:T(8,128)(2,1)} %bitcast.51), channel_id=1, source_target_pairs={{0,4},{4,0},{8,12},{12,8},{16,20},{20,16},{24,28},{28,24},{1,5},{5... | collective-permute-start | bytes 1327112 | tf_op jit(solution)/shard_map/ppermute | solution.py:18
  16.2 0.0 collective-permute-done.5.refs_2_
  16.2 1.5 %collective-permute-done.4.refs_1_ = bf16[144,1536]{1,0:T(8,128)(2,1)S(1)} collective-permute-done((bf16[144,1536]{1,0:T(8,128)(2,1)}, bf16[144,1536]{1,0:T(8,128)(2,1)S(1)}, u32[]{:S(2)}, u32[]{:S(2)}) %collective-permute-start.4) | collective-permute-done | bytes 442400 | tf_op jit(solution)/shard_map/ppermute | solution.py:18
  17.7 1.0 copy-done
  18.7 0.0 copy-start.4
  18.7 0.0 copy-start.5
  18.8 0.0 copy-start.6
  18.8 0.1 shard_map.121
  18.9 0.8 collective-permute-start.11
  19.7 7.9 %collective-permute-start.10 = (bf16[432,768]{1,0:T(8,128)(2,1)S(1)}, bf16[432,768]{1,0:T(8,128)(2,1)S(1)}, u32[]{:S(2)}, u32[]{:S(2)}) collective-permute-start(bf16[432,768]{1,0:T(8,128)(2,1)S(1)} %get-tuple-element.37.refs_3_), channel_id=1, source_target_pairs={{0,4},{4,0},{8,12},{12,8},{16,20},{20,16},{24,28},{28,24},{1,5},{5... | collective-permute-start | bytes 1990664 | tf_op jit(solution)/shard_map/ppermute | solution.py:18
  27.6 0.0 collective-permute-done.1.refs_2_
  27.6 0.0 collective-permute-done.refs_1_
  27.6 0.0 copy-done.1
  27.6 0.1 shard_map.120
  27.7 0.7 collective-permute-start.9
  28.4 5.3 %collective-permute-start.8 = (bf16[432,768]{1,0:T(8,128)(2,1)S(1)}, bf16[432,768]{1,0:T(8,128)(2,1)S(1)}, u32[]{:S(2)}, u32[]{:S(2)}) collective-permute-start(bf16[432,768]{1,0:T(8,128)(2,1)S(1)} %get-tuple-element.36.refs_0_), channel_id=1, source_target_pairs={{0,1},{1,0},{2,3},{3,2},{4,5},{5,4},{6,7},{7,6},{8,9},{9,8},{10,11... | collective-permute-start | bytes 1990664 | tf_op jit(solution)/shard_map/ppermute | solution.py:18
  33.7 0.7 collective-permute-start.7
  34.4 0.0 collective-permute-done.11.refs_5_
  34.4 9.1 %collective-permute-start.6 = (bf16[432,768]{1,0:T(8,128)(2,1)S(1)}, bf16[432,768]{1,0:T(8,128)(2,1)S(1)}, u32[]{:S(2)}, u32[]{:S(2)}) collective-permute-start(bf16[432,768]{1,0:T(8,128)(2,1)S(1)} %get-tuple-element.35.refs_3_), channel_id=1, source_target_pairs={{0,4},{4,0},{8,12},{12,8},{16,20},{20,16},{24,28},{28,24},{1,5},{5... | collective-permute-start | bytes 1990664 | tf_op jit(solution)/shard_map/ppermute | solution.py:18
  43.5 0.0 collective-permute-done.10.refs_4_
  43.5 0.7 collective-permute-start.3
  44.2 0.0 collective-permute-done.9.refs_2_
  44.2 4.8 %collective-permute-start.2 = (bf16[432,768]{1,0:T(8,128)(2,1)S(1)}, bf16[432,768]{1,0:T(8,128)(2,1)S(1)}, u32[]{:S(2)}, u32[]{:S(2)}) collective-permute-start(bf16[432,768]{1,0:T(8,128)(2,1)S(1)} %get-tuple-element.34.refs_0_), channel_id=1, source_target_pairs={{0,1},{1,0},{2,3},{3,2},{4,5},{5,4},{6,7},{7,6},{8,9},{9,8},{10,11... | collective-permute-start | bytes 1990664 | tf_op jit(solution)/shard_map/ppermute | solution.py:18
  49.0 0.0 copy-done.8
  49.0 0.0 collective-permute-done.8.refs_1_
  49.1 0.0 copy-done.7
  49.1 0.0 copy-done.2
  49.1 0.0 copy-done.3
  49.1 0.0 copy-done.4
  49.1 9.2 %shard_map.122 = (bf16[144,1536]{1,0:T(8,128)(2,1)}, f32[12,1,128]{2,1,0:T(1,128)S(1)}, bf16[432,1536]{1,0:T(8,128)(2,1)S(1)}, bf16[432,1536]{1,0:T(8,128)(2,1)}...) custom-call(f32[12]{0:T(128)S(1)} %copy-done.7, ...), custom_call_target="tpu_custom_call" | custom-call | flops 1433272320 | bytes 7962624 | tf_op jit(solution)/shard_map/pallas_call | solution.py:228
  58.3 0.0 collective-permute-done.7.refs_5_
  58.3 0.0 collective-permute-done.6.refs_4_
  58.3 0.0 collective-permute-done.3.refs_2_
  58.3 2.6 %collective-permute-done.2.refs_1_ = bf16[432,768]{1,0:T(8,128)(2,1)S(1)} collective-permute-done((bf16[432,768]{1,0:T(8,128)(2,1)S(1)}, bf16[432,768]{1,0:T(8,128)(2,1)S(1)}, u32[]{:S(2)}, u32[]{:S(2)}) %collective-permute-start.2) | collective-permute-done | bytes 663584 | tf_op jit(solution)/shard_map/ppermute | solution.py:18
  61.0 9.1 %shard_map.123 = (bf16[144,1536]{1,0:T(8,128)(2,1)}, f32[12,1,128]{2,1,0:T(1,128)S(1)}, bf16[432,1536]{1,0:T(8,128)(2,1)S(1)}, bf16[432,1536]{1,0:T(8,128)(2,1)}...) custom-call(f32[12]{0:T(128)S(1)} %copy-done.7, ...), custom_call_target="tpu_custom_call", output_to_operand_aliasing={{0}: (13, {}), {1}: (14, {}), {2}: (15, {}), {3}: (16, {}),... | custom-call | flops 1433272320 | bytes 7962624 | tf_op jit(solution)/shard_map/pallas_call | solution.py:228
  70.1 3.6 %collective-permute-start.12 = (bf16[432,1536]{1,0:T(8,128)(2,1)}, bf16[432,1536]{1,0:T(8,128)(2,1)}, u32[]{:S(2)}, u32[]{:S(2)}) collective-permute-start(bf16[432,1536]{1,0:T(8,128)(2,1)} %get-tuple-element.49), channel_id=1, source_target_pairs={{0,1},{1,0},{2,3},{3,2},{4,5},{5,4},{6,7},{7,6},{8,9},{9,8},{10,11... | collective-permute-start | bytes 3981320 | tf_op jit(solution)/shard_map/ppermute | solution.py:18
  73.7 1.7 %collective-permute-start.13 = (bf16[432,1536]{1,0:T(8,128)(2,1)}, bf16[432,1536]{1,0:T(8,128)(2,1)}, u32[]{:S(2)}, u32[]{:S(2)}) collective-permute-start(bf16[432,1536]{1,0:T(8,128)(2,1)} %get-tuple-element.50), channel_id=1, source_target_pairs={{1,2},{2,1},{5,6},{6,5},{9,10},{10,9},{13,14},{14,13},{17,18},{18,... | collective-permute-start | bytes 3981320 | tf_op jit(solution)/shard_map/ppermute | solution.py:18
  75.5 2.2 %collective-permute-start.16 = (bf16[432,1536]{1,0:T(8,128)(2,1)}, bf16[432,1536]{1,0:T(8,128)(2,1)}, u32[]{:S(2)}, u32[]{:S(2)}) collective-permute-start(bf16[432,1536]{1,0:T(8,128)(2,1)} %get-tuple-element.56), channel_id=1, source_target_pairs={{0,4},{4,0},{8,12},{12,8},{16,20},{20,16},{24,28},{28,24},{1,5},{5... | collective-permute-start | bytes 3981320 | tf_op jit(solution)/shard_map/ppermute | solution.py:18
  77.7 1.7 %collective-permute-start.17 = (bf16[432,1536]{1,0:T(8,128)(2,1)}, bf16[432,1536]{1,0:T(8,128)(2,1)}, u32[]{:S(2)}, u32[]{:S(2)}) collective-permute-start(bf16[432,1536]{1,0:T(8,128)(2,1)} %get-tuple-element.57), channel_id=1, source_target_pairs={{4,8},{8,4},{12,16},{16,12},{20,24},{24,20},{5,9},{9,5},{13,17},{1... | collective-permute-start | bytes 3981320 | tf_op jit(solution)/shard_map/ppermute | solution.py:18
  79.4 0.2 reduce_sum.9
  79.6 26.5 %all_to_all.10.refs_0_ = f32[16,1,12]{2,1,0:T(1,128)S(1)} all-to-all(f32[16,1,12]{2,1,0:T(1,128)S(1)} %broadcast_in_dim.26), channel_id=1, replica_groups=mesh['dp'=16,'tm'=8,'height'=4] {'dp'}, dimensions={0} | all-to-all | bytes 1536 | tf_op jit(solution)/shard_map/all_to_all | solution.py:24
  106.1 0.0 collective-permute-done.12.refs_2_
  106.1 0.0 collective-permute-done.13.refs_3_
  106.1 2.8 %shard_map.124 = (f32[1,12]{1,0:T(1,128)S(1)}, f32[144,1536]{1,0:T(8,128)S(1)}, bf16[144,1536]{1,0:T(8,128)(2,1)}, bf16[144,1536]{1,0:T(8,128)(2,1)}) custom-call(f32[16,1,12]{2,1,0:T(1,128)S(1)} %all_to_all.10.refs_0_, bf16[432,1536]{1,0:T(8,128)(2,1)S(1)} %get-tuple-element.48.refs_1_, bf16[432,1536]{1,0:T(8,128)(2,1)} %collective-permute-done.12.refs_2_, ...), custom_call_target="tpu_custom_call" | custom-call | tf_op jit(solution)/shard_map/pallas_call | solution.py:58
  108.9 1.9 %collective-permute-start.14 = (bf16[144,1536]{1,0:T(8,128)(2,1)}, bf16[144,1536]{1,0:T(8,128)(2,1)}, u32[]{:S(2)}, u32[]{:S(2)}) collective-permute-start(bf16[144,1536]{1,0:T(8,128)(2,1)} %get-tuple-element.52), channel_id=1, source_target_pairs={{0,4},{4,0},{8,12},{12,8},{16,20},{20,16},{24,28},{28,24},{1,5},{5... | collective-permute-start | bytes 1327112 | tf_op jit(solution)/shard_map/ppermute | solution.py:18
  110.9 1.4 %collective-permute-start.15 = (bf16[144,1536]{1,0:T(8,128)(2,1)}, bf16[144,1536]{1,0:T(8,128)(2,1)}, u32[]{:S(2)}, u32[]{:S(2)}) collective-permute-start(bf16[144,1536]{1,0:T(8,128)(2,1)} %get-tuple-element.53), channel_id=1, source_target_pairs={{4,8},{8,4},{12,16},{16,12},{20,24},{24,20},{5,9},{9,5},{13,17},{1... | collective-permute-start | bytes 1327112 | tf_op jit(solution)/shard_map/ppermute | solution.py:18
  112.3 0.0 collective-permute-done.16.refs_2_
  112.3 0.0 collective-permute-done.17.refs_3_
  112.3 2.8 %shard_map.126 = (f32[1,12]{1,0:T(1,128)S(1)}, f32[144,1536]{1,0:T(8,128)S(1)}, bf16[144,1536]{1,0:T(8,128)(2,1)}, bf16[144,1536]{1,0:T(8,128)(2,1)}) custom-call(f32[1,1,12]{2,1,0:T(1,128)S(1)} %bitcast.61, bf16[432,1536]{1,0:T(8,128)(2,1)S(1)} %get-tuple-element.55.refs_1_, bf16[432,1536]{1,0:T(8,128)(2,1)} %collective-permute-done.16.refs_2_, ...), custom_call_target="tpu_custom_call" | custom-call | tf_op jit(solution)/shard_map/pallas_call | solution.py:58
  115.1 2.3 %collective-permute-start.18 = (bf16[144,1536]{1,0:T(8,128)(2,1)}, bf16[144,1536]{1,0:T(8,128)(2,1)S(1)}, u32[]{:S(2)}, u32[]{:S(2)}) collective-permute-start(bf16[144,1536]{1,0:T(8,128)(2,1)} %get-tuple-element.60), channel_id=1, source_target_pairs={{0,1},{1,0},{2,3},{3,2},{4,5},{5,4},{6,7},{7,6},{8,9},{9,8},{10,11... | collective-permute-start | bytes 1327112 | tf_op jit(solution)/shard_map/ppermute | solution.py:18
  117.4 0.7 collective-permute-start.19
  118.1 0.6 broadcast_in_dim.30
  118.7 14.1 %all-to-all-start.1 = ((f32[32,1,12]{2,1,0:T(1,128)}), f32[32,1,12]{2,1,0:T(1,128)S(1)}, u32[]{:S(2)}, u32[]{:S(2)}) async-start(f32[32,1,12]{2,1,0:T(1,128)} %broadcast_in_dim.30), calls=%async_computation.1 | async-start | bytes 32768 | tf_op jit(solution)/shard_map/all_to_all | solution.py:24
  132.8 0.0 collective-permute-done.14.refs_1_
  132.8 0.0 collective-permute-done.15.refs_2_
  132.8 2.0 %shard_map.125 = bf16[144,1536]{1,0:T(8,128)(2,1)} custom-call(f32[144,1536]{1,0:T(8,128)S(1)} %get-tuple-element.51.refs_0_, bf16[144,1536]{1,0:T(8,128)(2,1)} %collective-permute-done.14.refs_1_, bf16[144,1536]{1,0:T(8,128)(2,1)} %collective-permute-done.15.refs_2_), custom_call_target="tpu_custom_call" | custom-call | tf_op jit(solution)/shard_map/pallas_call | solution.py:84
  134.9 8.1 %all-to-all-done.1.refs_0_ = f32[32,1,12]{2,1,0:T(1,128)S(1)} async-done(((f32[32,1,12]{2,1,0:T(1,128)}), f32[32,1,12]{2,1,0:T(1,128)S(1)}, u32[]{:S(2)}, u32[]{:S(2)}) %all-to-all-start.1) | async-done | bytes 1568 | tf_op jit(solution)/shard_map/all_to_all | solution.py:24
  142.9 0.0 collective-permute-done.18.refs_2_
  142.9 0.0 collective-permute-done.19.refs_3_
  142.9 0.9 shard_map.127
  (10 shorter events, 0.0 us)
Async XLA Ops:
  0.6 15.6 %collective-permute-start.5 = (bf16[144,1536]{1,0:T(8,128)(2,1)}, bf16[144,1536]{1,0:T(8,128)(2,1)S(1)}, u32[]{:S(2)}, u32[]{:S(2)}) collective-permute-start(bf16[144,1536]{1,0:T(8,128)(2,1)} %bitcast.47), channel_id=1, source_target_pairs={{1,2},{2,1},{5,6},{6,5},{9,10},{10,9},{13,14},{14,13},{17,18},{18,... | collective-permute-start | bytes 1327112 | tf_op jit(solution)/shard_map/ppermute | solution.py:18
  1.3 16.4 %collective-permute-start.4 = (bf16[144,1536]{1,0:T(8,128)(2,1)}, bf16[144,1536]{1,0:T(8,128)(2,1)S(1)}, u32[]{:S(2)}, u32[]{:S(2)}) collective-permute-start(bf16[144,1536]{1,0:T(8,128)(2,1)} %bitcast.48), channel_id=1, source_target_pairs={{0,1},{1,0},{2,3},{3,2},{4,5},{5,4},{6,7},{7,6},{8,9},{9,8},{10,11... | collective-permute-start | bytes 1327112 | tf_op jit(solution)/shard_map/ppermute | solution.py:18
  7.6 41.4 %copy-start.7 = (f32[12]{0:T(128)S(1)}, f32[12]{0:T(128)}, u32[]{:S(2)}) copy-start(f32[12]{0:T(128)} %sharpness_ref.3) | copy-start | bytes 148
  7.6 19.9 %collective-permute-start.1 = (bf16[144,1536]{1,0:T(8,128)(2,1)}, bf16[144,1536]{1,0:T(8,128)(2,1)S(1)}, u32[]{:S(2)}, u32[]{:S(2)}) collective-permute-start(bf16[144,1536]{1,0:T(8,128)(2,1)} %bitcast.50), channel_id=1, source_target_pairs={{4,8},{8,4},{12,16},{16,12},{20,24},{24,20},{5,9},{9,5},{13,17},{1... | collective-permute-start | bytes 1327112 | tf_op jit(solution)/shard_map/ppermute | solution.py:18
  8.3 19.3 %collective-permute-start = (bf16[144,1536]{1,0:T(8,128)(2,1)}, bf16[144,1536]{1,0:T(8,128)(2,1)S(1)}, u32[]{:S(2)}, u32[]{:S(2)}) collective-permute-start(bf16[144,1536]{1,0:T(8,128)(2,1)} %bitcast.51), channel_id=1, source_target_pairs={{0,4},{4,0},{8,12},{12,8},{16,20},{20,16},{24,28},{28,24},{1,5},{5... | collective-permute-start | bytes 1327112 | tf_op jit(solution)/shard_map/ppermute | solution.py:18
  17.7 1.0 copy-start
  18.7 8.9 %copy-start.1 = (bf16[1,6,8,3,1536]{4,2,3,1,0:T(8,128)(2,1)S(1)}, bf16[1,6,8,3,1536]{4,2,3,1,0:T(8,128)(2,1)}, u32[]{:S(2)}) copy-start(bf16[1,6,8,3,1536]{4,2,3,1,0:T(8,128)(2,1)} %param.10) | copy-start | bytes 1327108
  18.7 30.3 %copy-start.8 = (s32[1,8,4,2]{1,3,2,0:T(2,128)S(1)}, s32[1,8,4,2]{1,3,2,0:T(2,128)}, u32[]{:S(2)}) copy-start(s32[1,8,4,2]{1,3,2,0:T(2,128)} %param.14) | copy-start | bytes 772
  18.7 30.3 %copy-start.2 = (bf16[1,6,8,3,1536]{4,2,3,1,0:T(8,128)(2,1)S(1)}, bf16[1,6,8,3,1536]{4,2,3,1,0:T(8,128)(2,1)}, u32[]{:S(2)}) copy-start(bf16[1,6,8,3,1536]{4,2,3,1,0:T(8,128)(2,1)} %param.9) | copy-start | bytes 1327108
  18.7 30.4 %copy-start.3 = (bf16[1,6,8,3,1536]{4,2,3,1,0:T(8,128)(2,1)S(1)}, bf16[1,6,8,3,1536]{4,2,3,1,0:T(8,128)(2,1)}, u32[]{:S(2)}) copy-start(bf16[1,6,8,3,1536]{4,2,3,1,0:T(8,128)(2,1)} %param.12) | copy-start | bytes 1327108
  18.7 30.4 %copy-start.4 = (s32[144,1]{1,0:T(8,128)S(1)}, s32[144,1]{1,0:T(8,128)}, u32[]{:S(2)}) copy-start(s32[144,1]{1,0:T(8,128)} %constant.7.clone.slot_col_ref) | copy-start | bytes 1732
  18.7 30.4 %copy-start.5 = (s32[1,1296]{1,0:T(1,128)S(1)}, s32[1,1296]{1,0:T(1,128)}, u32[]{:S(2)}) copy-start(s32[1,1296]{1,0:T(1,128)} %constant.6.clone.slot_row_ref) | copy-start | bytes 15556
  18.8 30.4 %copy-start.6 = (s32[1,8,4]{1,2,0:T(4,128)S(1)}, s32[1,8,4]{1,2,0:T(4,128)}, u32[]{:S(2)}) copy-start(s32[1,8,4]{1,2,0:T(4,128)} %param.13) | copy-start | bytes 388
  18.9 15.6 %collective-permute-start.11 = (bf16[432,768]{1,0:T(8,128)(2,1)S(1)}, bf16[432,768]{1,0:T(8,128)(2,1)S(1)}, u32[]{:S(2)}, u32[]{:S(2)}) collective-permute-start(bf16[432,768]{1,0:T(8,128)(2,1)S(1)} %get-tuple-element.37.refs_3_), channel_id=1, source_target_pairs={{4,8},{8,4},{12,16},{16,12},{20,24},{24,20},{5,9},{9,5},{13,17},{1... | collective-permute-start | bytes 1990664 | tf_op jit(solution)/shard_map/ppermute | solution.py:18
  19.7 23.8 %collective-permute-start.10 = (bf16[432,768]{1,0:T(8,128)(2,1)S(1)}, bf16[432,768]{1,0:T(8,128)(2,1)S(1)}, u32[]{:S(2)}, u32[]{:S(2)}) collective-permute-start(bf16[432,768]{1,0:T(8,128)(2,1)S(1)} %get-tuple-element.37.refs_3_), channel_id=1, source_target_pairs={{0,4},{4,0},{8,12},{12,8},{16,20},{20,16},{24,28},{28,24},{1,5},{5... | collective-permute-start | bytes 1990664 | tf_op jit(solution)/shard_map/ppermute | solution.py:18
  27.7 16.5 %collective-permute-start.9 = (bf16[432,768]{1,0:T(8,128)(2,1)S(1)}, bf16[432,768]{1,0:T(8,128)(2,1)S(1)}, u32[]{:S(2)}, u32[]{:S(2)}) collective-permute-start(bf16[432,768]{1,0:T(8,128)(2,1)S(1)} %get-tuple-element.36.refs_0_), channel_id=1, source_target_pairs={{1,2},{2,1},{5,6},{6,5},{9,10},{10,9},{13,14},{14,13},{17,18},{18,... | collective-permute-start | bytes 1990664 | tf_op jit(solution)/shard_map/ppermute | solution.py:18
  28.4 20.6 %collective-permute-start.8 = (bf16[432,768]{1,0:T(8,128)(2,1)S(1)}, bf16[432,768]{1,0:T(8,128)(2,1)S(1)}, u32[]{:S(2)}, u32[]{:S(2)}) collective-permute-start(bf16[432,768]{1,0:T(8,128)(2,1)S(1)} %get-tuple-element.36.refs_0_), channel_id=1, source_target_pairs={{0,1},{1,0},{2,3},{3,2},{4,5},{5,4},{6,7},{7,6},{8,9},{9,8},{10,11... | collective-permute-start | bytes 1990664 | tf_op jit(solution)/shard_map/ppermute | solution.py:18
  33.7 24.6 %collective-permute-start.7 = (bf16[432,768]{1,0:T(8,128)(2,1)S(1)}, bf16[432,768]{1,0:T(8,128)(2,1)S(1)}, u32[]{:S(2)}, u32[]{:S(2)}) collective-permute-start(bf16[432,768]{1,0:T(8,128)(2,1)S(1)} %get-tuple-element.35.refs_3_), channel_id=1, source_target_pairs={{4,8},{8,4},{12,16},{16,12},{20,24},{24,20},{5,9},{9,5},{13,17},{1... | collective-permute-start | bytes 1990664 | tf_op jit(solution)/shard_map/ppermute | solution.py:18
  34.4 23.9 %collective-permute-start.6 = (bf16[432,768]{1,0:T(8,128)(2,1)S(1)}, bf16[432,768]{1,0:T(8,128)(2,1)S(1)}, u32[]{:S(2)}, u32[]{:S(2)}) collective-permute-start(bf16[432,768]{1,0:T(8,128)(2,1)S(1)} %get-tuple-element.35.refs_3_), channel_id=1, source_target_pairs={{0,4},{4,0},{8,12},{12,8},{16,20},{20,16},{24,28},{28,24},{1,5},{5... | collective-permute-start | bytes 1990664 | tf_op jit(solution)/shard_map/ppermute | solution.py:18
  43.5 14.8 %collective-permute-start.3 = (bf16[432,768]{1,0:T(8,128)(2,1)S(1)}, bf16[432,768]{1,0:T(8,128)(2,1)S(1)}, u32[]{:S(2)}, u32[]{:S(2)}) collective-permute-start(bf16[432,768]{1,0:T(8,128)(2,1)S(1)} %get-tuple-element.34.refs_0_), channel_id=1, source_target_pairs={{1,2},{2,1},{5,6},{6,5},{9,10},{10,9},{13,14},{14,13},{17,18},{18,... | collective-permute-start | bytes 1990664 | tf_op jit(solution)/shard_map/ppermute | solution.py:18
  44.2 16.7 %collective-permute-start.2 = (bf16[432,768]{1,0:T(8,128)(2,1)S(1)}, bf16[432,768]{1,0:T(8,128)(2,1)S(1)}, u32[]{:S(2)}, u32[]{:S(2)}) collective-permute-start(bf16[432,768]{1,0:T(8,128)(2,1)S(1)} %get-tuple-element.34.refs_0_), channel_id=1, source_target_pairs={{0,1},{1,0},{2,3},{3,2},{4,5},{5,4},{6,7},{7,6},{8,9},{9,8},{10,11... | collective-permute-start | bytes 1990664 | tf_op jit(solution)/shard_map/ppermute | solution.py:18
  70.1 36.0 %collective-permute-start.12 = (bf16[432,1536]{1,0:T(8,128)(2,1)}, bf16[432,1536]{1,0:T(8,128)(2,1)}, u32[]{:S(2)}, u32[]{:S(2)}) collective-permute-start(bf16[432,1536]{1,0:T(8,128)(2,1)} %get-tuple-element.49), channel_id=1, source_target_pairs={{0,1},{1,0},{2,3},{3,2},{4,5},{5,4},{6,7},{7,6},{8,9},{9,8},{10,11... | collective-permute-start | bytes 3981320 | tf_op jit(solution)/shard_map/ppermute | solution.py:18
  73.7 32.4 %collective-permute-start.13 = (bf16[432,1536]{1,0:T(8,128)(2,1)}, bf16[432,1536]{1,0:T(8,128)(2,1)}, u32[]{:S(2)}, u32[]{:S(2)}) collective-permute-start(bf16[432,1536]{1,0:T(8,128)(2,1)} %get-tuple-element.50), channel_id=1, source_target_pairs={{1,2},{2,1},{5,6},{6,5},{9,10},{10,9},{13,14},{14,13},{17,18},{18,... | collective-permute-start | bytes 3981320 | tf_op jit(solution)/shard_map/ppermute | solution.py:18
  75.5 36.8 %collective-permute-start.16 = (bf16[432,1536]{1,0:T(8,128)(2,1)}, bf16[432,1536]{1,0:T(8,128)(2,1)}, u32[]{:S(2)}, u32[]{:S(2)}) collective-permute-start(bf16[432,1536]{1,0:T(8,128)(2,1)} %get-tuple-element.56), channel_id=1, source_target_pairs={{0,4},{4,0},{8,12},{12,8},{16,20},{20,16},{24,28},{28,24},{1,5},{5... | collective-permute-start | bytes 3981320 | tf_op jit(solution)/shard_map/ppermute | solution.py:18
  77.7 34.6 %collective-permute-start.17 = (bf16[432,1536]{1,0:T(8,128)(2,1)}, bf16[432,1536]{1,0:T(8,128)(2,1)}, u32[]{:S(2)}, u32[]{:S(2)}) collective-permute-start(bf16[432,1536]{1,0:T(8,128)(2,1)} %get-tuple-element.57), channel_id=1, source_target_pairs={{4,8},{8,4},{12,16},{16,12},{20,24},{24,20},{5,9},{9,5},{13,17},{1... | collective-permute-start | bytes 3981320 | tf_op jit(solution)/shard_map/ppermute | solution.py:18
  108.9 23.9 %collective-permute-start.14 = (bf16[144,1536]{1,0:T(8,128)(2,1)}, bf16[144,1536]{1,0:T(8,128)(2,1)}, u32[]{:S(2)}, u32[]{:S(2)}) collective-permute-start(bf16[144,1536]{1,0:T(8,128)(2,1)} %get-tuple-element.52), channel_id=1, source_target_pairs={{0,4},{4,0},{8,12},{12,8},{16,20},{20,16},{24,28},{28,24},{1,5},{5... | collective-permute-start | bytes 1327112 | tf_op jit(solution)/shard_map/ppermute | solution.py:18
  110.9 22.0 %collective-permute-start.15 = (bf16[144,1536]{1,0:T(8,128)(2,1)}, bf16[144,1536]{1,0:T(8,128)(2,1)}, u32[]{:S(2)}, u32[]{:S(2)}) collective-permute-start(bf16[144,1536]{1,0:T(8,128)(2,1)} %get-tuple-element.53), channel_id=1, source_target_pairs={{4,8},{8,4},{12,16},{16,12},{20,24},{24,20},{5,9},{9,5},{13,17},{1... | collective-permute-start | bytes 1327112 | tf_op jit(solution)/shard_map/ppermute | solution.py:18
  115.1 27.8 %collective-permute-start.18 = (bf16[144,1536]{1,0:T(8,128)(2,1)}, bf16[144,1536]{1,0:T(8,128)(2,1)S(1)}, u32[]{:S(2)}, u32[]{:S(2)}) collective-permute-start(bf16[144,1536]{1,0:T(8,128)(2,1)} %get-tuple-element.60), channel_id=1, source_target_pairs={{0,1},{1,0},{2,3},{3,2},{4,5},{5,4},{6,7},{7,6},{8,9},{9,8},{10,11... | collective-permute-start | bytes 1327112 | tf_op jit(solution)/shard_map/ppermute | solution.py:18
  117.4 25.5 %collective-permute-start.19 = (bf16[144,1536]{1,0:T(8,128)(2,1)}, bf16[144,1536]{1,0:T(8,128)(2,1)S(1)}, u32[]{:S(2)}, u32[]{:S(2)}) collective-permute-start(bf16[144,1536]{1,0:T(8,128)(2,1)} %get-tuple-element.61), channel_id=1, source_target_pairs={{1,2},{2,1},{5,6},{6,5},{9,10},{10,9},{13,14},{14,13},{17,18},{18,... | collective-permute-start | bytes 1327112 | tf_op jit(solution)/shard_map/ppermute | solution.py:18
  118.7 24.2 %all-to-all-start.1 = ((f32[32,1,12]{2,1,0:T(1,128)}), f32[32,1,12]{2,1,0:T(1,128)S(1)}, u32[]{:S(2)}, u32[]{:S(2)}) async-start(f32[32,1,12]{2,1,0:T(1,128)} %broadcast_in_dim.30), calls=%async_computation.1 | async-start | bytes 32768 | tf_op jit(solution)/shard_map/all_to_all | solution.py:24

commit v2 on v1

--- a/solution.py
+++ b/solution.py
@@ -18,16 +18,14 @@
     return lax.ppermute(block, axis, [(i, j) for i, j in enumerate(partner) if 0 <= j < count])
 
 
-def gathered(row, axes):
-    count = math.prod(lax.axis_size(axis) for axis in axes)
-    sent = jnp.broadcast_to(row[None], (count,) + row.shape)
-    return lax.all_to_all(sent, axes, 0, 0)
+def swapped(rows, axes):
+    return lax.all_to_all(rows, axes, 0, 0)
 
 
 def sum_body(with_rows, *refs):
     if with_rows:
         rows_ref, row_ref = refs[0], refs[4]
-        row_ref[...] = jnp.sum(rows_ref[...], axis=0)
+        row_ref[...] = jnp.broadcast_to(jnp.sum(rows_ref[...], axis=0)[None], row_ref.shape)
         refs = refs[1:4] + refs[5:]
     own_ref, below_ref, above_ref, own_sum_ref, *side_refs = refs
     length = own_sum_ref.shape[0]
@@ -44,7 +42,7 @@
             side_refs[n - 1][...] = summed.astype(jnp.bfloat16)
 
 
-def summed_parts(parts, rows=None):
+def summed_parts(parts, rows=None, copies=1):
     tile = (parts[0].shape[0] // 3, parts[0].shape[1])
     vmem = pl.BlockSpec(memory_space=pltpu.VMEM)
     given = (() if rows is None else (rows,)) + tuple(parts)
@@ -54,7 +52,7 @@
         jax.ShapeDtypeStruct(tile, jnp.bfloat16),
     ]
     if rows is not None:
-        out_shape = [jax.ShapeDtypeStruct(rows.shape[1:], jnp.float32)] + out_shape
+        out_shape = [jax.ShapeDtypeStruct((copies,) + rows.shape[1:], jnp.float32)] + out_shape
     return pl.pallas_call(
         functools.partial(sum_body, rows is not None),
         in_specs=[vmem] * len(given),
@@ -270,14 +268,26 @@
             out_ref[n * tile_len : (n + 1) * tile_len] = inputs[n][:, columns]
 
 
+def own_body(own_ref, out_ref):
+    out_ref[...] = own_ref[...]
+
+
 def packed(chunks, line):
     tile_len, width = line[0].shape
+    whole = pl.BlockSpec(memory_space=pltpu.VMEM)
+    own = pl.pallas_call(
+        own_body,
+        in_specs=[whole],
+        out_specs=whole,
+        out_shape=jax.ShapeDtypeStruct(line[0].shape, line[0].dtype),
+        compiler_params=pltpu.CompilerParams(vmem_limit_bytes=8 * 1024 * 1024),
+    )(line[0])
+    line = (own,) + line[1:]
     per_head = width // sum(heads for _, heads in chunks)
-    vmem = pl.BlockSpec(memory_space=pltpu.VMEM)
     return pl.pallas_call(
         functools.partial(pack_body, chunks),
-        in_specs=[vmem] * 3,
-        out_specs=[vmem] * len(chunks),
+        in_specs=[whole] * 3,
+        out_specs=[whole] * len(chunks),
         out_shape=[
             jax.ShapeDtypeStruct((3 * tile_len, heads * per_head), jnp.bfloat16)
             for _, heads in chunks
@@ -341,11 +351,13 @@
 
     key_parts = met(results[2:5], "height")
     value_parts = met(results[5:8], "tm")
-    row = jnp.sum(sharpness_grad, axis=(1, 2))[None]
-    row, *summed = summed_parts(key_parts, gathered(row, ("dp",)))
+    wide, time_count = ("dp", "height"), lax.axis_size("tm")
+    row = jnp.sum(sharpness_grad, axis=(1, 2))
+    rows = jnp.broadcast_to(row, (math.prod(lax.axis_size(axis) for axis in wide), 1, branches))
+    row, *summed = summed_parts(key_parts, swapped(rows, wide))
     (key_grad,) = final_sum(met(summed, "tm"))
-    row, *summed = summed_parts(value_parts, row[None])
-    rows = gathered(row, ("tm", "height"))
+    rows, *summed = summed_parts(value_parts, row, time_count)
+    rows = swapped(rows, ("tm",))
     row, value_grad = final_sum(met(summed, "height"), rows)
     return as_field(query_grad), as_field(key_grad), as_field(value_grad), row[0]
 

time: 145 us -> 142 us (0.979)
  the two profiles are of different devices: /device:TPU:2 before, /device:TPU:8 now
where the time goes in v2:
time: 142 us; the launch traced here: 141 us
  starting transfers between devices  73.4 us (52%)
  Pallas kernels  27.1 us (19%)
  blocking collectives  25.7 us (18%)
  waiting for transfers between devices  11.4 us (8%)
  local copies, waits for them, and re-layouts  2.1 us (1%)
    ppermute x20, starting transfers between devices, exchanged(): lax.ppermute(block, axis, [(i, j) for i, j in enumerate(partner) if 0 <=...  64 us
    all_to_all x1, blocking collectives, swapped(): return lax.all_to_all(rows, axes, 0, 0)  25.7 us
    pallas_call x2, Pallas kernels, attention(): pl.pallas_call(functools.partial(attention_body, opening, tile_len, toget...  18.3 us
    all_to_all x1, starting transfers between devices, swapped(): return lax.all_to_all(rows, axes, 0, 0)  9.4 us
    ppermute x20, waiting for transfers between devices, exchanged(): lax.ppermute(block, axis, [(i, j) for i, j in enumerate(partner) if 0 <=...  5.82 us
    pallas_call x2, Pallas kernels, summed_parts(): pl.pallas_call(functools.partial(sum_body, rows is not None), in_specs=[v...  5.63 us
    all_to_all x1, waiting for transfers between devices, swapped(): return lax.all_to_all(rows, axes, 0, 0)  5.61 us
    pallas_call x2, Pallas kernels, final_sum(): pl.pallas_call(functools.partial(final_body, rows is not None), in_specs=...  2.94 us
  transfers between devices with their start and end apart: 21, of which 5 were waited for; matrix products, arithmetic and copies ran while one was open for 0% of the time, Pallas kernels for 12%

profile of v2, /device:TPU:8, one launch (start us, length us, event | category | flops | bytes accessed | tf_op | source)
XLA Modules:
  0.0 140.9 jit_solution(7842803098325557207)
XLA Ops:
  0.6 3.5 %collective-permute-start.5 = (bf16[144,1536]{1,0:T(8,128)(2,1)}, bf16[144,1536]{1,0:T(8,128)(2,1)S(1)}, u32[]{:S(2)}, u32[]{:S(2)}) collective-permute-start(bf16[144,1536]{1,0:T(8,128)(2,1)} %bitcast.45), channel_id=1, source_target_pairs={{1,2},{2,1},{5,6},{6,5},{9,10},{10,9},{13,14},{14,13},{17,18},{18,... | collective-permute-start | bytes 1327112 | tf_op jit(solution)/shard_map/ppermute | solution.py:18
  4.1 4.9 %collective-permute-start.4 = (bf16[144,1536]{1,0:T(8,128)(2,1)}, bf16[144,1536]{1,0:T(8,128)(2,1)S(1)}, u32[]{:S(2)}, u32[]{:S(2)}) collective-permute-start(bf16[144,1536]{1,0:T(8,128)(2,1)} %bitcast.46), channel_id=1, source_target_pairs={{0,1},{1,0},{2,3},{3,2},{4,5},{5,4},{6,7},{7,6},{8,9},{9,8},{10,11... | collective-permute-start | bytes 1327112 | tf_op jit(solution)/shard_map/ppermute | solution.py:18
  9.1 0.7 collective-permute-start.1
  9.8 4.9 %collective-permute-start = (bf16[144,1536]{1,0:T(8,128)(2,1)}, bf16[144,1536]{1,0:T(8,128)(2,1)S(1)}, u32[]{:S(2)}, u32[]{:S(2)}) collective-permute-start(bf16[144,1536]{1,0:T(8,128)(2,1)} %bitcast.49), channel_id=1, source_target_pairs={{0,4},{4,0},{8,12},{12,8},{16,20},{20,16},{24,28},{28,24},{1,5},{5... | collective-permute-start | bytes 1327112 | tf_op jit(solution)/shard_map/ppermute | solution.py:18
  14.6 0.0 copy-start.1
  14.6 1.0 copy-done.1
  15.7 0.0 copy-start
  15.7 1.0 copy-done
  16.7 0.0 copy-start.8
  16.8 0.0 copy-start.2
  16.8 0.0 copy-start.3
  16.8 0.0 copy-start.4
  16.8 0.0 copy-start.5
  16.8 0.0 copy-start.6
  16.8 0.0 copy-start.7
  16.8 0.0 collective-permute-done.5.refs_2_
  16.8 1.0 collective-permute-done.4.refs_1_
  17.9 0.1 shard_map.123
  17.9 0.7 collective-permute-start.11
  18.7 8.2 %collective-permute-start.10 = (bf16[432,768]{1,0:T(8,128)(2,1)S(1)}, bf16[432,768]{1,0:T(8,128)(2,1)S(1)}, u32[]{:S(2)}, u32[]{:S(2)}) collective-permute-start(bf16[432,768]{1,0:T(8,128)(2,1)S(1)} %get-tuple-element.37.refs_3_), channel_id=1, source_target_pairs={{0,4},{4,0},{8,12},{12,8},{16,20},{20,16},{24,28},{28,24},{1,5},{5... | collective-permute-start | bytes 1990664 | tf_op jit(solution)/shard_map/ppermute | solution.py:18
  26.9 0.0 collective-permute-done.1.refs_2_
  26.9 0.0 collective-permute-done.refs_1_
  26.9 0.1 shard_map.121
  27.0 2.4 %collective-permute-start.9 = (bf16[432,768]{1,0:T(8,128)(2,1)S(1)}, bf16[432,768]{1,0:T(8,128)(2,1)S(1)}, u32[]{:S(2)}, u32[]{:S(2)}) collective-permute-start(bf16[432,768]{1,0:T(8,128)(2,1)S(1)} %get-tuple-element.36.refs_0_), channel_id=1, source_target_pairs={{1,2},{2,1},{5,6},{6,5},{9,10},{10,9},{13,14},{14,13},{17,18},{18,... | collective-permute-start | bytes 1990664 | tf_op jit(solution)/shard_map/ppermute | solution.py:18
  29.3 2.3 %collective-permute-start.8 = (bf16[432,768]{1,0:T(8,128)(2,1)S(1)}, bf16[432,768]{1,0:T(8,128)(2,1)S(1)}, u32[]{:S(2)}, u32[]{:S(2)}) collective-permute-start(bf16[432,768]{1,0:T(8,128)(2,1)S(1)} %get-tuple-element.36.refs_0_), channel_id=1, source_target_pairs={{0,1},{1,0},{2,3},{3,2},{4,5},{5,4},{6,7},{7,6},{8,9},{9,8},{10,11... | collective-permute-start | bytes 1990664 | tf_op jit(solution)/shard_map/ppermute | solution.py:18
  31.6 0.7 collective-permute-start.7
  32.3 0.0 collective-permute-done.11.refs_5_
  32.3 10.0 %collective-permute-start.6 = (bf16[432,768]{1,0:T(8,128)(2,1)S(1)}, bf16[432,768]{1,0:T(8,128)(2,1)S(1)}, u32[]{:S(2)}, u32[]{:S(2)}) collective-permute-start(bf16[432,768]{1,0:T(8,128)(2,1)S(1)} %get-tuple-element.35.refs_3_), channel_id=1, source_target_pairs={{0,4},{4,0},{8,12},{12,8},{16,20},{20,16},{24,28},{28,24},{1,5},{5... | collective-permute-start | bytes 1990664 | tf_op jit(solution)/shard_map/ppermute | solution.py:18
  42.4 0.0 collective-permute-done.10.refs_4_
  42.4 1.9 %collective-permute-start.3 = (bf16[432,768]{1,0:T(8,128)(2,1)S(1)}, bf16[432,768]{1,0:T(8,128)(2,1)S(1)}, u32[]{:S(2)}, u32[]{:S(2)}) collective-permute-start(bf16[432,768]{1,0:T(8,128)(2,1)S(1)} %get-tuple-element.34.refs_0_), channel_id=1, source_target_pairs={{1,2},{2,1},{5,6},{6,5},{9,10},{10,9},{13,14},{14,13},{17,18},{18,... | collective-permute-start | bytes 1990664 | tf_op jit(solution)/shard_map/ppermute | solution.py:18
  44.3 0.4 collective-permute-done.9.refs_2_
  44.7 2.0 %collective-permute-start.2 = (bf16[432,768]{1,0:T(8,128)(2,1)S(1)}, bf16[432,768]{1,0:T(8,128)(2,1)S(1)}, u32[]{:S(2)}, u32[]{:S(2)}) collective-permute-start(bf16[432,768]{1,0:T(8,128)(2,1)S(1)} %get-tuple-element.34.refs_0_), channel_id=1, source_target_pairs={{0,1},{1,0},{2,3},{3,2},{4,5},{5,4},{6,7},{7,6},{8,9},{9,8},{10,11... | collective-permute-start | bytes 1990664 | tf_op jit(solution)/shard_map/ppermute | solution.py:18
  46.8 0.0 copy-done.8
  46.8 0.0 collective-permute-done.8.refs_1_
  46.9 9.2 %shard_map.124 = (bf16[144,1536]{1,0:T(8,128)(2,1)}, f32[12,1,128]{2,1,0:T(1,128)S(1)}, bf16[432,1536]{1,0:T(8,128)(2,1)S(1)}, bf16[432,1536]{1,0:T(8,128)(2,1)}...) custom-call(f32[12]{0:T(128)S(1)} %copy-done.7, ...), custom_call_target="tpu_custom_call" | custom-call | flops 1433272320 | bytes 7962624 | tf_op jit(solution)/shard_map/pallas_call | solution.py:226
  56.0 0.0 collective-permute-done.7.refs_5_
  56.0 0.0 collective-permute-done.6.refs_4_
  56.1 2.3 %collective-permute-done.3.refs_2_ = bf16[432,768]{1,0:T(8,128)(2,1)S(1)} collective-permute-done((bf16[432,768]{1,0:T(8,128)(2,1)S(1)}, bf16[432,768]{1,0:T(8,128)(2,1)S(1)}, u32[]{:S(2)}, u32[]{:S(2)}) %collective-permute-start.3) | collective-permute-done | bytes 663584 | tf_op jit(solution)/shard_map/ppermute | solution.py:18
  58.3 2.1 %collective-permute-done.2.refs_1_ = bf16[432,768]{1,0:T(8,128)(2,1)S(1)} collective-permute-done((bf16[432,768]{1,0:T(8,128)(2,1)S(1)}, bf16[432,768]{1,0:T(8,128)(2,1)S(1)}, u32[]{:S(2)}, u32[]{:S(2)}) %collective-permute-start.2) | collective-permute-done | bytes 663584 | tf_op jit(solution)/shard_map/ppermute | solution.py:18
  60.4 9.1 %shard_map.125 = (bf16[144,1536]{1,0:T(8,128)(2,1)}, f32[12,1,128]{2,1,0:T(1,128)S(1)}, bf16[432,1536]{1,0:T(8,128)(2,1)S(1)}, bf16[432,1536]{1,0:T(8,128)(2,1)}...) custom-call(f32[12]{0:T(128)S(1)} %copy-done.7, ...), custom_call_target="tpu_custom_call", output_to_operand_aliasing={{0}: (13, {}), {1}: (14, {}), {2}: (15, {}), {3}: (16, {}),... | custom-call | flops 1433272320 | bytes 7962624 | tf_op jit(solution)/shard_map/pallas_call | solution.py:226
  69.6 2.3 %collective-permute-start.12 = (bf16[432,1536]{1,0:T(8,128)(2,1)}, bf16[432,1536]{1,0:T(8,128)(2,1)}, u32[]{:S(2)}, u32[]{:S(2)}) collective-permute-start(bf16[432,1536]{1,0:T(8,128)(2,1)} %get-tuple-element.49), channel_id=1, source_target_pairs={{0,1},{1,0},{2,3},{3,2},{4,5},{5,4},{6,7},{7,6},{8,9},{9,8},{10,11... | collective-permute-start | bytes 3981320 | tf_op jit(solution)/shard_map/ppermute | solution.py:18
  71.8 3.4 %collective-permute-start.13 = (bf16[432,1536]{1,0:T(8,128)(2,1)}, bf16[432,1536]{1,0:T(8,128)(2,1)}, u32[]{:S(2)}, u32[]{:S(2)}) collective-permute-start(bf16[432,1536]{1,0:T(8,128)(2,1)} %get-tuple-element.50), channel_id=1, source_target_pairs={{1,2},{2,1},{5,6},{6,5},{9,10},{10,9},{13,14},{14,13},{17,18},{18,... | collective-permute-start | bytes 3981320 | tf_op jit(solution)/shard_map/ppermute | solution.py:18
  75.3 2.4 %collective-permute-start.16 = (bf16[432,1536]{1,0:T(8,128)(2,1)}, bf16[432,1536]{1,0:T(8,128)(2,1)}, u32[]{:S(2)}, u32[]{:S(2)}) collective-permute-start(bf16[432,1536]{1,0:T(8,128)(2,1)} %get-tuple-element.56), channel_id=1, source_target_pairs={{0,4},{4,0},{8,12},{12,8},{16,20},{20,16},{24,28},{28,24},{1,5},{5... | collective-permute-start | bytes 3981320 | tf_op jit(solution)/shard_map/ppermute | solution.py:18
  77.7 1.7 %collective-permute-start.17 = (bf16[432,1536]{1,0:T(8,128)(2,1)}, bf16[432,1536]{1,0:T(8,128)(2,1)}, u32[]{:S(2)}, u32[]{:S(2)}) collective-permute-start(bf16[432,1536]{1,0:T(8,128)(2,1)} %get-tuple-element.57), channel_id=1, source_target_pairs={{4,8},{8,4},{12,16},{16,12},{20,24},{24,20},{5,9},{9,5},{13,17},{1... | collective-permute-start | bytes 3981320 | tf_op jit(solution)/shard_map/ppermute | solution.py:18
  79.4 0.2 reduce_sum.9
  79.6 25.7 %all_to_all.10.refs_0_ = f32[64,1,12]{2,1,0:T(1,128)S(1)} all-to-all(f32[64,1,12]{2,1,0:T(1,128)S(1)} %broadcast_in_dim.13), channel_id=1, replica_groups=mesh['dp'=16,'tm'=8,'height'=4] {'dp','height'}, dimensions={0} | all-to-all | bytes 6144 | tf_op jit(solution)/shard_map/all_to_all | solution.py:22
  105.3 0.0 collective-permute-done.12.refs_2_
  105.3 0.0 collective-permute-done.13.refs_3_
  105.3 2.8 %shard_map.126 = (f32[1,1,12]{2,1,0:T(1,128)S(1)}, f32[144,1536]{1,0:T(8,128)S(1)}, bf16[144,1536]{1,0:T(8,128)(2,1)}, bf16[144,1536]{1,0:T(8,128)(2,1)}) custom-call(f32[64,1,12]{2,1,0:T(1,128)S(1)} %all_to_all.10.refs_0_, bf16[432,1536]{1,0:T(8,128)(2,1)S(1)} %get-tuple-element.48.refs_1_, bf16[432,1536]{1,0:T(8,128)(2,1)} %collective-permute-done.12.refs_2_, ...), custom_call_target="tpu_custom_call" | custom-call | tf_op jit(solution)/shard_map/pallas_call | solution.py:56
  108.2 2.3 %collective-permute-start.14 = (bf16[144,1536]{1,0:T(8,128)(2,1)}, bf16[144,1536]{1,0:T(8,128)(2,1)}, u32[]{:S(2)}, u32[]{:S(2)}) collective-permute-start(bf16[144,1536]{1,0:T(8,128)(2,1)} %get-tuple-element.52), channel_id=1, source_target_pairs={{0,4},{4,0},{8,12},{12,8},{16,20},{20,16},{24,28},{28,24},{1,5},{5... | collective-permute-start | bytes 1327112 | tf_op jit(solution)/shard_map/ppermute | solution.py:18
  110.4 1.4 %collective-permute-start.15 = (bf16[144,1536]{1,0:T(8,128)(2,1)}, bf16[144,1536]{1,0:T(8,128)(2,1)}, u32[]{:S(2)}, u32[]{:S(2)}) collective-permute-start(bf16[144,1536]{1,0:T(8,128)(2,1)} %get-tuple-element.53), channel_id=1, source_target_pairs={{4,8},{8,4},{12,16},{16,12},{20,24},{24,20},{5,9},{9,5},{13,17},{1... | collective-permute-start | bytes 1327112 | tf_op jit(solution)/shard_map/ppermute | solution.py:18
  111.9 0.0 collective-permute-done.16.refs_2_
  111.9 0.0 collective-permute-done.17.refs_3_
  111.9 2.8 %shard_map.128 = (f32[8,1,12]{2,1,0:T(1,128)}, f32[144,1536]{1,0:T(8,128)S(1)}, bf16[144,1536]{1,0:T(8,128)(2,1)}, bf16[144,1536]{1,0:T(8,128)(2,1)}) custom-call(f32[1,1,12]{2,1,0:T(1,128)S(1)} %get-tuple-element.54.refs_0_, bf16[432,1536]{1,0:T(8,128)(2,1)S(1)} %get-tuple-element.55.refs_1_, bf16[432,1536]{1,0:T(8,128)(2,1)} %collective-permute-done.16.refs_2_, ...), custom_call_target="tpu_custom_call" | custom-call | tf_op jit(solution)/shard_map/pallas_call | solution.py:56
  114.7 4.8 %collective-permute-start.18 = (bf16[144,1536]{1,0:T(8,128)(2,1)}, bf16[144,1536]{1,0:T(8,128)(2,1)S(1)}, u32[]{:S(2)}, u32[]{:S(2)}) collective-permute-start(bf16[144,1536]{1,0:T(8,128)(2,1)} %get-tuple-element.60), channel_id=1, source_target_pairs={{0,1},{1,0},{2,3},{3,2},{4,5},{5,4},{6,7},{7,6},{8,9},{9,8},{10,11... | collective-permute-start | bytes 1327112 | tf_op jit(solution)/shard_map/ppermute | solution.py:18
  119.5 3.4 %collective-permute-start.19 = (bf16[144,1536]{1,0:T(8,128)(2,1)}, bf16[144,1536]{1,0:T(8,128)(2,1)S(1)}, u32[]{:S(2)}, u32[]{:S(2)}) collective-permute-start(bf16[144,1536]{1,0:T(8,128)(2,1)} %get-tuple-element.61), channel_id=1, source_target_pairs={{1,2},{2,1},{5,6},{6,5},{9,10},{10,9},{13,14},{14,13},{17,18},{18,... | collective-permute-start | bytes 1327112 | tf_op jit(solution)/shard_map/ppermute | solution.py:18
  122.9 9.4 %all-to-all-start.1 = ((f32[8,1,12]{2,1,0:T(1,128)}), f32[8,1,12]{2,1,0:T(1,128)S(1)}, u32[]{:S(2)}, u32[]{:S(2)}) async-start(f32[8,1,12]{2,1,0:T(1,128)} %get-tuple-element.58), calls=%async_computation.1 | async-start | bytes 8192 | tf_op jit(solution)/shard_map/all_to_all | solution.py:22
  132.4 0.0 collective-permute-done.14.refs_1_
  132.4 0.0 collective-permute-done.15.refs_2_
  132.4 2.0 %shard_map.127 = bf16[144,1536]{1,0:T(8,128)(2,1)} custom-call(f32[144,1536]{1,0:T(8,128)S(1)} %get-tuple-element.51.refs_0_, bf16[144,1536]{1,0:T(8,128)(2,1)} %collective-permute-done.14.refs_1_, bf16[144,1536]{1,0:T(8,128)(2,1)} %collective-permute-done.15.refs_2_), custom_call_target="tpu_custom_call" | custom-call | tf_op jit(solution)/shard_map/pallas_call | solution.py:82
  134.4 5.6 %all-to-all-done.1.refs_0_ = f32[8,1,12]{2,1,0:T(1,128)S(1)} async-done(((f32[8,1,12]{2,1,0:T(1,128)}), f32[8,1,12]{2,1,0:T(1,128)S(1)}, u32[]{:S(2)}, u32[]{:S(2)}) %all-to-all-start.1) | async-done | bytes 416 | tf_op jit(solution)/shard_map/all_to_all | solution.py:22
  140.0 0.0 collective-permute-done.18.refs_2_
  140.0 0.0 collective-permute-done.19.refs_3_
  140.0 0.9 shard_map.129
  (11 shorter events, 0.1 us)
Async XLA Ops:
  0.6 16.2 %collective-permute-start.5 = (bf16[144,1536]{1,0:T(8,128)(2,1)}, bf16[144,1536]{1,0:T(8,128)(2,1)S(1)}, u32[]{:S(2)}, u32[]{:S(2)}) collective-permute-start(bf16[144,1536]{1,0:T(8,128)(2,1)} %bitcast.45), channel_id=1, source_target_pairs={{1,2},{2,1},{5,6},{6,5},{9,10},{10,9},{13,14},{14,13},{17,18},{18,... | collective-permute-start | bytes 1327112 | tf_op jit(solution)/shard_map/ppermute | solution.py:18
  4.1 13.7 %collective-permute-start.4 = (bf16[144,1536]{1,0:T(8,128)(2,1)}, bf16[144,1536]{1,0:T(8,128)(2,1)S(1)}, u32[]{:S(2)}, u32[]{:S(2)}) collective-permute-start(bf16[144,1536]{1,0:T(8,128)(2,1)} %bitcast.46), channel_id=1, source_target_pairs={{0,1},{1,0},{2,3},{3,2},{4,5},{5,4},{6,7},{7,6},{8,9},{9,8},{10,11... | collective-permute-start | bytes 1327112 | tf_op jit(solution)/shard_map/ppermute | solution.py:18
  9.1 17.8 %collective-permute-start.1 = (bf16[144,1536]{1,0:T(8,128)(2,1)}, bf16[144,1536]{1,0:T(8,128)(2,1)S(1)}, u32[]{:S(2)}, u32[]{:S(2)}) collective-permute-start(bf16[144,1536]{1,0:T(8,128)(2,1)} %bitcast.48), channel_id=1, source_target_pairs={{4,8},{8,4},{12,16},{16,12},{20,24},{24,20},{5,9},{9,5},{13,17},{1... | collective-permute-start | bytes 1327112 | tf_op jit(solution)/shard_map/ppermute | solution.py:18
  9.8 17.1 %collective-permute-start = (bf16[144,1536]{1,0:T(8,128)(2,1)}, bf16[144,1536]{1,0:T(8,128)(2,1)S(1)}, u32[]{:S(2)}, u32[]{:S(2)}) collective-permute-start(bf16[144,1536]{1,0:T(8,128)(2,1)} %bitcast.49), channel_id=1, source_target_pairs={{0,4},{4,0},{8,12},{12,8},{16,20},{20,16},{24,28},{28,24},{1,5},{5... | collective-permute-start | bytes 1327112 | tf_op jit(solution)/shard_map/ppermute | solution.py:18
  14.6 1.0 copy-start.1
  15.7 1.0 copy-start
  16.7 30.0 %copy-start.8 = (s32[1,8,4,2]{1,3,2,0:T(2,128)S(1)}, s32[1,8,4,2]{1,3,2,0:T(2,128)}, u32[]{:S(2)}) copy-start(s32[1,8,4,2]{1,3,2,0:T(2,128)} %param.14) | copy-start | bytes 772
  16.8 30.1 %copy-start.2 = (bf16[1,6,8,3,1536]{4,2,3,1,0:T(8,128)(2,1)S(1)}, bf16[1,6,8,3,1536]{4,2,3,1,0:T(8,128)(2,1)}, u32[]{:S(2)}) copy-start(bf16[1,6,8,3,1536]{4,2,3,1,0:T(8,128)(2,1)} %param.9) | copy-start | bytes 1327108
  16.8 30.1 %copy-start.3 = (bf16[1,6,8,3,1536]{4,2,3,1,0:T(8,128)(2,1)S(1)}, bf16[1,6,8,3,1536]{4,2,3,1,0:T(8,128)(2,1)}, u32[]{:S(2)}) copy-start(bf16[1,6,8,3,1536]{4,2,3,1,0:T(8,128)(2,1)} %param.12) | copy-start | bytes 1327108
  16.8 30.0 %copy-start.4 = (s32[144,1]{1,0:T(8,128)S(1)}, s32[144,1]{1,0:T(8,128)}, u32[]{:S(2)}) copy-start(s32[144,1]{1,0:T(8,128)} %constant.7.clone.slot_col_ref) | copy-start | bytes 1732
  16.8 30.0 %copy-start.5 = (s32[1,1296]{1,0:T(1,128)S(1)}, s32[1,1296]{1,0:T(1,128)}, u32[]{:S(2)}) copy-start(s32[1,1296]{1,0:T(1,128)} %constant.6.clone.slot_row_ref) | copy-start | bytes 15556
  16.8 30.0 %copy-start.6 = (s32[1,8,4]{1,2,0:T(4,128)S(1)}, s32[1,8,4]{1,2,0:T(4,128)}, u32[]{:S(2)}) copy-start(s32[1,8,4]{1,2,0:T(4,128)} %param.13) | copy-start | bytes 388
  16.8 30.0 %copy-start.7 = (f32[12]{0:T(128)S(1)}, f32[12]{0:T(128)}, u32[]{:S(2)}) copy-start(f32[12]{0:T(128)} %sharpness_ref.3) | copy-start | bytes 148
  17.9 14.4 %collective-permute-start.11 = (bf16[432,768]{1,0:T(8,128)(2,1)S(1)}, bf16[432,768]{1,0:T(8,128)(2,1)S(1)}, u32[]{:S(2)}, u32[]{:S(2)}) collective-permute-start(bf16[432,768]{1,0:T(8,128)(2,1)S(1)} %get-tuple-element.37.refs_3_), channel_id=1, source_target_pairs={{4,8},{8,4},{12,16},{16,12},{20,24},{24,20},{5,9},{9,5},{13,17},{1... | collective-permute-start | bytes 1990664 | tf_op jit(solution)/shard_map/ppermute | solution.py:18
  18.7 23.7 %collective-permute-start.10 = (bf16[432,768]{1,0:T(8,128)(2,1)S(1)}, bf16[432,768]{1,0:T(8,128)(2,1)S(1)}, u32[]{:S(2)}, u32[]{:S(2)}) collective-permute-start(bf16[432,768]{1,0:T(8,128)(2,1)S(1)} %get-tuple-element.37.refs_3_), channel_id=1, source_target_pairs={{0,4},{4,0},{8,12},{12,8},{16,20},{20,16},{24,28},{28,24},{1,5},{5... | collective-permute-start | bytes 1990664 | tf_op jit(solution)/shard_map/ppermute | solution.py:18
  27.0 17.7 %collective-permute-start.9 = (bf16[432,768]{1,0:T(8,128)(2,1)S(1)}, bf16[432,768]{1,0:T(8,128)(2,1)S(1)}, u32[]{:S(2)}, u32[]{:S(2)}) collective-permute-start(bf16[432,768]{1,0:T(8,128)(2,1)S(1)} %get-tuple-element.36.refs_0_), channel_id=1, source_target_pairs={{1,2},{2,1},{5,6},{6,5},{9,10},{10,9},{13,14},{14,13},{17,18},{18,... | collective-permute-start | bytes 1990664 | tf_op jit(solution)/shard_map/ppermute | solution.py:18
  29.3 17.4 %collective-permute-start.8 = (bf16[432,768]{1,0:T(8,128)(2,1)S(1)}, bf16[432,768]{1,0:T(8,128)(2,1)S(1)}, u32[]{:S(2)}, u32[]{:S(2)}) collective-permute-start(bf16[432,768]{1,0:T(8,128)(2,1)S(1)} %get-tuple-element.36.refs_0_), channel_id=1, source_target_pairs={{0,1},{1,0},{2,3},{3,2},{4,5},{5,4},{6,7},{7,6},{8,9},{9,8},{10,11... | collective-permute-start | bytes 1990664 | tf_op jit(solution)/shard_map/ppermute | solution.py:18
  31.6 24.4 %collective-permute-start.7 = (bf16[432,768]{1,0:T(8,128)(2,1)S(1)}, bf16[432,768]{1,0:T(8,128)(2,1)S(1)}, u32[]{:S(2)}, u32[]{:S(2)}) collective-permute-start(bf16[432,768]{1,0:T(8,128)(2,1)S(1)} %get-tuple-element.35.refs_3_), channel_id=1, source_target_pairs={{4,8},{8,4},{12,16},{16,12},{20,24},{24,20},{5,9},{9,5},{13,17},{1... | collective-permute-start | bytes 1990664 | tf_op jit(solution)/shard_map/ppermute | solution.py:18
  32.3 23.7 %collective-permute-start.6 = (bf16[432,768]{1,0:T(8,128)(2,1)S(1)}, bf16[432,768]{1,0:T(8,128)(2,1)S(1)}, u32[]{:S(2)}, u32[]{:S(2)}) collective-permute-start(bf16[432,768]{1,0:T(8,128)(2,1)S(1)} %get-tuple-element.35.refs_3_), channel_id=1, source_target_pairs={{0,4},{4,0},{8,12},{12,8},{16,20},{20,16},{24,28},{28,24},{1,5},{5... | collective-permute-start | bytes 1990664 | tf_op jit(solution)/shard_map/ppermute | solution.py:18
  42.4 16.0 %collective-permute-start.3 = (bf16[432,768]{1,0:T(8,128)(2,1)S(1)}, bf16[432,768]{1,0:T(8,128)(2,1)S(1)}, u32[]{:S(2)}, u32[]{:S(2)}) collective-permute-start(bf16[432,768]{1,0:T(8,128)(2,1)S(1)} %get-tuple-element.34.refs_0_), channel_id=1, source_target_pairs={{1,2},{2,1},{5,6},{6,5},{9,10},{10,9},{13,14},{14,13},{17,18},{18,... | collective-permute-start | bytes 1990664 | tf_op jit(solution)/shard_map/ppermute | solution.py:18
  44.7 15.7 %collective-permute-start.2 = (bf16[432,768]{1,0:T(8,128)(2,1)S(1)}, bf16[432,768]{1,0:T(8,128)(2,1)S(1)}, u32[]{:S(2)}, u32[]{:S(2)}) collective-permute-start(bf16[432,768]{1,0:T(8,128)(2,1)S(1)} %get-tuple-element.34.refs_0_), channel_id=1, source_target_pairs={{0,1},{1,0},{2,3},{3,2},{4,5},{5,4},{6,7},{7,6},{8,9},{9,8},{10,11... | collective-permute-start | bytes 1990664 | tf_op jit(solution)/shard_map/ppermute | solution.py:18
  69.6 35.8 %collective-permute-start.12 = (bf16[432,1536]{1,0:T(8,128)(2,1)}, bf16[432,1536]{1,0:T(8,128)(2,1)}, u32[]{:S(2)}, u32[]{:S(2)}) collective-permute-start(bf16[432,1536]{1,0:T(8,128)(2,1)} %get-tuple-element.49), channel_id=1, source_target_pairs={{0,1},{1,0},{2,3},{3,2},{4,5},{5,4},{6,7},{7,6},{8,9},{9,8},{10,11... | collective-permute-start | bytes 3981320 | tf_op jit(solution)/shard_map/ppermute | solution.py:18
  71.8 33.5 %collective-permute-start.13 = (bf16[432,1536]{1,0:T(8,128)(2,1)}, bf16[432,1536]{1,0:T(8,128)(2,1)}, u32[]{:S(2)}, u32[]{:S(2)}) collective-permute-start(bf16[432,1536]{1,0:T(8,128)(2,1)} %get-tuple-element.50), channel_id=1, source_target_pairs={{1,2},{2,1},{5,6},{6,5},{9,10},{10,9},{13,14},{14,13},{17,18},{18,... | collective-permute-start | bytes 3981320 | tf_op jit(solution)/shard_map/ppermute | solution.py:18
  75.3 36.6 %collective-permute-start.16 = (bf16[432,1536]{1,0:T(8,128)(2,1)}, bf16[432,1536]{1,0:T(8,128)(2,1)}, u32[]{:S(2)}, u32[]{:S(2)}) collective-permute-start(bf16[432,1536]{1,0:T(8,128)(2,1)} %get-tuple-element.56), channel_id=1, source_target_pairs={{0,4},{4,0},{8,12},{12,8},{16,20},{20,16},{24,28},{28,24},{1,5},{5... | collective-permute-start | bytes 3981320 | tf_op jit(solution)/shard_map/ppermute | solution.py:18
  77.7 34.2 %collective-permute-start.17 = (bf16[432,1536]{1,0:T(8,128)(2,1)}, bf16[432,1536]{1,0:T(8,128)(2,1)}, u32[]{:S(2)}, u32[]{:S(2)}) collective-permute-start(bf16[432,1536]{1,0:T(8,128)(2,1)} %get-tuple-element.57), channel_id=1, source_target_pairs={{4,8},{8,4},{12,16},{16,12},{20,24},{24,20},{5,9},{9,5},{13,17},{1... | collective-permute-start | bytes 3981320 | tf_op jit(solution)/shard_map/ppermute | solution.py:18
  108.2 24.2 %collective-permute-start.14 = (bf16[144,1536]{1,0:T(8,128)(2,1)}, bf16[144,1536]{1,0:T(8,128)(2,1)}, u32[]{:S(2)}, u32[]{:S(2)}) collective-permute-start(bf16[144,1536]{1,0:T(8,128)(2,1)} %get-tuple-element.52), channel_id=1, source_target_pairs={{0,4},{4,0},{8,12},{12,8},{16,20},{20,16},{24,28},{28,24},{1,5},{5... | collective-permute-start | bytes 1327112 | tf_op jit(solution)/shard_map/ppermute | solution.py:18
  110.4 21.9 %collective-permute-start.15 = (bf16[144,1536]{1,0:T(8,128)(2,1)}, bf16[144,1536]{1,0:T(8,128)(2,1)}, u32[]{:S(2)}, u32[]{:S(2)}) collective-permute-start(bf16[144,1536]{1,0:T(8,128)(2,1)} %get-tuple-element.53), channel_id=1, source_target_pairs={{4,8},{8,4},{12,16},{16,12},{20,24},{24,20},{5,9},{9,5},{13,17},{1... | collective-permute-start | bytes 1327112 | tf_op jit(solution)/shard_map/ppermute | solution.py:18
  114.7 25.3 %collective-permute-start.18 = (bf16[144,1536]{1,0:T(8,128)(2,1)}, bf16[144,1536]{1,0:T(8,128)(2,1)S(1)}, u32[]{:S(2)}, u32[]{:S(2)}) collective-permute-start(bf16[144,1536]{1,0:T(8,128)(2,1)} %get-tuple-element.60), channel_id=1, source_target_pairs={{0,1},{1,0},{2,3},{3,2},{4,5},{5,4},{6,7},{7,6},{8,9},{9,8},{10,11... | collective-permute-start | bytes 1327112 | tf_op jit(solution)/shard_map/ppermute | solution.py:18
  119.5 20.5 %collective-permute-start.19 = (bf16[144,1536]{1,0:T(8,128)(2,1)}, bf16[144,1536]{1,0:T(8,128)(2,1)S(1)}, u32[]{:S(2)}, u32[]{:S(2)}) collective-permute-start(bf16[144,1536]{1,0:T(8,128)(2,1)} %get-tuple-element.61), channel_id=1, source_target_pairs={{1,2},{2,1},{5,6},{6,5},{9,10},{10,9},{13,14},{14,13},{17,18},{18,... | collective-permute-start | bytes 1327112 | tf_op jit(solution)/shard_map/ppermute | solution.py:18
  122.9 17.1 %all-to-all-start.1 = ((f32[8,1,12]{2,1,0:T(1,128)}), f32[8,1,12]{2,1,0:T(1,128)S(1)}, u32[]{:S(2)}, u32[]{:S(2)}) async-start(f32[8,1,12]{2,1,0:T(1,128)} %get-tuple-element.58), calls=%async_computation.1 | async-start | bytes 8192 | tf_op jit(solution)/shard_map/all_to_all | solution.py:22

commit v3 on v2

--- a/solution.py
+++ b/solution.py
@@ -139,7 +139,7 @@
     query_grad_ref, sharpness_grad_ref = refs[0], refs[1]
     key_part_refs, value_part_refs = refs[2:5], refs[5:8]
     bias_ref, valid_ref = refs[8], refs[9]
-    work = [refs[10 + 4 * j : 14 + 4 * j] for j in range(together)]
+    work = (refs[10:14], refs[14:18])
     head_dim = query_ref.shape[1] // together
     time_tile = lax.axis_index("tm")
     high_tile = lax.axis_index("height")
@@ -185,8 +185,8 @@
         query, grad, keys, values = operands(j)
         sharp = sharpness_ref[opening + pl.program_id(0) * together + j]
         factor = sharp * (1.0 / math.sqrt(head_dim))
-        logits_ref, grad_weight_ref, low_ref, scaled_ref = work[j]
-        score_gradients(factor * math.log2(math.e), bias_ref, valid_ref, *work[j])
+        logits_ref, grad_weight_ref, low_ref, scaled_ref = work[j % 2]
+        score_gradients(factor * math.log2(math.e), bias_ref, valid_ref, *work[j % 2])
         low, scaled = low_ref[...], scaled_ref[...]
         down = (((0,), (0,)), ((), ()))
         query_grad = jnp.dot(scaled, keys, preferred_element_type=jnp.float32) * factor
@@ -208,13 +208,13 @@
     raw_scores(*operands(0), *work[0][:2])
     for j in range(together):
         if j + 1 < together:
-            raw_scores(*operands(j + 1), *work[j + 1][:2])
+            raw_scores(*operands(j + 1), *work[(j + 1) % 2][:2])
         gradients(j)
 
 
 def attention(chunk, branches, tile_len, head_dim, small, query, grad, keys, values, so_far):
     opening, heads = chunk
-    together = 2
+    together = heads
     first = opening // together
     smem = pl.BlockSpec(memory_space=pltpu.SMEM)
     whole = lambda array: pl.BlockSpec(array.shape, lambda h: (0, 0))
@@ -248,7 +248,7 @@
             pltpu.VMEM(score, jnp.bfloat16),
             pltpu.VMEM(score, jnp.bfloat16),
         ]
-        * together,
+        * 2,
         compiler_params=pltpu.CompilerParams(vmem_limit_bytes=24 * 1024 * 1024),
         cost_estimate=pl.CostEstimate(
             flops=10 * pairs * head_dim,

time: 142 us -> 141 us (level)
  no operation moved by 1% of the time
where the time goes in v3:
time: 141 us; the launch traced here: 140 us
  starting transfers between devices  73.6 us (52%)
  Pallas kernels  26.2 us (19%)
  blocking collectives  25.5 us (18%)
  waiting for transfers between devices  11.9 us (8%)
  local copies, waits for them, and re-layouts  2.1 us (1%)
    ppermute x20, starting transfers between devices, exchanged(): lax.ppermute(block, axis, [(i, j) for i, j in enumerate(partner) if 0 <=...  64.2 us
    all_to_all x1, blocking collectives, swapped(): return lax.all_to_all(rows, axes, 0, 0)  25.5 us
    pallas_call x2, Pallas kernels, attention(): pl.pallas_call(functools.partial(attention_body, opening, tile_len, toget...  17.4 us
    all_to_all x1, starting transfers between devices, swapped(): return lax.all_to_all(rows, axes, 0, 0)  9.4 us
    ppermute x20, waiting for transfers between devices, exchanged(): lax.ppermute(block, axis, [(i, j) for i, j in enumerate(partner) if 0 <=...  6.28 us
    pallas_call x2, Pallas kernels, summed_parts(): pl.pallas_call(functools.partial(sum_body, rows is not None), in_specs=[v...  5.63 us
    all_to_all x1, waiting for transfers between devices, swapped(): return lax.all_to_all(rows, axes, 0, 0)  5.61 us
    pallas_call x2, Pallas kernels, final_sum(): pl.pallas_call(functools.partial(final_body, rows is not None), in_specs=...  2.94 us
  transfers between devices with their start and end apart: 21, of which 5 were waited for; matrix products, arithmetic and copies ran while one was open for 0% of the time, Pallas kernels for 12%

profile of v3, /device:TPU:8, one launch (start us, length us, event | category | flops | bytes accessed | tf_op | source)
XLA Modules:
  0.0 140.4 jit_solution(11977006350279176072)
XLA Ops:
  0.6 3.5 %collective-permute-start.5 = (bf16[144,1536]{1,0:T(8,128)(2,1)}, bf16[144,1536]{1,0:T(8,128)(2,1)S(1)}, u32[]{:S(2)}, u32[]{:S(2)}) collective-permute-start(bf16[144,1536]{1,0:T(8,128)(2,1)} %bitcast.45), channel_id=1, source_target_pairs={{1,2},{2,1},{5,6},{6,5},{9,10},{10,9},{13,14},{14,13},{17,18},{18,... | collective-permute-start | bytes 1327112 | tf_op jit(solution)/shard_map/ppermute | solution.py:18
  4.1 4.9 %collective-permute-start.4 = (bf16[144,1536]{1,0:T(8,128)(2,1)}, bf16[144,1536]{1,0:T(8,128)(2,1)S(1)}, u32[]{:S(2)}, u32[]{:S(2)}) collective-permute-start(bf16[144,1536]{1,0:T(8,128)(2,1)} %bitcast.46), channel_id=1, source_target_pairs={{0,1},{1,0},{2,3},{3,2},{4,5},{5,4},{6,7},{7,6},{8,9},{9,8},{10,11... | collective-permute-start | bytes 1327112 | tf_op jit(solution)/shard_map/ppermute | solution.py:18
  9.1 0.7 collective-permute-start.1
  9.8 4.9 %collective-permute-start = (bf16[144,1536]{1,0:T(8,128)(2,1)}, bf16[144,1536]{1,0:T(8,128)(2,1)S(1)}, u32[]{:S(2)}, u32[]{:S(2)}) collective-permute-start(bf16[144,1536]{1,0:T(8,128)(2,1)} %bitcast.49), channel_id=1, source_target_pairs={{0,4},{4,0},{8,12},{12,8},{16,20},{20,16},{24,28},{28,24},{1,5},{5... | collective-permute-start | bytes 1327112 | tf_op jit(solution)/shard_map/ppermute | solution.py:18
  14.6 0.0 copy-start.1
  14.6 1.0 copy-done.1
  15.7 0.0 copy-start
  15.7 1.0 copy-done
  16.7 0.0 copy-start.8
  16.8 0.0 copy-start.2
  16.8 0.0 copy-start.3
  16.8 0.0 copy-start.4
  16.8 0.0 copy-start.5
  16.8 0.0 copy-start.6
  16.8 0.0 copy-start.7
  16.8 0.0 collective-permute-done.5.refs_2_
  16.8 1.0 collective-permute-done.4.refs_1_
  17.9 0.1 shard_map.123
  17.9 0.7 collective-permute-start.11
  18.7 8.2 %collective-permute-start.10 = (bf16[432,768]{1,0:T(8,128)(2,1)S(1)}, bf16[432,768]{1,0:T(8,128)(2,1)S(1)}, u32[]{:S(2)}, u32[]{:S(2)}) collective-permute-start(bf16[432,768]{1,0:T(8,128)(2,1)S(1)} %get-tuple-element.37.refs_3_), channel_id=1, source_target_pairs={{0,4},{4,0},{8,12},{12,8},{16,20},{20,16},{24,28},{28,24},{1,5},{5... | collective-permute-start | bytes 1990664 | tf_op jit(solution)/shard_map/ppermute | solution.py:18
  26.9 0.0 collective-permute-done.1.refs_2_
  26.9 0.0 collective-permute-done.refs_1_
  26.9 0.1 shard_map.121
  27.0 2.4 %collective-permute-start.9 = (bf16[432,768]{1,0:T(8,128)(2,1)S(1)}, bf16[432,768]{1,0:T(8,128)(2,1)S(1)}, u32[]{:S(2)}, u32[]{:S(2)}) collective-permute-start(bf16[432,768]{1,0:T(8,128)(2,1)S(1)} %get-tuple-element.36.refs_0_), channel_id=1, source_target_pairs={{1,2},{2,1},{5,6},{6,5},{9,10},{10,9},{13,14},{14,13},{17,18},{18,... | collective-permute-start | bytes 1990664 | tf_op jit(solution)/shard_map/ppermute | solution.py:18
  29.3 2.3 %collective-permute-start.8 = (bf16[432,768]{1,0:T(8,128)(2,1)S(1)}, bf16[432,768]{1,0:T(8,128)(2,1)S(1)}, u32[]{:S(2)}, u32[]{:S(2)}) collective-permute-start(bf16[432,768]{1,0:T(8,128)(2,1)S(1)} %get-tuple-element.36.refs_0_), channel_id=1, source_target_pairs={{0,1},{1,0},{2,3},{3,2},{4,5},{5,4},{6,7},{7,6},{8,9},{9,8},{10,11... | collective-permute-start | bytes 1990664 | tf_op jit(solution)/shard_map/ppermute | solution.py:18
  31.6 0.7 collective-permute-start.7
  32.3 0.0 collective-permute-done.11.refs_5_
  32.3 10.0 %collective-permute-start.6 = (bf16[432,768]{1,0:T(8,128)(2,1)S(1)}, bf16[432,768]{1,0:T(8,128)(2,1)S(1)}, u32[]{:S(2)}, u32[]{:S(2)}) collective-permute-start(bf16[432,768]{1,0:T(8,128)(2,1)S(1)} %get-tuple-element.35.refs_3_), channel_id=1, source_target_pairs={{0,4},{4,0},{8,12},{12,8},{16,20},{20,16},{24,28},{28,24},{1,5},{5... | collective-permute-start | bytes 1990664 | tf_op jit(solution)/shard_map/ppermute | solution.py:18
  42.4 0.0 collective-permute-done.10.refs_4_
  42.4 1.9 %collective-permute-start.3 = (bf16[432,768]{1,0:T(8,128)(2,1)S(1)}, bf16[432,768]{1,0:T(8,128)(2,1)S(1)}, u32[]{:S(2)}, u32[]{:S(2)}) collective-permute-start(bf16[432,768]{1,0:T(8,128)(2,1)S(1)} %get-tuple-element.34.refs_0_), channel_id=1, source_target_pairs={{1,2},{2,1},{5,6},{6,5},{9,10},{10,9},{13,14},{14,13},{17,18},{18,... | collective-permute-start | bytes 1990664 | tf_op jit(solution)/shard_map/ppermute | solution.py:18
  44.3 0.4 collective-permute-done.9.refs_2_
  44.7 2.0 %collective-permute-start.2 = (bf16[432,768]{1,0:T(8,128)(2,1)S(1)}, bf16[432,768]{1,0:T(8,128)(2,1)S(1)}, u32[]{:S(2)}, u32[]{:S(2)}) collective-permute-start(bf16[432,768]{1,0:T(8,128)(2,1)S(1)} %get-tuple-element.34.refs_0_), channel_id=1, source_target_pairs={{0,1},{1,0},{2,3},{3,2},{4,5},{5,4},{6,7},{7,6},{8,9},{9,8},{10,11... | collective-permute-start | bytes 1990664 | tf_op jit(solution)/shard_map/ppermute | solution.py:18
  46.8 0.0 copy-done.8
  46.8 0.0 collective-permute-done.8.refs_1_
  46.9 8.7 %shard_map.124 = (bf16[144,1536]{1,0:T(8,128)(2,1)}, f32[12,1,128]{2,1,0:T(1,128)S(1)}, bf16[432,1536]{1,0:T(8,128)(2,1)S(1)}, bf16[432,1536]{1,0:T(8,128)(2,1)}...) custom-call(f32[12]{0:T(128)S(1)} %copy-done.7, ...), custom_call_target="tpu_custom_call" | custom-call | flops 1433272320 | bytes 7962624 | tf_op jit(solution)/shard_map/pallas_call | solution.py:226
  55.6 0.0 collective-permute-done.7.refs_5_
  55.6 0.0 collective-permute-done.6.refs_4_
  55.6 2.7 %collective-permute-done.3.refs_2_ = bf16[432,768]{1,0:T(8,128)(2,1)S(1)} collective-permute-done((bf16[432,768]{1,0:T(8,128)(2,1)S(1)}, bf16[432,768]{1,0:T(8,128)(2,1)S(1)}, u32[]{:S(2)}, u32[]{:S(2)}) %collective-permute-start.3) | collective-permute-done | bytes 663584 | tf_op jit(solution)/shard_map/ppermute | solution.py:18
  58.3 2.1 %collective-permute-done.2.refs_1_ = bf16[432,768]{1,0:T(8,128)(2,1)S(1)} collective-permute-done((bf16[432,768]{1,0:T(8,128)(2,1)S(1)}, bf16[432,768]{1,0:T(8,128)(2,1)S(1)}, u32[]{:S(2)}, u32[]{:S(2)}) %collective-permute-start.2) | collective-permute-done | bytes 663584 | tf_op jit(solution)/shard_map/ppermute | solution.py:18
  60.4 8.6 %shard_map.125 = (bf16[144,1536]{1,0:T(8,128)(2,1)}, f32[12,1,128]{2,1,0:T(1,128)S(1)}, bf16[432,1536]{1,0:T(8,128)(2,1)S(1)}, bf16[432,1536]{1,0:T(8,128)(2,1)}...) custom-call(f32[12]{0:T(128)S(1)} %copy-done.7, ...), custom_call_target="tpu_custom_call", output_to_operand_aliasing={{0}: (13, {}), {1}: (14, {}), {2}: (15, {}), {3}: (16, {}),... | custom-call | flops 1433272320 | bytes 7962624 | tf_op jit(solution)/shard_map/pallas_call | solution.py:226
  69.1 2.3 %collective-permute-start.12 = (bf16[432,1536]{1,0:T(8,128)(2,1)}, bf16[432,1536]{1,0:T(8,128)(2,1)}, u32[]{:S(2)}, u32[]{:S(2)}) collective-permute-start(bf16[432,1536]{1,0:T(8,128)(2,1)} %get-tuple-element.49), channel_id=1, source_target_pairs={{0,1},{1,0},{2,3},{3,2},{4,5},{5,4},{6,7},{7,6},{8,9},{9,8},{10,11... | collective-permute-start | bytes 3981320 | tf_op jit(solution)/shard_map/ppermute | solution.py:18
  71.3 3.6 %collective-permute-start.13 = (bf16[432,1536]{1,0:T(8,128)(2,1)}, bf16[432,1536]{1,0:T(8,128)(2,1)}, u32[]{:S(2)}, u32[]{:S(2)}) collective-permute-start(bf16[432,1536]{1,0:T(8,128)(2,1)} %get-tuple-element.50), channel_id=1, source_target_pairs={{1,2},{2,1},{5,6},{6,5},{9,10},{10,9},{13,14},{14,13},{17,18},{18,... | collective-permute-start | bytes 3981320 | tf_op jit(solution)/shard_map/ppermute | solution.py:18
  74.9 2.4 %collective-permute-start.16 = (bf16[432,1536]{1,0:T(8,128)(2,1)}, bf16[432,1536]{1,0:T(8,128)(2,1)}, u32[]{:S(2)}, u32[]{:S(2)}) collective-permute-start(bf16[432,1536]{1,0:T(8,128)(2,1)} %get-tuple-element.56), channel_id=1, source_target_pairs={{0,4},{4,0},{8,12},{12,8},{16,20},{20,16},{24,28},{28,24},{1,5},{5... | collective-permute-start | bytes 3981320 | tf_op jit(solution)/shard_map/ppermute | solution.py:18
  77.4 1.7 %collective-permute-start.17 = (bf16[432,1536]{1,0:T(8,128)(2,1)}, bf16[432,1536]{1,0:T(8,128)(2,1)}, u32[]{:S(2)}, u32[]{:S(2)}) collective-permute-start(bf16[432,1536]{1,0:T(8,128)(2,1)} %get-tuple-element.57), channel_id=1, source_target_pairs={{4,8},{8,4},{12,16},{16,12},{20,24},{24,20},{5,9},{9,5},{13,17},{1... | collective-permute-start | bytes 3981320 | tf_op jit(solution)/shard_map/ppermute | solution.py:18
  79.1 0.2 reduce_sum.9
  79.3 25.5 %all_to_all.10.refs_0_ = f32[64,1,12]{2,1,0:T(1,128)S(1)} all-to-all(f32[64,1,12]{2,1,0:T(1,128)S(1)} %broadcast_in_dim.13), channel_id=1, replica_groups=mesh['dp'=16,'tm'=8,'height'=4] {'dp','height'}, dimensions={0} | all-to-all | bytes 6144 | tf_op jit(solution)/shard_map/all_to_all | solution.py:22
  104.8 0.0 collective-permute-done.12.refs_2_
  104.9 0.0 collective-permute-done.13.refs_3_
  104.9 2.8 %shard_map.126 = (f32[1,1,12]{2,1,0:T(1,128)S(1)}, f32[144,1536]{1,0:T(8,128)S(1)}, bf16[144,1536]{1,0:T(8,128)(2,1)}, bf16[144,1536]{1,0:T(8,128)(2,1)}) custom-call(f32[64,1,12]{2,1,0:T(1,128)S(1)} %all_to_all.10.refs_0_, bf16[432,1536]{1,0:T(8,128)(2,1)S(1)} %get-tuple-element.48.refs_1_, bf16[432,1536]{1,0:T(8,128)(2,1)} %collective-permute-done.12.refs_2_, ...), custom_call_target="tpu_custom_call" | custom-call | tf_op jit(solution)/shard_map/pallas_call | solution.py:56
  107.7 2.3 %collective-permute-start.14 = (bf16[144,1536]{1,0:T(8,128)(2,1)}, bf16[144,1536]{1,0:T(8,128)(2,1)}, u32[]{:S(2)}, u32[]{:S(2)}) collective-permute-start(bf16[144,1536]{1,0:T(8,128)(2,1)} %get-tuple-element.52), channel_id=1, source_target_pairs={{0,4},{4,0},{8,12},{12,8},{16,20},{20,16},{24,28},{28,24},{1,5},{5... | collective-permute-start | bytes 1327112 | tf_op jit(solution)/shard_map/ppermute | solution.py:18
  109.9 1.4 %collective-permute-start.15 = (bf16[144,1536]{1,0:T(8,128)(2,1)}, bf16[144,1536]{1,0:T(8,128)(2,1)}, u32[]{:S(2)}, u32[]{:S(2)}) collective-permute-start(bf16[144,1536]{1,0:T(8,128)(2,1)} %get-tuple-element.53), channel_id=1, source_target_pairs={{4,8},{8,4},{12,16},{16,12},{20,24},{24,20},{5,9},{9,5},{13,17},{1... | collective-permute-start | bytes 1327112 | tf_op jit(solution)/shard_map/ppermute | solution.py:18
  111.4 0.0 collective-permute-done.16.refs_2_
  111.4 0.0 collective-permute-done.17.refs_3_
  111.4 2.8 %shard_map.128 = (f32[8,1,12]{2,1,0:T(1,128)}, f32[144,1536]{1,0:T(8,128)S(1)}, bf16[144,1536]{1,0:T(8,128)(2,1)}, bf16[144,1536]{1,0:T(8,128)(2,1)}) custom-call(f32[1,1,12]{2,1,0:T(1,128)S(1)} %get-tuple-element.54.refs_0_, bf16[432,1536]{1,0:T(8,128)(2,1)S(1)} %get-tuple-element.55.refs_1_, bf16[432,1536]{1,0:T(8,128)(2,1)} %collective-permute-done.16.refs_2_, ...), custom_call_target="tpu_custom_call" | custom-call | tf_op jit(solution)/shard_map/pallas_call | solution.py:56
  114.2 4.8 %collective-permute-start.18 = (bf16[144,1536]{1,0:T(8,128)(2,1)}, bf16[144,1536]{1,0:T(8,128)(2,1)S(1)}, u32[]{:S(2)}, u32[]{:S(2)}) collective-permute-start(bf16[144,1536]{1,0:T(8,128)(2,1)} %get-tuple-element.60), channel_id=1, source_target_pairs={{0,1},{1,0},{2,3},{3,2},{4,5},{5,4},{6,7},{7,6},{8,9},{9,8},{10,11... | collective-permute-start | bytes 1327112 | tf_op jit(solution)/shard_map/ppermute | solution.py:18
  119.0 3.4 %collective-permute-start.19 = (bf16[144,1536]{1,0:T(8,128)(2,1)}, bf16[144,1536]{1,0:T(8,128)(2,1)S(1)}, u32[]{:S(2)}, u32[]{:S(2)}) collective-permute-start(bf16[144,1536]{1,0:T(8,128)(2,1)} %get-tuple-element.61), channel_id=1, source_target_pairs={{1,2},{2,1},{5,6},{6,5},{9,10},{10,9},{13,14},{14,13},{17,18},{18,... | collective-permute-start | bytes 1327112 | tf_op jit(solution)/shard_map/ppermute | solution.py:18
  122.5 9.4 %all-to-all-start.1 = ((f32[8,1,12]{2,1,0:T(1,128)}), f32[8,1,12]{2,1,0:T(1,128)S(1)}, u32[]{:S(2)}, u32[]{:S(2)}) async-start(f32[8,1,12]{2,1,0:T(1,128)} %get-tuple-element.58), calls=%async_computation.1 | async-start | bytes 8192 | tf_op jit(solution)/shard_map/all_to_all | solution.py:22
  131.9 0.0 collective-permute-done.14.refs_1_
  131.9 0.0 collective-permute-done.15.refs_2_
  131.9 2.0 %shard_map.127 = bf16[144,1536]{1,0:T(8,128)(2,1)} custom-call(f32[144,1536]{1,0:T(8,128)S(1)} %get-tuple-element.51.refs_0_, bf16[144,1536]{1,0:T(8,128)(2,1)} %collective-permute-done.14.refs_1_, bf16[144,1536]{1,0:T(8,128)(2,1)} %collective-permute-done.15.refs_2_), custom_call_target="tpu_custom_call" | custom-call | tf_op jit(solution)/shard_map/pallas_call | solution.py:82
  133.9 5.6 %all-to-all-done.1.refs_0_ = f32[8,1,12]{2,1,0:T(1,128)S(1)} async-done(((f32[8,1,12]{2,1,0:T(1,128)}), f32[8,1,12]{2,1,0:T(1,128)S(1)}, u32[]{:S(2)}, u32[]{:S(2)}) %all-to-all-start.1) | async-done | bytes 416 | tf_op jit(solution)/shard_map/all_to_all | solution.py:22
  139.5 0.0 collective-permute-done.18.refs_2_
  139.5 0.0 collective-permute-done.19.refs_3_
  139.5 0.9 shard_map.129
  (11 shorter events, 0.1 us)
Async XLA Ops:
  0.6 16.2 %collective-permute-start.5 = (bf16[144,1536]{1,0:T(8,128)(2,1)}, bf16[144,1536]{1,0:T(8,128)(2,1)S(1)}, u32[]{:S(2)}, u32[]{:S(2)}) collective-permute-start(bf16[144,1536]{1,0:T(8,128)(2,1)} %bitcast.45), channel_id=1, source_target_pairs={{1,2},{2,1},{5,6},{6,5},{9,10},{10,9},{13,14},{14,13},{17,18},{18,... | collective-permute-start | bytes 1327112 | tf_op jit(solution)/shard_map/ppermute | solution.py:18
  4.1 13.7 %collective-permute-start.4 = (bf16[144,1536]{1,0:T(8,128)(2,1)}, bf16[144,1536]{1,0:T(8,128)(2,1)S(1)}, u32[]{:S(2)}, u32[]{:S(2)}) collective-permute-start(bf16[144,1536]{1,0:T(8,128)(2,1)} %bitcast.46), channel_id=1, source_target_pairs={{0,1},{1,0},{2,3},{3,2},{4,5},{5,4},{6,7},{7,6},{8,9},{9,8},{10,11... | collective-permute-start | bytes 1327112 | tf_op jit(solution)/shard_map/ppermute | solution.py:18
  9.1 17.8 %collective-permute-start.1 = (bf16[144,1536]{1,0:T(8,128)(2,1)}, bf16[144,1536]{1,0:T(8,128)(2,1)S(1)}, u32[]{:S(2)}, u32[]{:S(2)}) collective-permute-start(bf16[144,1536]{1,0:T(8,128)(2,1)} %bitcast.48), channel_id=1, source_target_pairs={{4,8},{8,4},{12,16},{16,12},{20,24},{24,20},{5,9},{9,5},{13,17},{1... | collective-permute-start | bytes 1327112 | tf_op jit(solution)/shard_map/ppermute | solution.py:18
  9.8 17.1 %collective-permute-start = (bf16[144,1536]{1,0:T(8,128)(2,1)}, bf16[144,1536]{1,0:T(8,128)(2,1)S(1)}, u32[]{:S(2)}, u32[]{:S(2)}) collective-permute-start(bf16[144,1536]{1,0:T(8,128)(2,1)} %bitcast.49), channel_id=1, source_target_pairs={{0,4},{4,0},{8,12},{12,8},{16,20},{20,16},{24,28},{28,24},{1,5},{5... | collective-permute-start | bytes 1327112 | tf_op jit(solution)/shard_map/ppermute | solution.py:18
  14.6 1.0 copy-start.1
  15.7 1.0 copy-start
  16.7 30.0 %copy-start.8 = (s32[1,8,4,2]{1,3,2,0:T(2,128)S(1)}, s32[1,8,4,2]{1,3,2,0:T(2,128)}, u32[]{:S(2)}) copy-start(s32[1,8,4,2]{1,3,2,0:T(2,128)} %param.14) | copy-start | bytes 772
  16.8 30.1 %copy-start.2 = (bf16[1,6,8,3,1536]{4,2,3,1,0:T(8,128)(2,1)S(1)}, bf16[1,6,8,3,1536]{4,2,3,1,0:T(8,128)(2,1)}, u32[]{:S(2)}) copy-start(bf16[1,6,8,3,1536]{4,2,3,1,0:T(8,128)(2,1)} %param.9) | copy-start | bytes 1327108
  16.8 30.1 %copy-start.3 = (bf16[1,6,8,3,1536]{4,2,3,1,0:T(8,128)(2,1)S(1)}, bf16[1,6,8,3,1536]{4,2,3,1,0:T(8,128)(2,1)}, u32[]{:S(2)}) copy-start(bf16[1,6,8,3,1536]{4,2,3,1,0:T(8,128)(2,1)} %param.12) | copy-start | bytes 1327108
  16.8 30.0 %copy-start.4 = (s32[144,1]{1,0:T(8,128)S(1)}, s32[144,1]{1,0:T(8,128)}, u32[]{:S(2)}) copy-start(s32[144,1]{1,0:T(8,128)} %constant.7.clone.slot_col_ref) | copy-start | bytes 1732
  16.8 30.0 %copy-start.5 = (s32[1,1296]{1,0:T(1,128)S(1)}, s32[1,1296]{1,0:T(1,128)}, u32[]{:S(2)}) copy-start(s32[1,1296]{1,0:T(1,128)} %constant.6.clone.slot_row_ref) | copy-start | bytes 15556
  16.8 30.0 %copy-start.6 = (s32[1,8,4]{1,2,0:T(4,128)S(1)}, s32[1,8,4]{1,2,0:T(4,128)}, u32[]{:S(2)}) copy-start(s32[1,8,4]{1,2,0:T(4,128)} %param.13) | copy-start | bytes 388
  16.8 30.0 %copy-start.7 = (f32[12]{0:T(128)S(1)}, f32[12]{0:T(128)}, u32[]{:S(2)}) copy-start(f32[12]{0:T(128)} %sharpness_ref.3) | copy-start | bytes 148
  17.9 14.4 %collective-permute-start.11 = (bf16[432,768]{1,0:T(8,128)(2,1)S(1)}, bf16[432,768]{1,0:T(8,128)(2,1)S(1)}, u32[]{:S(2)}, u32[]{:S(2)}) collective-permute-start(bf16[432,768]{1,0:T(8,128)(2,1)S(1)} %get-tuple-element.37.refs_3_), channel_id=1, source_target_pairs={{4,8},{8,4},{12,16},{16,12},{20,24},{24,20},{5,9},{9,5},{13,17},{1... | collective-permute-start | bytes 1990664 | tf_op jit(solution)/shard_map/ppermute | solution.py:18
  18.7 23.7 %collective-permute-start.10 = (bf16[432,768]{1,0:T(8,128)(2,1)S(1)}, bf16[432,768]{1,0:T(8,128)(2,1)S(1)}, u32[]{:S(2)}, u32[]{:S(2)}) collective-permute-start(bf16[432,768]{1,0:T(8,128)(2,1)S(1)} %get-tuple-element.37.refs_3_), channel_id=1, source_target_pairs={{0,4},{4,0},{8,12},{12,8},{16,20},{20,16},{24,28},{28,24},{1,5},{5... | collective-permute-start | bytes 1990664 | tf_op jit(solution)/shard_map/ppermute | solution.py:18
  27.0 17.7 %collective-permute-start.9 = (bf16[432,768]{1,0:T(8,128)(2,1)S(1)}, bf16[432,768]{1,0:T(8,128)(2,1)S(1)}, u32[]{:S(2)}, u32[]{:S(2)}) collective-permute-start(bf16[432,768]{1,0:T(8,128)(2,1)S(1)} %get-tuple-element.36.refs_0_), channel_id=1, source_target_pairs={{1,2},{2,1},{5,6},{6,5},{9,10},{10,9},{13,14},{14,13},{17,18},{18,... | collective-permute-start | bytes 1990664 | tf_op jit(solution)/shard_map/ppermute | solution.py:18
  29.3 17.4 %collective-permute-start.8 = (bf16[432,768]{1,0:T(8,128)(2,1)S(1)}, bf16[432,768]{1,0:T(8,128)(2,1)S(1)}, u32[]{:S(2)}, u32[]{:S(2)}) collective-permute-start(bf16[432,768]{1,0:T(8,128)(2,1)S(1)} %get-tuple-element.36.refs_0_), channel_id=1, source_target_pairs={{0,1},{1,0},{2,3},{3,2},{4,5},{5,4},{6,7},{7,6},{8,9},{9,8},{10,11... | collective-permute-start | bytes 1990664 | tf_op jit(solution)/shard_map/ppermute | solution.py:18
  31.6 24.0 %collective-permute-start.7 = (bf16[432,768]{1,0:T(8,128)(2,1)S(1)}, bf16[432,768]{1,0:T(8,128)(2,1)S(1)}, u32[]{:S(2)}, u32[]{:S(2)}) collective-permute-start(bf16[432,768]{1,0:T(8,128)(2,1)S(1)} %get-tuple-element.35.refs_3_), channel_id=1, source_target_pairs={{4,8},{8,4},{12,16},{16,12},{20,24},{24,20},{5,9},{9,5},{13,17},{1... | collective-permute-start | bytes 1990664 | tf_op jit(solution)/shard_map/ppermute | solution.py:18
  32.3 23.2 %collective-permute-start.6 = (bf16[432,768]{1,0:T(8,128)(2,1)S(1)}, bf16[432,768]{1,0:T(8,128)(2,1)S(1)}, u32[]{:S(2)}, u32[]{:S(2)}) collective-permute-start(bf16[432,768]{1,0:T(8,128)(2,1)S(1)} %get-tuple-element.35.refs_3_), channel_id=1, source_target_pairs={{0,4},{4,0},{8,12},{12,8},{16,20},{20,16},{24,28},{28,24},{1,5},{5... | collective-permute-start | bytes 1990664 | tf_op jit(solution)/shard_map/ppermute | solution.py:18
  42.4 16.0 %collective-permute-start.3 = (bf16[432,768]{1,0:T(8,128)(2,1)S(1)}, bf16[432,768]{1,0:T(8,128)(2,1)S(1)}, u32[]{:S(2)}, u32[]{:S(2)}) collective-permute-start(bf16[432,768]{1,0:T(8,128)(2,1)S(1)} %get-tuple-element.34.refs_0_), channel_id=1, source_target_pairs={{1,2},{2,1},{5,6},{6,5},{9,10},{10,9},{13,14},{14,13},{17,18},{18,... | collective-permute-start | bytes 1990664 | tf_op jit(solution)/shard_map/ppermute | solution.py:18
  44.7 15.7 %collective-permute-start.2 = (bf16[432,768]{1,0:T(8,128)(2,1)S(1)}, bf16[432,768]{1,0:T(8,128)(2,1)S(1)}, u32[]{:S(2)}, u32[]{:S(2)}) collective-permute-start(bf16[432,768]{1,0:T(8,128)(2,1)S(1)} %get-tuple-element.34.refs_0_), channel_id=1, source_target_pairs={{0,1},{1,0},{2,3},{3,2},{4,5},{5,4},{6,7},{7,6},{8,9},{9,8},{10,11... | collective-permute-start | bytes 1990664 | tf_op jit(solution)/shard_map/ppermute | solution.py:18
  69.1 35.8 %collective-permute-start.12 = (bf16[432,1536]{1,0:T(8,128)(2,1)}, bf16[432,1536]{1,0:T(8,128)(2,1)}, u32[]{:S(2)}, u32[]{:S(2)}) collective-permute-start(bf16[432,1536]{1,0:T(8,128)(2,1)} %get-tuple-element.49), channel_id=1, source_target_pairs={{0,1},{1,0},{2,3},{3,2},{4,5},{5,4},{6,7},{7,6},{8,9},{9,8},{10,11... | collective-permute-start | bytes 3981320 | tf_op jit(solution)/shard_map/ppermute | solution.py:18
  71.3 33.5 %collective-permute-start.13 = (bf16[432,1536]{1,0:T(8,128)(2,1)}, bf16[432,1536]{1,0:T(8,128)(2,1)}, u32[]{:S(2)}, u32[]{:S(2)}) collective-permute-start(bf16[432,1536]{1,0:T(8,128)(2,1)} %get-tuple-element.50), channel_id=1, source_target_pairs={{1,2},{2,1},{5,6},{6,5},{9,10},{10,9},{13,14},{14,13},{17,18},{18,... | collective-permute-start | bytes 3981320 | tf_op jit(solution)/shard_map/ppermute | solution.py:18
  74.9 36.4 %collective-permute-start.16 = (bf16[432,1536]{1,0:T(8,128)(2,1)}, bf16[432,1536]{1,0:T(8,128)(2,1)}, u32[]{:S(2)}, u32[]{:S(2)}) collective-permute-start(bf16[432,1536]{1,0:T(8,128)(2,1)} %get-tuple-element.56), channel_id=1, source_target_pairs={{0,4},{4,0},{8,12},{12,8},{16,20},{20,16},{24,28},{28,24},{1,5},{5... | collective-permute-start | bytes 3981320 | tf_op jit(solution)/shard_map/ppermute | solution.py:18
  77.4 34.0 %collective-permute-start.17 = (bf16[432,1536]{1,0:T(8,128)(2,1)}, bf16[432,1536]{1,0:T(8,128)(2,1)}, u32[]{:S(2)}, u32[]{:S(2)}) collective-permute-start(bf16[432,1536]{1,0:T(8,128)(2,1)} %get-tuple-element.57), channel_id=1, source_target_pairs={{4,8},{8,4},{12,16},{16,12},{20,24},{24,20},{5,9},{9,5},{13,17},{1... | collective-permute-start | bytes 3981320 | tf_op jit(solution)/shard_map/ppermute | solution.py:18
  107.7 24.2 %collective-permute-start.14 = (bf16[144,1536]{1,0:T(8,128)(2,1)}, bf16[144,1536]{1,0:T(8,128)(2,1)}, u32[]{:S(2)}, u32[]{:S(2)}) collective-permute-start(bf16[144,1536]{1,0:T(8,128)(2,1)} %get-tuple-element.52), channel_id=1, source_target_pairs={{0,4},{4,0},{8,12},{12,8},{16,20},{20,16},{24,28},{28,24},{1,5},{5... | collective-permute-start | bytes 1327112 | tf_op jit(solution)/shard_map/ppermute | solution.py:18
  109.9 21.9 %collective-permute-start.15 = (bf16[144,1536]{1,0:T(8,128)(2,1)}, bf16[144,1536]{1,0:T(8,128)(2,1)}, u32[]{:S(2)}, u32[]{:S(2)}) collective-permute-start(bf16[144,1536]{1,0:T(8,128)(2,1)} %get-tuple-element.53), channel_id=1, source_target_pairs={{4,8},{8,4},{12,16},{16,12},{20,24},{24,20},{5,9},{9,5},{13,17},{1... | collective-permute-start | bytes 1327112 | tf_op jit(solution)/shard_map/ppermute | solution.py:18
  114.2 25.3 %collective-permute-start.18 = (bf16[144,1536]{1,0:T(8,128)(2,1)}, bf16[144,1536]{1,0:T(8,128)(2,1)S(1)}, u32[]{:S(2)}, u32[]{:S(2)}) collective-permute-start(bf16[144,1536]{1,0:T(8,128)(2,1)} %get-tuple-element.60), channel_id=1, source_target_pairs={{0,1},{1,0},{2,3},{3,2},{4,5},{5,4},{6,7},{7,6},{8,9},{9,8},{10,11... | collective-permute-start | bytes 1327112 | tf_op jit(solution)/shard_map/ppermute | solution.py:18
  119.0 20.5 %collective-permute-start.19 = (bf16[144,1536]{1,0:T(8,128)(2,1)}, bf16[144,1536]{1,0:T(8,128)(2,1)S(1)}, u32[]{:S(2)}, u32[]{:S(2)}) collective-permute-start(bf16[144,1536]{1,0:T(8,128)(2,1)} %get-tuple-element.61), channel_id=1, source_target_pairs={{1,2},{2,1},{5,6},{6,5},{9,10},{10,9},{13,14},{14,13},{17,18},{18,... | collective-permute-start | bytes 1327112 | tf_op jit(solution)/shard_map/ppermute | solution.py:18
  122.5 17.1 %all-to-all-start.1 = ((f32[8,1,12]{2,1,0:T(1,128)}), f32[8,1,12]{2,1,0:T(1,128)S(1)}, u32[]{:S(2)}, u32[]{:S(2)}) async-start(f32[8,1,12]{2,1,0:T(1,128)} %get-tuple-element.58), calls=%async_computation.1 | async-start | bytes 8192 | tf_op jit(solution)/shard_map/all_to_all | solution.py:22

commit v4 on v3

--- a/solution.py
+++ b/solution.py
@@ -106,7 +106,7 @@
 
 
 def score_gradients(multiplier, bias_ref, valid_ref, logits_ref, grad_weight_ref, low_ref, scaled_ref):
-    rows_at_once = 16
+    rows_at_once = 48
     for first in range(0, logits_ref.shape[0], rows_at_once):
         rows = slice(first, first + rows_at_once)
         logits = logits_ref[rows] * multiplier + bias_ref[...]

time: 141 us -> 141 us (level)
  no operation moved by 1% of the time
where the time goes in v4:
time: 141 us
  starting transfers between devices  73.6 us (52%)
  Pallas kernels  26.3 us (19%)
  blocking collectives  25.5 us (18%)
  waiting for transfers between devices  11.8 us (8%)
  local copies, waits for them, and re-layouts  2.1 us (1%)
    ppermute x20, starting transfers between devices, exchanged(): lax.ppermute(block, axis, [(i, j) for i, j in enumerate(partner) if 0 <=...  64.2 us
    all_to_all x1, blocking collectives, swapped(): return lax.all_to_all(rows, axes, 0, 0)  25.5 us
    pallas_call x2, Pallas kernels, attention(): pl.pallas_call(functools.partial(attention_body, opening, tile_len, toget...  17.5 us
    all_to_all x1, starting transfers between devices, swapped(): return lax.all_to_all(rows, axes, 0, 0)  9.39 us
    ppermute x20, waiting for transfers between devices, exchanged(): lax.ppermute(block, axis, [(i, j) for i, j in enumerate(partner) if 0 <=...  6.21 us
    pallas_call x2, Pallas kernels, summed_parts(): pl.pallas_call(functools.partial(sum_body, rows is not None), in_specs=[v...  5.63 us
    all_to_all x1, waiting for transfers between devices, swapped(): return lax.all_to_all(rows, axes, 0, 0)  5.61 us
    pallas_call x2, Pallas kernels, final_sum(): pl.pallas_call(functools.partial(final_body, rows is not None), in_specs=...  2.94 us
  transfers between devices with their start and end apart: 21, of which 5 were waited for; matrix products, arithmetic and copies ran while one was open for 0% of the time, Pallas kernels for 12%

profile of v4, /device:TPU:8, one launch (start us, length us, event | category | flops | bytes accessed | tf_op | source)
XLA Modules:
  0.0 140.5 jit_solution(5530126462236781997)
XLA Ops:
  0.6 3.5 %collective-permute-start.5 = (bf16[144,1536]{1,0:T(8,128)(2,1)}, bf16[144,1536]{1,0:T(8,128)(2,1)S(1)}, u32[]{:S(2)}, u32[]{:S(2)}) collective-permute-start(bf16[144,1536]{1,0:T(8,128)(2,1)} %bitcast.45), channel_id=1, source_target_pairs={{1,2},{2,1},{5,6},{6,5},{9,10},{10,9},{13,14},{14,13},{17,18},{18,... | collective-permute-start | bytes 1327112 | tf_op jit(solution)/shard_map/ppermute | solution.py:18
  4.1 4.9 %collective-permute-start.4 = (bf16[144,1536]{1,0:T(8,128)(2,1)}, bf16[144,1536]{1,0:T(8,128)(2,1)S(1)}, u32[]{:S(2)}, u32[]{:S(2)}) collective-permute-start(bf16[144,1536]{1,0:T(8,128)(2,1)} %bitcast.46), channel_id=1, source_target_pairs={{0,1},{1,0},{2,3},{3,2},{4,5},{5,4},{6,7},{7,6},{8,9},{9,8},{10,11... | collective-permute-start | bytes 1327112 | tf_op jit(solution)/shard_map/ppermute | solution.py:18
  9.1 0.7 collective-permute-start.1
  9.8 4.9 %collective-permute-start = (bf16[144,1536]{1,0:T(8,128)(2,1)}, bf16[144,1536]{1,0:T(8,128)(2,1)S(1)}, u32[]{:S(2)}, u32[]{:S(2)}) collective-permute-start(bf16[144,1536]{1,0:T(8,128)(2,1)} %bitcast.49), channel_id=1, source_target_pairs={{0,4},{4,0},{8,12},{12,8},{16,20},{20,16},{24,28},{28,24},{1,5},{5... | collective-permute-start | bytes 1327112 | tf_op jit(solution)/shard_map/ppermute | solution.py:18
  14.6 0.0 copy-start.1
  14.6 1.0 copy-done.1
  15.7 0.0 copy-start
  15.7 1.0 copy-done
  16.7 0.0 copy-start.8
  16.8 0.0 copy-start.2
  16.8 0.0 copy-start.3
  16.8 0.0 copy-start.4
  16.8 0.0 copy-start.5
  16.8 0.0 copy-start.6
  16.8 0.0 copy-start.7
  16.8 0.0 collective-permute-done.5.refs_2_
  16.8 1.0 collective-permute-done.4.refs_1_
  17.9 0.1 shard_map.123
  17.9 0.7 collective-permute-start.11
  18.7 8.2 %collective-permute-start.10 = (bf16[432,768]{1,0:T(8,128)(2,1)S(1)}, bf16[432,768]{1,0:T(8,128)(2,1)S(1)}, u32[]{:S(2)}, u32[]{:S(2)}) collective-permute-start(bf16[432,768]{1,0:T(8,128)(2,1)S(1)} %get-tuple-element.37.refs_3_), channel_id=1, source_target_pairs={{0,4},{4,0},{8,12},{12,8},{16,20},{20,16},{24,28},{28,24},{1,5},{5... | collective-permute-start | bytes 1990664 | tf_op jit(solution)/shard_map/ppermute | solution.py:18
  26.9 0.0 collective-permute-done.1.refs_2_
  26.9 0.0 collective-permute-done.refs_1_
  26.9 0.1 shard_map.121
  27.0 2.4 %collective-permute-start.9 = (bf16[432,768]{1,0:T(8,128)(2,1)S(1)}, bf16[432,768]{1,0:T(8,128)(2,1)S(1)}, u32[]{:S(2)}, u32[]{:S(2)}) collective-permute-start(bf16[432,768]{1,0:T(8,128)(2,1)S(1)} %get-tuple-element.36.refs_0_), channel_id=1, source_target_pairs={{1,2},{2,1},{5,6},{6,5},{9,10},{10,9},{13,14},{14,13},{17,18},{18,... | collective-permute-start | bytes 1990664 | tf_op jit(solution)/shard_map/ppermute | solution.py:18
  29.3 2.3 %collective-permute-start.8 = (bf16[432,768]{1,0:T(8,128)(2,1)S(1)}, bf16[432,768]{1,0:T(8,128)(2,1)S(1)}, u32[]{:S(2)}, u32[]{:S(2)}) collective-permute-start(bf16[432,768]{1,0:T(8,128)(2,1)S(1)} %get-tuple-element.36.refs_0_), channel_id=1, source_target_pairs={{0,1},{1,0},{2,3},{3,2},{4,5},{5,4},{6,7},{7,6},{8,9},{9,8},{10,11... | collective-permute-start | bytes 1990664 | tf_op jit(solution)/shard_map/ppermute | solution.py:18
  31.6 0.7 collective-permute-start.7
  32.3 0.0 collective-permute-done.11.refs_5_
  32.3 10.0 %collective-permute-start.6 = (bf16[432,768]{1,0:T(8,128)(2,1)S(1)}, bf16[432,768]{1,0:T(8,128)(2,1)S(1)}, u32[]{:S(2)}, u32[]{:S(2)}) collective-permute-start(bf16[432,768]{1,0:T(8,128)(2,1)S(1)} %get-tuple-element.35.refs_3_), channel_id=1, source_target_pairs={{0,4},{4,0},{8,12},{12,8},{16,20},{20,16},{24,28},{28,24},{1,5},{5... | collective-permute-start | bytes 1990664 | tf_op jit(solution)/shard_map/ppermute | solution.py:18
  42.4 0.0 collective-permute-done.10.refs_4_
  42.4 1.9 %collective-permute-start.3 = (bf16[432,768]{1,0:T(8,128)(2,1)S(1)}, bf16[432,768]{1,0:T(8,128)(2,1)S(1)}, u32[]{:S(2)}, u32[]{:S(2)}) collective-permute-start(bf16[432,768]{1,0:T(8,128)(2,1)S(1)} %get-tuple-element.34.refs_0_), channel_id=1, source_target_pairs={{1,2},{2,1},{5,6},{6,5},{9,10},{10,9},{13,14},{14,13},{17,18},{18,... | collective-permute-start | bytes 1990664 | tf_op jit(solution)/shard_map/ppermute | solution.py:18
  44.3 0.4 collective-permute-done.9.refs_2_
  44.7 2.0 %collective-permute-start.2 = (bf16[432,768]{1,0:T(8,128)(2,1)S(1)}, bf16[432,768]{1,0:T(8,128)(2,1)S(1)}, u32[]{:S(2)}, u32[]{:S(2)}) collective-permute-start(bf16[432,768]{1,0:T(8,128)(2,1)S(1)} %get-tuple-element.34.refs_0_), channel_id=1, source_target_pairs={{0,1},{1,0},{2,3},{3,2},{4,5},{5,4},{6,7},{7,6},{8,9},{9,8},{10,11... | collective-permute-start | bytes 1990664 | tf_op jit(solution)/shard_map/ppermute | solution.py:18
  46.8 0.0 copy-done.8
  46.8 0.0 collective-permute-done.8.refs_1_
  46.9 8.8 %shard_map.124 = (bf16[144,1536]{1,0:T(8,128)(2,1)}, f32[12,1,128]{2,1,0:T(1,128)S(1)}, bf16[432,1536]{1,0:T(8,128)(2,1)S(1)}, bf16[432,1536]{1,0:T(8,128)(2,1)}...) custom-call(f32[12]{0:T(128)S(1)} %copy-done.7, ...), custom_call_target="tpu_custom_call" | custom-call | flops 1433272320 | bytes 7962624 | tf_op jit(solution)/shard_map/pallas_call | solution.py:226
  55.7 0.0 collective-permute-done.7.refs_5_
  55.7 0.0 collective-permute-done.6.refs_4_
  55.7 2.7 %collective-permute-done.3.refs_2_ = bf16[432,768]{1,0:T(8,128)(2,1)S(1)} collective-permute-done((bf16[432,768]{1,0:T(8,128)(2,1)S(1)}, bf16[432,768]{1,0:T(8,128)(2,1)S(1)}, u32[]{:S(2)}, u32[]{:S(2)}) %collective-permute-start.3) | collective-permute-done | bytes 663584 | tf_op jit(solution)/shard_map/ppermute | solution.py:18
  58.3 2.1 %collective-permute-done.2.refs_1_ = bf16[432,768]{1,0:T(8,128)(2,1)S(1)} collective-permute-done((bf16[432,768]{1,0:T(8,128)(2,1)S(1)}, bf16[432,768]{1,0:T(8,128)(2,1)S(1)}, u32[]{:S(2)}, u32[]{:S(2)}) %collective-permute-start.2) | collective-permute-done | bytes 663584 | tf_op jit(solution)/shard_map/ppermute | solution.py:18
  60.4 8.7 %shard_map.125 = (bf16[144,1536]{1,0:T(8,128)(2,1)}, f32[12,1,128]{2,1,0:T(1,128)S(1)}, bf16[432,1536]{1,0:T(8,128)(2,1)S(1)}, bf16[432,1536]{1,0:T(8,128)(2,1)}...) custom-call(f32[12]{0:T(128)S(1)} %copy-done.7, ...), custom_call_target="tpu_custom_call", output_to_operand_aliasing={{0}: (13, {}), {1}: (14, {}), {2}: (15, {}), {3}: (16, {}),... | custom-call | flops 1433272320 | bytes 7962624 | tf_op jit(solution)/shard_map/pallas_call | solution.py:226
  69.1 2.3 %collective-permute-start.12 = (bf16[432,1536]{1,0:T(8,128)(2,1)}, bf16[432,1536]{1,0:T(8,128)(2,1)}, u32[]{:S(2)}, u32[]{:S(2)}) collective-permute-start(bf16[432,1536]{1,0:T(8,128)(2,1)} %get-tuple-element.49), channel_id=1, source_target_pairs={{0,1},{1,0},{2,3},{3,2},{4,5},{5,4},{6,7},{7,6},{8,9},{9,8},{10,11... | collective-permute-start | bytes 3981320 | tf_op jit(solution)/shard_map/ppermute | solution.py:18
  71.4 3.4 %collective-permute-start.13 = (bf16[432,1536]{1,0:T(8,128)(2,1)}, bf16[432,1536]{1,0:T(8,128)(2,1)}, u32[]{:S(2)}, u32[]{:S(2)}) collective-permute-start(bf16[432,1536]{1,0:T(8,128)(2,1)} %get-tuple-element.50), channel_id=1, source_target_pairs={{1,2},{2,1},{5,6},{6,5},{9,10},{10,9},{13,14},{14,13},{17,18},{18,... | collective-permute-start | bytes 3981320 | tf_op jit(solution)/shard_map/ppermute | solution.py:18
  74.8 2.6 %collective-permute-start.16 = (bf16[432,1536]{1,0:T(8,128)(2,1)}, bf16[432,1536]{1,0:T(8,128)(2,1)}, u32[]{:S(2)}, u32[]{:S(2)}) collective-permute-start(bf16[432,1536]{1,0:T(8,128)(2,1)} %get-tuple-element.56), channel_id=1, source_target_pairs={{0,4},{4,0},{8,12},{12,8},{16,20},{20,16},{24,28},{28,24},{1,5},{5... | collective-permute-start | bytes 3981320 | tf_op jit(solution)/shard_map/ppermute | solution.py:18
  77.5 1.7 %collective-permute-start.17 = (bf16[432,1536]{1,0:T(8,128)(2,1)}, bf16[432,1536]{1,0:T(8,128)(2,1)}, u32[]{:S(2)}, u32[]{:S(2)}) collective-permute-start(bf16[432,1536]{1,0:T(8,128)(2,1)} %get-tuple-element.57), channel_id=1, source_target_pairs={{4,8},{8,4},{12,16},{16,12},{20,24},{24,20},{5,9},{9,5},{13,17},{1... | collective-permute-start | bytes 3981320 | tf_op jit(solution)/shard_map/ppermute | solution.py:18
  79.2 0.2 reduce_sum.9
  79.4 25.5 %all_to_all.10.refs_0_ = f32[64,1,12]{2,1,0:T(1,128)S(1)} all-to-all(f32[64,1,12]{2,1,0:T(1,128)S(1)} %broadcast_in_dim.13), channel_id=1, replica_groups=mesh['dp'=16,'tm'=8,'height'=4] {'dp','height'}, dimensions={0} | all-to-all | bytes 6144 | tf_op jit(solution)/shard_map/all_to_all | solution.py:22
  104.9 0.0 collective-permute-done.12.refs_2_
  104.9 0.0 collective-permute-done.13.refs_3_
  104.9 2.8 %shard_map.126 = (f32[1,1,12]{2,1,0:T(1,128)S(1)}, f32[144,1536]{1,0:T(8,128)S(1)}, bf16[144,1536]{1,0:T(8,128)(2,1)}, bf16[144,1536]{1,0:T(8,128)(2,1)}) custom-call(f32[64,1,12]{2,1,0:T(1,128)S(1)} %all_to_all.10.refs_0_, bf16[432,1536]{1,0:T(8,128)(2,1)S(1)} %get-tuple-element.48.refs_1_, bf16[432,1536]{1,0:T(8,128)(2,1)} %collective-permute-done.12.refs_2_, ...), custom_call_target="tpu_custom_call" | custom-call | tf_op jit(solution)/shard_map/pallas_call | solution.py:56
  107.7 2.3 %collective-permute-start.14 = (bf16[144,1536]{1,0:T(8,128)(2,1)}, bf16[144,1536]{1,0:T(8,128)(2,1)}, u32[]{:S(2)}, u32[]{:S(2)}) collective-permute-start(bf16[144,1536]{1,0:T(8,128)(2,1)} %get-tuple-element.52), channel_id=1, source_target_pairs={{0,4},{4,0},{8,12},{12,8},{16,20},{20,16},{24,28},{28,24},{1,5},{5... | collective-permute-start | bytes 1327112 | tf_op jit(solution)/shard_map/ppermute | solution.py:18
  110.0 1.4 %collective-permute-start.15 = (bf16[144,1536]{1,0:T(8,128)(2,1)}, bf16[144,1536]{1,0:T(8,128)(2,1)}, u32[]{:S(2)}, u32[]{:S(2)}) collective-permute-start(bf16[144,1536]{1,0:T(8,128)(2,1)} %get-tuple-element.53), channel_id=1, source_target_pairs={{4,8},{8,4},{12,16},{16,12},{20,24},{24,20},{5,9},{9,5},{13,17},{1... | collective-permute-start | bytes 1327112 | tf_op jit(solution)/shard_map/ppermute | solution.py:18
  111.5 0.0 collective-permute-done.16.refs_2_
  111.5 0.0 collective-permute-done.17.refs_3_
  111.5 2.8 %shard_map.128 = (f32[8,1,12]{2,1,0:T(1,128)}, f32[144,1536]{1,0:T(8,128)S(1)}, bf16[144,1536]{1,0:T(8,128)(2,1)}, bf16[144,1536]{1,0:T(8,128)(2,1)}) custom-call(f32[1,1,12]{2,1,0:T(1,128)S(1)} %get-tuple-element.54.refs_0_, bf16[432,1536]{1,0:T(8,128)(2,1)S(1)} %get-tuple-element.55.refs_1_, bf16[432,1536]{1,0:T(8,128)(2,1)} %collective-permute-done.16.refs_2_, ...), custom_call_target="tpu_custom_call" | custom-call | tf_op jit(solution)/shard_map/pallas_call | solution.py:56
  114.3 4.8 %collective-permute-start.18 = (bf16[144,1536]{1,0:T(8,128)(2,1)}, bf16[144,1536]{1,0:T(8,128)(2,1)S(1)}, u32[]{:S(2)}, u32[]{:S(2)}) collective-permute-start(bf16[144,1536]{1,0:T(8,128)(2,1)} %get-tuple-element.60), channel_id=1, source_target_pairs={{0,1},{1,0},{2,3},{3,2},{4,5},{5,4},{6,7},{7,6},{8,9},{9,8},{10,11... | collective-permute-start | bytes 1327112 | tf_op jit(solution)/shard_map/ppermute | solution.py:18
  119.1 3.4 %collective-permute-start.19 = (bf16[144,1536]{1,0:T(8,128)(2,1)}, bf16[144,1536]{1,0:T(8,128)(2,1)S(1)}, u32[]{:S(2)}, u32[]{:S(2)}) collective-permute-start(bf16[144,1536]{1,0:T(8,128)(2,1)} %get-tuple-element.61), channel_id=1, source_target_pairs={{1,2},{2,1},{5,6},{6,5},{9,10},{10,9},{13,14},{14,13},{17,18},{18,... | collective-permute-start | bytes 1327112 | tf_op jit(solution)/shard_map/ppermute | solution.py:18
  122.5 9.4 %all-to-all-start.1 = ((f32[8,1,12]{2,1,0:T(1,128)}), f32[8,1,12]{2,1,0:T(1,128)S(1)}, u32[]{:S(2)}, u32[]{:S(2)}) async-start(f32[8,1,12]{2,1,0:T(1,128)} %get-tuple-element.58), calls=%async_computation.1 | async-start | bytes 8192 | tf_op jit(solution)/shard_map/all_to_all | solution.py:22
  131.9 0.0 collective-permute-done.14.refs_1_
  131.9 0.0 collective-permute-done.15.refs_2_
  131.9 2.0 %shard_map.127 = bf16[144,1536]{1,0:T(8,128)(2,1)} custom-call(f32[144,1536]{1,0:T(8,128)S(1)} %get-tuple-element.51.refs_0_, bf16[144,1536]{1,0:T(8,128)(2,1)} %collective-permute-done.14.refs_1_, bf16[144,1536]{1,0:T(8,128)(2,1)} %collective-permute-done.15.refs_2_), custom_call_target="tpu_custom_call" | custom-call | tf_op jit(solution)/shard_map/pallas_call | solution.py:82
  134.0 5.6 %all-to-all-done.1.refs_0_ = f32[8,1,12]{2,1,0:T(1,128)S(1)} async-done(((f32[8,1,12]{2,1,0:T(1,128)}), f32[8,1,12]{2,1,0:T(1,128)S(1)}, u32[]{:S(2)}, u32[]{:S(2)}) %all-to-all-start.1) | async-done | bytes 416 | tf_op jit(solution)/shard_map/all_to_all | solution.py:22
  139.6 0.0 collective-permute-done.18.refs_2_
  139.6 0.0 collective-permute-done.19.refs_3_
  139.6 0.9 shard_map.129
  (11 shorter events, 0.1 us)
Async XLA Ops:
  0.6 16.2 %collective-permute-start.5 = (bf16[144,1536]{1,0:T(8,128)(2,1)}, bf16[144,1536]{1,0:T(8,128)(2,1)S(1)}, u32[]{:S(2)}, u32[]{:S(2)}) collective-permute-start(bf16[144,1536]{1,0:T(8,128)(2,1)} %bitcast.45), channel_id=1, source_target_pairs={{1,2},{2,1},{5,6},{6,5},{9,10},{10,9},{13,14},{14,13},{17,18},{18,... | collective-permute-start | bytes 1327112 | tf_op jit(solution)/shard_map/ppermute | solution.py:18
  4.1 13.7 %collective-permute-start.4 = (bf16[144,1536]{1,0:T(8,128)(2,1)}, bf16[144,1536]{1,0:T(8,128)(2,1)S(1)}, u32[]{:S(2)}, u32[]{:S(2)}) collective-permute-start(bf16[144,1536]{1,0:T(8,128)(2,1)} %bitcast.46), channel_id=1, source_target_pairs={{0,1},{1,0},{2,3},{3,2},{4,5},{5,4},{6,7},{7,6},{8,9},{9,8},{10,11... | collective-permute-start | bytes 1327112 | tf_op jit(solution)/shard_map/ppermute | solution.py:18
  9.1 17.8 %collective-permute-start.1 = (bf16[144,1536]{1,0:T(8,128)(2,1)}, bf16[144,1536]{1,0:T(8,128)(2,1)S(1)}, u32[]{:S(2)}, u32[]{:S(2)}) collective-permute-start(bf16[144,1536]{1,0:T(8,128)(2,1)} %bitcast.48), channel_id=1, source_target_pairs={{4,8},{8,4},{12,16},{16,12},{20,24},{24,20},{5,9},{9,5},{13,17},{1... | collective-permute-start | bytes 1327112 | tf_op jit(solution)/shard_map/ppermute | solution.py:18
  9.8 17.1 %collective-permute-start = (bf16[144,1536]{1,0:T(8,128)(2,1)}, bf16[144,1536]{1,0:T(8,128)(2,1)S(1)}, u32[]{:S(2)}, u32[]{:S(2)}) collective-permute-start(bf16[144,1536]{1,0:T(8,128)(2,1)} %bitcast.49), channel_id=1, source_target_pairs={{0,4},{4,0},{8,12},{12,8},{16,20},{20,16},{24,28},{28,24},{1,5},{5... | collective-permute-start | bytes 1327112 | tf_op jit(solution)/shard_map/ppermute | solution.py:18
  14.6 1.0 copy-start.1
  15.7 1.0 copy-start
  16.7 30.0 %copy-start.8 = (s32[1,8,4,2]{1,3,2,0:T(2,128)S(1)}, s32[1,8,4,2]{1,3,2,0:T(2,128)}, u32[]{:S(2)}) copy-start(s32[1,8,4,2]{1,3,2,0:T(2,128)} %param.14) | copy-start | bytes 772
  16.8 30.1 %copy-start.2 = (bf16[1,6,8,3,1536]{4,2,3,1,0:T(8,128)(2,1)S(1)}, bf16[1,6,8,3,1536]{4,2,3,1,0:T(8,128)(2,1)}, u32[]{:S(2)}) copy-start(bf16[1,6,8,3,1536]{4,2,3,1,0:T(8,128)(2,1)} %param.9) | copy-start | bytes 1327108
  16.8 30.1 %copy-start.3 = (bf16[1,6,8,3,1536]{4,2,3,1,0:T(8,128)(2,1)S(1)}, bf16[1,6,8,3,1536]{4,2,3,1,0:T(8,128)(2,1)}, u32[]{:S(2)}) copy-start(bf16[1,6,8,3,1536]{4,2,3,1,0:T(8,128)(2,1)} %param.12) | copy-start | bytes 1327108
  16.8 30.0 %copy-start.4 = (s32[144,1]{1,0:T(8,128)S(1)}, s32[144,1]{1,0:T(8,128)}, u32[]{:S(2)}) copy-start(s32[144,1]{1,0:T(8,128)} %constant.7.clone.slot_col_ref) | copy-start | bytes 1732
  16.8 30.0 %copy-start.5 = (s32[1,1296]{1,0:T(1,128)S(1)}, s32[1,1296]{1,0:T(1,128)}, u32[]{:S(2)}) copy-start(s32[1,1296]{1,0:T(1,128)} %constant.6.clone.slot_row_ref) | copy-start | bytes 15556
  16.8 30.0 %copy-start.6 = (s32[1,8,4]{1,2,0:T(4,128)S(1)}, s32[1,8,4]{1,2,0:T(4,128)}, u32[]{:S(2)}) copy-start(s32[1,8,4]{1,2,0:T(4,128)} %param.13) | copy-start | bytes 388
  16.8 30.0 %copy-start.7 = (f32[12]{0:T(128)S(1)}, f32[12]{0:T(128)}, u32[]{:S(2)}) copy-start(f32[12]{0:T(128)} %sharpness_ref.3) | copy-start | bytes 148
  17.9 14.4 %collective-permute-start.11 = (bf16[432,768]{1,0:T(8,128)(2,1)S(1)}, bf16[432,768]{1,0:T(8,128)(2,1)S(1)}, u32[]{:S(2)}, u32[]{:S(2)}) collective-permute-start(bf16[432,768]{1,0:T(8,128)(2,1)S(1)} %get-tuple-element.37.refs_3_), channel_id=1, source_target_pairs={{4,8},{8,4},{12,16},{16,12},{20,24},{24,20},{5,9},{9,5},{13,17},{1... | collective-permute-start | bytes 1990664 | tf_op jit(solution)/shard_map/ppermute | solution.py:18
  18.7 23.7 %collective-permute-start.10 = (bf16[432,768]{1,0:T(8,128)(2,1)S(1)}, bf16[432,768]{1,0:T(8,128)(2,1)S(1)}, u32[]{:S(2)}, u32[]{:S(2)}) collective-permute-start(bf16[432,768]{1,0:T(8,128)(2,1)S(1)} %get-tuple-element.37.refs_3_), channel_id=1, source_target_pairs={{0,4},{4,0},{8,12},{12,8},{16,20},{20,16},{24,28},{28,24},{1,5},{5... | collective-permute-start | bytes 1990664 | tf_op jit(solution)/shard_map/ppermute | solution.py:18
  27.0 17.7 %collective-permute-start.9 = (bf16[432,768]{1,0:T(8,128)(2,1)S(1)}, bf16[432,768]{1,0:T(8,128)(2,1)S(1)}, u32[]{:S(2)}, u32[]{:S(2)}) collective-permute-start(bf16[432,768]{1,0:T(8,128)(2,1)S(1)} %get-tuple-element.36.refs_0_), channel_id=1, source_target_pairs={{1,2},{2,1},{5,6},{6,5},{9,10},{10,9},{13,14},{14,13},{17,18},{18,... | collective-permute-start | bytes 1990664 | tf_op jit(solution)/shard_map/ppermute | solution.py:18
  29.3 17.4 %collective-permute-start.8 = (bf16[432,768]{1,0:T(8,128)(2,1)S(1)}, bf16[432,768]{1,0:T(8,128)(2,1)S(1)}, u32[]{:S(2)}, u32[]{:S(2)}) collective-permute-start(bf16[432,768]{1,0:T(8,128)(2,1)S(1)} %get-tuple-element.36.refs_0_), channel_id=1, source_target_pairs={{0,1},{1,0},{2,3},{3,2},{4,5},{5,4},{6,7},{7,6},{8,9},{9,8},{10,11... | collective-permute-start | bytes 1990664 | tf_op jit(solution)/shard_map/ppermute | solution.py:18
  31.6 24.0 %collective-permute-start.7 = (bf16[432,768]{1,0:T(8,128)(2,1)S(1)}, bf16[432,768]{1,0:T(8,128)(2,1)S(1)}, u32[]{:S(2)}, u32[]{:S(2)}) collective-permute-start(bf16[432,768]{1,0:T(8,128)(2,1)S(1)} %get-tuple-element.35.refs_3_), channel_id=1, source_target_pairs={{4,8},{8,4},{12,16},{16,12},{20,24},{24,20},{5,9},{9,5},{13,17},{1... | collective-permute-start | bytes 1990664 | tf_op jit(solution)/shard_map/ppermute | solution.py:18
  32.3 23.3 %collective-permute-start.6 = (bf16[432,768]{1,0:T(8,128)(2,1)S(1)}, bf16[432,768]{1,0:T(8,128)(2,1)S(1)}, u32[]{:S(2)}, u32[]{:S(2)}) collective-permute-start(bf16[432,768]{1,0:T(8,128)(2,1)S(1)} %get-tuple-element.35.refs_3_), channel_id=1, source_target_pairs={{0,4},{4,0},{8,12},{12,8},{16,20},{20,16},{24,28},{28,24},{1,5},{5... | collective-permute-start | bytes 1990664 | tf_op jit(solution)/shard_map/ppermute | solution.py:18
  42.4 16.0 %collective-permute-start.3 = (bf16[432,768]{1,0:T(8,128)(2,1)S(1)}, bf16[432,768]{1,0:T(8,128)(2,1)S(1)}, u32[]{:S(2)}, u32[]{:S(2)}) collective-permute-start(bf16[432,768]{1,0:T(8,128)(2,1)S(1)} %get-tuple-element.34.refs_0_), channel_id=1, source_target_pairs={{1,2},{2,1},{5,6},{6,5},{9,10},{10,9},{13,14},{14,13},{17,18},{18,... | collective-permute-start | bytes 1990664 | tf_op jit(solution)/shard_map/ppermute | solution.py:18
  44.7 15.7 %collective-permute-start.2 = (bf16[432,768]{1,0:T(8,128)(2,1)S(1)}, bf16[432,768]{1,0:T(8,128)(2,1)S(1)}, u32[]{:S(2)}, u32[]{:S(2)}) collective-permute-start(bf16[432,768]{1,0:T(8,128)(2,1)S(1)} %get-tuple-element.34.refs_0_), channel_id=1, source_target_pairs={{0,1},{1,0},{2,3},{3,2},{4,5},{5,4},{6,7},{7,6},{8,9},{9,8},{10,11... | collective-permute-start | bytes 1990664 | tf_op jit(solution)/shard_map/ppermute | solution.py:18
  69.1 35.8 %collective-permute-start.12 = (bf16[432,1536]{1,0:T(8,128)(2,1)}, bf16[432,1536]{1,0:T(8,128)(2,1)}, u32[]{:S(2)}, u32[]{:S(2)}) collective-permute-start(bf16[432,1536]{1,0:T(8,128)(2,1)} %get-tuple-element.49), channel_id=1, source_target_pairs={{0,1},{1,0},{2,3},{3,2},{4,5},{5,4},{6,7},{7,6},{8,9},{9,8},{10,11... | collective-permute-start | bytes 3981320 | tf_op jit(solution)/shard_map/ppermute | solution.py:18
  71.4 33.5 %collective-permute-start.13 = (bf16[432,1536]{1,0:T(8,128)(2,1)}, bf16[432,1536]{1,0:T(8,128)(2,1)}, u32[]{:S(2)}, u32[]{:S(2)}) collective-permute-start(bf16[432,1536]{1,0:T(8,128)(2,1)} %get-tuple-element.50), channel_id=1, source_target_pairs={{1,2},{2,1},{5,6},{6,5},{9,10},{10,9},{13,14},{14,13},{17,18},{18,... | collective-permute-start | bytes 3981320 | tf_op jit(solution)/shard_map/ppermute | solution.py:18
  74.8 36.6 %collective-permute-start.16 = (bf16[432,1536]{1,0:T(8,128)(2,1)}, bf16[432,1536]{1,0:T(8,128)(2,1)}, u32[]{:S(2)}, u32[]{:S(2)}) collective-permute-start(bf16[432,1536]{1,0:T(8,128)(2,1)} %get-tuple-element.56), channel_id=1, source_target_pairs={{0,4},{4,0},{8,12},{12,8},{16,20},{20,16},{24,28},{28,24},{1,5},{5... | collective-permute-start | bytes 3981320 | tf_op jit(solution)/shard_map/ppermute | solution.py:18
  77.5 34.0 %collective-permute-start.17 = (bf16[432,1536]{1,0:T(8,128)(2,1)}, bf16[432,1536]{1,0:T(8,128)(2,1)}, u32[]{:S(2)}, u32[]{:S(2)}) collective-permute-start(bf16[432,1536]{1,0:T(8,128)(2,1)} %get-tuple-element.57), channel_id=1, source_target_pairs={{4,8},{8,4},{12,16},{16,12},{20,24},{24,20},{5,9},{9,5},{13,17},{1... | collective-permute-start | bytes 3981320 | tf_op jit(solution)/shard_map/ppermute | solution.py:18
  107.7 24.2 %collective-permute-start.14 = (bf16[144,1536]{1,0:T(8,128)(2,1)}, bf16[144,1536]{1,0:T(8,128)(2,1)}, u32[]{:S(2)}, u32[]{:S(2)}) collective-permute-start(bf16[144,1536]{1,0:T(8,128)(2,1)} %get-tuple-element.52), channel_id=1, source_target_pairs={{0,4},{4,0},{8,12},{12,8},{16,20},{20,16},{24,28},{28,24},{1,5},{5... | collective-permute-start | bytes 1327112 | tf_op jit(solution)/shard_map/ppermute | solution.py:18
  110.0 21.9 %collective-permute-start.15 = (bf16[144,1536]{1,0:T(8,128)(2,1)}, bf16[144,1536]{1,0:T(8,128)(2,1)}, u32[]{:S(2)}, u32[]{:S(2)}) collective-permute-start(bf16[144,1536]{1,0:T(8,128)(2,1)} %get-tuple-element.53), channel_id=1, source_target_pairs={{4,8},{8,4},{12,16},{16,12},{20,24},{24,20},{5,9},{9,5},{13,17},{1... | collective-permute-start | bytes 1327112 | tf_op jit(solution)/shard_map/ppermute | solution.py:18
  114.3 25.3 %collective-permute-start.18 = (bf16[144,1536]{1,0:T(8,128)(2,1)}, bf16[144,1536]{1,0:T(8,128)(2,1)S(1)}, u32[]{:S(2)}, u32[]{:S(2)}) collective-permute-start(bf16[144,1536]{1,0:T(8,128)(2,1)} %get-tuple-element.60), channel_id=1, source_target_pairs={{0,1},{1,0},{2,3},{3,2},{4,5},{5,4},{6,7},{7,6},{8,9},{9,8},{10,11... | collective-permute-start | bytes 1327112 | tf_op jit(solution)/shard_map/ppermute | solution.py:18
  119.1 20.5 %collective-permute-start.19 = (bf16[144,1536]{1,0:T(8,128)(2,1)}, bf16[144,1536]{1,0:T(8,128)(2,1)S(1)}, u32[]{:S(2)}, u32[]{:S(2)}) collective-permute-start(bf16[144,1536]{1,0:T(8,128)(2,1)} %get-tuple-element.61), channel_id=1, source_target_pairs={{1,2},{2,1},{5,6},{6,5},{9,10},{10,9},{13,14},{14,13},{17,18},{18,... | collective-permute-start | bytes 1327112 | tf_op jit(solution)/shard_map/ppermute | solution.py:18
  122.5 17.1 %all-to-all-start.1 = ((f32[8,1,12]{2,1,0:T(1,128)}), f32[8,1,12]{2,1,0:T(1,128)S(1)}, u32[]{:S(2)}, u32[]{:S(2)}) async-start(f32[8,1,12]{2,1,0:T(1,128)} %get-tuple-element.58), calls=%async_computation.1 | async-start | bytes 8192 | tf_op jit(solution)/shard_map/all_to_all | solution.py:22
